TPU v7x, 32 devices: a whole 2x2x4 slice. The times are simulated.
32 devices in a mesh: dp: 4 (over y, core), mp: 8 (over z, x).
Axes of the slice: x: 2, y: 2, z: 4, core: 2. Of those that a mesh axis runs over, the one named last changes fastest.
Arguments:
- layer_in: float32 [8192, 2048], P('dp', 'mp'), may hold values from -18 to 18
- out_grad: float32 [8192, 2048], P('dp', 'mp'), may hold values from -6 to 6
- doc_ids: int32 [4, 2048], P('dp'), may hold values from 0 to 7, as said below
- group_owner: int32 [272], replicated, may hold values from 0 to 7, as said below
- norm_gains: float32 [2, 2048], P(None, 'mp'), may hold values from 0.5 to 1.5
- norm_gains_moment: float32 [2, 2048], P(None, 'mp'), may hold values from -768 to 768
- norm_gains_average: float32 [2, 2048], P(None, 'mp'), may hold values from 0.5 to 1.5
- feature_proj: float32 [2048, 2, 256], P('dp', None, 'mp'), may hold values from -0.125 to 0.125
- feature_proj_moment: float32 [2048, 2, 256], P('dp', None, 'mp'), may hold values from -512 to 512
- feature_proj_average: float32 [2048, 2, 256], P('dp', None, 'mp'), may hold values from -0.125 to 0.125
- head_proj: float32 [2048, 4, 2048], P('dp', None, 'mp'), may hold values from -0.125 to 0.125
- head_proj_moment: float32 [2048, 4, 2048], P('dp', None, 'mp'), may hold values from -512 to 512
- head_proj_average: float32 [2048, 4, 2048], P('dp', None, 'mp'), may hold values from -0.125 to 0.125
- mixer_out: float32 [2, 2048, 2048], P(None, 'mp', 'dp'), may hold values from -0.75 to 0.75
- mixer_out_moment: float32 [2, 2048, 2048], P(None, 'mp', 'dp'), may hold values from -112 to 112
- mixer_out_average: float32 [2, 2048, 2048], P(None, 'mp', 'dp'), may hold values from -0.75 to 0.75
- gate_up: float32 [2048, 2, 5632], P('dp', None, 'mp'), may hold values from -0.125 to 0.125
- gate_up_moment: float32 [2048, 2, 5632], P('dp', None, 'mp'), may hold values from -192 to 192
- gate_up_average: float32 [2048, 2, 5632], P('dp', None, 'mp'), may hold values from -0.125 to 0.125
- down_proj: float32 [5632, 2048], P('mp', 'dp'), may hold values from -0.078125 to 0.078125
- down_proj_moment: float32 [5632, 2048], P('mp', 'dp'), may hold values from -320 to 320
- down_proj_average: float32 [5632, 2048], P('mp', 'dp'), may hold values from -0.078125 to 0.078125
Outputs:
- out_y: float32 [8192, 2048], P('dp', 'mp')
- grad_x: float32 [8192, 2048], P('dp', 'mp')
- row_state: float32 [4, 544, 17, 128], P('dp', 'mp')
- norm_gains_grad: float32 [2, 2048], P(None, 'mp')
- norm_gains_new: float32 [2, 2048], P(None, 'mp')
- norm_gains_moment_new: float32 [2, 2048], P(None, 'mp')
- norm_gains_average_new: float32 [2, 2048], P(None, 'mp')
- norm_gains_copy: bfloat16 [2, 2048], P(None, 'mp')
- feature_proj_grad: float32 [2048, 2, 256], P('dp', None, 'mp')
- feature_proj_new: float32 [2048, 2, 256], P('dp', None, 'mp')
- feature_proj_moment_new: float32 [2048, 2, 256], P('dp', None, 'mp')
- feature_proj_average_new: float32 [2048, 2, 256], P('dp', None, 'mp')
- feature_proj_copy: bfloat16 [2048, 2, 256], P('dp', None, 'mp')
- head_proj_grad: float32 [2048, 4, 2048], P('dp', None, 'mp')
- head_proj_new: float32 [2048, 4, 2048], P('dp', None, 'mp')
- head_proj_moment_new: float32 [2048, 4, 2048], P('dp', None, 'mp')
- head_proj_average_new: float32 [2048, 4, 2048], P('dp', None, 'mp')
- head_proj_copy: bfloat16 [2048, 4, 2048], P('dp', None, 'mp')
- mixer_out_grad: float32 [2, 2048, 2048], P(None, 'mp', 'dp')
- mixer_out_new: float32 [2, 2048, 2048], P(None, 'mp', 'dp')
- mixer_out_moment_new: float32 [2, 2048, 2048], P(None, 'mp', 'dp')
- mixer_out_average_new: float32 [2, 2048, 2048], P(None, 'mp', 'dp')
- mixer_out_copy: bfloat16 [2, 2048, 2048], P(None, 'mp', 'dp')
- gate_up_grad: float32 [2048, 2, 5632], P('dp', None, 'mp')
- gate_up_new: float32 [2048, 2, 5632], P('dp', None, 'mp')
- gate_up_moment_new: float32 [2048, 2, 5632], P('dp', None, 'mp')
- gate_up_average_new: float32 [2048, 2, 5632], P('dp', None, 'mp')
- gate_up_copy: bfloat16 [2048, 2, 5632], P('dp', None, 'mp')
- down_proj_grad: float32 [5632, 2048], P('mp', 'dp')
- down_proj_new: float32 [5632, 2048], P('mp', 'dp')
- down_proj_moment_new: float32 [5632, 2048], P('mp', 'dp')
- down_proj_average_new: float32 [5632, 2048], P('mp', 'dp')
- down_proj_copy: bfloat16 [5632, 2048], P('mp', 'dp')
Inputs may be any that keep to these rules, and one draw needn't show every extreme that they name: `doc_ids`: within each row the document number starts at 0, rises by one at each new document and never falls; a row holds at most 8 documents, and some row holds exactly 8; each document has 1 to 512 tokens, and at least one document of each row has exactly that many. `group_owner`: exactly one index of mp owns 68 groups; every other index owns (204) // (number of mp indices - 1) groups or one more.
All inputs are finite; a program needn't handle non-finite values.
Results may differ from a plain program's by a relative error of at most 0.025.
Values may be sent and summed in bfloat16 or wider, within the bound.
No kernel may reach another device: no remote copies, remote signals or barrier semaphores. Data moves between devices by JAX's collectives and lax.ppermute only.
A program may use at most 448 MiB of HBM per device.

v0:
```python
import math

import jax
import jax.numpy as jnp
from jax import lax
from jax.sharding import PartitionSpec as P

D = 2048
HEADS = 16
FEAT = 16
HV = 128
WIN = 64
F1 = 17
GROUPS = 272


EPSILON = 1e-05
MOMENTUM = 0.9
AVERAGE_OLD = 0.99 * 0.01 / (1.0 - 0.99 * 0.99)
AVERAGE_NEW = 0.01 / (1.0 - 0.99 * 0.99)
RATE_FACTORS = (0.03, 0.01, 0.01, 0.28, 0.029, 0.01)
HIGHEST = lax.Precision.HIGHEST
HALF_ROOT = 0.7071067811865476
MASKED = -1e30


def bf_dot(left, right):
    return jnp.dot(left, right, preferred_element_type=jnp.float32)


def row_total(values):
    return lax.psum(values, "mp")


def norm_rows(values, gains):
    factor = lax.rsqrt(row_total(jnp.sum(values * values, axis=1)) / D + EPSILON)
    normed = (values * factor[:, None] * gains).astype(jnp.bfloat16)
    return (lax.all_gather(normed, "mp", axis=1, tiled=True), factor)


def norm_backward(values, factor, gains, upstream):
    gain_grad = jnp.sum(upstream * values * factor[:, None], axis=0)
    inner = row_total(jnp.sum(upstream * gains * values, axis=1))
    result = (
        factor[:, None] * gains * upstream
        - values * (factor * factor * factor * inner / D)[:, None]
    )
    return (result, gain_grad)


def gather_rows(values):
    return lax.all_gather(values, "mp", axis=1, tiled=True)


def branch_total(terms):
    return lax.psum_scatter(terms, "mp", scatter_dimension=1, tiled=True)


def input_total(terms):
    return lax.psum_scatter(terms, "mp", scatter_dimension=1, tiled=True)


def owner_pick(owner, device, slots):
    mine = owner == device
    ordinal = jnp.cumsum(mine.astype(jnp.int32)) - 1
    return (
        mine[None, :] & (ordinal[None, :] == jnp.arange(slots, dtype=jnp.int32)[:, None])
    ).astype(jnp.float32)


def slot_tables(picked, head_count):
    group_ids = jnp.arange(picked.shape[1], dtype=jnp.int32)
    head_onehot = (
        group_ids[:, None] // F1 == jnp.arange(head_count, dtype=jnp.int32)[None, :]
    ).astype(jnp.float32)
    within = group_ids % F1
    row_onehot = (within[:, None] == jnp.arange(FEAT, dtype=jnp.int32)[None, :]).astype(jnp.float32)
    linear_flag = (within == FEAT).astype(jnp.float32)
    head_select = jnp.dot(picked, head_onehot, precision=HIGHEST)
    row_select = jnp.dot(picked, row_onehot, precision=HIGHEST)
    flag_select = jnp.dot(picked, linear_flag, precision=HIGHEST)
    return (head_select, row_select, flag_select, jnp.sum(picked, axis=1))


def taylor_features(scaled, tables):
    head_select, row_select, flag_select, valid_slot = tables
    picked = jnp.einsum("bhf,ch->bcf", scaled, head_select, precision=HIGHEST)
    leading = jnp.einsum("bcf,cf->bc", picked, row_select, precision=HIGHEST)
    squares = leading[:, :, None] * picked * HALF_ROOT
    squares = jnp.concatenate([squares, jnp.zeros(leading.shape + (1,), jnp.float32)], axis=2)
    linear_row = jnp.concatenate([jnp.ones(leading.shape + (1,), jnp.float32), picked], axis=2)
    flagged = flag_select[None, :, None]
    return (squares * (1.0 - flagged) + linear_row * flagged) * valid_slot[None, :, None]


def linear_row_partial(pairs_row, values_row, docs_row, tables):
    head_select = tables[0]
    head_count = head_select.shape[1]
    length = docs_row.shape[0]
    block_rows = min(128, length)
    block_count = length // block_rows
    slots = head_select.shape[0]
    query_feats = taylor_features(pairs_row[:, 0] * 0.5, tables)
    key_feats = taylor_features(pairs_row[:, 1] * 0.5, tables)
    causal = jnp.arange(block_rows)[:, None] >= jnp.arange(block_rows)[None, :]

    def scan_step(carry, operands):
        state, key_total, previous = carry
        query_block, key_block, value_block, docs_block = operands
        slot_values = jnp.einsum("bhv,ch->bcv", value_block, head_select, precision=HIGHEST)
        allowed = (causal & (docs_block[:, None] == docs_block[None, :])).astype(jnp.float32)
        slot_scores = jnp.einsum("tcf,scf->tsc", query_block, key_block, precision=HIGHEST)
        head_scores = (
            jnp.einsum("tsc,ch->hts", slot_scores, head_select, precision=HIGHEST) * allowed[None]
        )
        numer = jnp.einsum("hts,shv->thv", head_scores, value_block, precision=HIGHEST)
        denom = jnp.transpose(jnp.sum(head_scores, axis=2))
        carried = (docs_block == previous).astype(jnp.float32)
        from_state = jnp.einsum("tcf,cfv->tcv", query_block, state, precision=HIGHEST)
        numer = (
            numer
            + jnp.einsum("tcv,ch->thv", from_state, head_select, precision=HIGHEST)
            * carried[:, None, None]
        )
        from_total = jnp.einsum("tcf,cf->tc", query_block, key_total, precision=HIGHEST)
        denom = denom + jnp.dot(from_total, head_select, precision=HIGHEST) * carried[:, None]
        last_doc = docs_block[block_rows - 1]
        in_last = (docs_block == last_doc).astype(jnp.float32)
        keep_state = (last_doc == previous).astype(jnp.float32)
        key_last = key_block * in_last[:, None, None]
        state = keep_state * state + jnp.einsum(
            "scf,scv->cfv", key_last, slot_values, precision=HIGHEST
        )
        key_total = keep_state * key_total + jnp.sum(key_last, axis=0)
        return ((state, key_total, last_doc), (numer, denom))

    initial = (
        jnp.zeros((slots, F1, HV), jnp.float32),
        jnp.zeros((slots, F1), jnp.float32),
        jnp.array(-1, jnp.int32),
    )
    blocked = (
        query_feats.reshape(block_count, block_rows, slots, F1),
        key_feats.reshape(block_count, block_rows, slots, F1),
        values_row.reshape(block_count, block_rows, head_count, HV),
        docs_row.reshape(block_count, block_rows),
    )
    (state, key_total, previous), (numer, denom) = lax.scan(
        jax.checkpoint(scan_step), initial, blocked
    )
    return (numer.reshape(length, head_count, HV), denom.reshape(length, head_count), state)


def window_pieces(queries, keys, values, documents):
    length = queries.shape[0]
    block_rows = min(512, length)
    key_padded = jnp.pad(keys, ((WIN, 0), (0, 0), (0, 0)))
    value_padded = jnp.pad(values, ((WIN, 0), (0, 0), (0, 0)))
    docs_padded = jnp.pad(documents, (WIN, 0), constant_values=-1)
    offsets = (
        jnp.arange(block_rows, dtype=jnp.int32)[:, None]
        + WIN
        - jnp.arange(block_rows + WIN, dtype=jnp.int32)[None, :]
    )

    def pieces(block_index):
        start = block_index * block_rows
        query_block = lax.dynamic_slice_in_dim(queries, start, block_rows, 0)
        key_block = lax.dynamic_slice_in_dim(key_padded, start, block_rows + WIN, 0)
        value_block = lax.dynamic_slice_in_dim(value_padded, start, block_rows + WIN, 0)
        docs_query = lax.dynamic_slice_in_dim(documents, start, block_rows, 0)
        docs_key = lax.dynamic_slice_in_dim(docs_padded, start, block_rows + WIN, 0)
        allowed = (offsets >= 0) & (offsets < WIN) & (docs_query[:, None] == docs_key[None, :])
        scores = jnp.einsum(
            "qhd,khd->hqk", query_block, key_block, preferred_element_type=jnp.float32
        ) * HV ** (-0.5)
        return (query_block, key_block, value_block, jnp.where(allowed[None], scores, MASKED))

    return (block_rows, length // block_rows, pieces)


def window_forward(queries, keys, values, documents):
    block_rows, block_count, pieces = window_pieces(queries, keys, values, documents)

    def attend_block(block_index):
        query_block, key_block, value_block, scores = pieces(block_index)
        peak = jnp.max(scores, axis=-1, keepdims=True)
        exponent = jnp.exp(scores - peak)
        denominator = jnp.sum(exponent, axis=-1, keepdims=True)
        probabilities = (exponent / denominator).astype(jnp.bfloat16)
        result = jnp.einsum(
            "hqk,khd->qhd", probabilities, value_block, preferred_element_type=jnp.float32
        )
        return (result, jnp.swapaxes((peak + jnp.log(denominator))[:, :, 0], 0, 1))

    result, log_totals = lax.map(attend_block, jnp.arange(block_count, dtype=jnp.int32))
    return (
        result.reshape(queries.shape[0], queries.shape[1], HV),
        log_totals.reshape(queries.shape[0], queries.shape[1]),
    )


def window_backward(queries, keys, values, documents, log_totals, upstream):
    block_rows, block_count, pieces = window_pieces(queries, keys, values, documents)

    def back_block(block_index):
        query_block, key_block, value_block, scores = pieces(block_index)
        start = block_index * block_rows
        totals_block = lax.dynamic_slice_in_dim(log_totals, start, block_rows, 0)
        upstream_block = lax.dynamic_slice_in_dim(upstream, start, block_rows, 0)
        probabilities = jnp.exp(scores - jnp.swapaxes(totals_block, 0, 1)[:, :, None])
        value_grad = jnp.einsum(
            "hqk,qhd->khd",
            probabilities.astype(jnp.bfloat16),
            upstream_block,
            preferred_element_type=jnp.float32,
        )
        prob_grad = jnp.einsum(
            "qhd,khd->hqk", upstream_block, value_block, preferred_element_type=jnp.float32
        )
        score_grad = (
            probabilities * (prob_grad - jnp.sum(probabilities * prob_grad, axis=-1, keepdims=True))
        ).astype(jnp.bfloat16)
        query_grad = jnp.einsum(
            "hqk,khd->qhd", score_grad, key_block, preferred_element_type=jnp.float32
        ) * HV ** (-0.5)
        key_grad = jnp.einsum(
            "hqk,qhd->khd", score_grad, query_block, preferred_element_type=jnp.float32
        ) * HV ** (-0.5)
        return (query_grad, key_grad, value_grad)

    query_grad, key_grad, value_grad = lax.map(back_block, jnp.arange(block_count, dtype=jnp.int32))

    def settle(extended):
        central = extended[:, WIN:]
        central = central.at[:-1, block_rows - WIN :].add(extended[1:, :WIN])
        return central.reshape(queries.shape[0], queries.shape[1], HV)

    return (
        query_grad.reshape(queries.shape[0], queries.shape[1], HV),
        settle(key_grad),
        settle(value_grad),
    )


def own_part(values, dim, pieces_count, position):
    width = values.shape[dim] // pieces_count
    return lax.dynamic_slice_in_dim(values, position * width, width, dim)


def momentum_update(weights, moment, average, gradient, factor, token_total):
    step_rate = factor / math.sqrt(token_total)
    moment_new = MOMENTUM * moment + gradient
    weights_new = weights - step_rate * (gradient + MOMENTUM * moment_new)
    average_new = AVERAGE_OLD * average + AVERAGE_NEW * weights_new
    return (gradient, weights_new, moment_new, average_new, weights_new.astype(jnp.bfloat16))


def local(
    layer_in,
    out_grad,
    doc_ids,
    group_owner,
    norm_gains,
    norm_gains_moment,
    norm_gains_average,
    feature_proj,
    feature_proj_moment,
    feature_proj_average,
    head_proj,
    head_proj_moment,
    head_proj_average,
    mixer_out,
    mixer_out_moment,
    mixer_out_average,
    gate_up,
    gate_up_moment,
    gate_up_average,
    down_proj,
    down_proj_moment,
    down_proj_average,
):
    model_ways = lax.axis_size("mp")
    data_ways = lax.axis_size("dp")
    row_count, length = doc_ids.shape
    tokens_here = layer_in.shape[0]
    heads_here = HEADS // model_ways
    head_share = heads_here * HV
    feature_share = heads_here * FEAT
    slots = 2 * GROUPS // model_ways
    feature_full, head_full, mixer_full, gate_full, down_full = (
        lax.all_gather(feature_proj.astype(jnp.bfloat16), "dp", axis=0, tiled=True),
        lax.all_gather(head_proj.astype(jnp.bfloat16), "dp", axis=0, tiled=True),
        lax.all_gather(mixer_out.astype(jnp.bfloat16), "dp", axis=2, tiled=True),
        lax.all_gather(gate_up.astype(jnp.bfloat16), "dp", axis=0, tiled=True),
        lax.all_gather(down_proj.astype(jnp.bfloat16), "dp", axis=1, tiled=True),
    )
    normed_one, factor_one = norm_rows(layer_in, norm_gains[0])
    pairs_local = (
        bf_dot(normed_one, feature_full.reshape(D, 2 * feature_share))
        .astype(jnp.bfloat16)
        .reshape(tokens_here, 2, feature_share)
    )
    projected = (
        bf_dot(normed_one, head_full.reshape(D, 4 * head_share))
        .astype(jnp.bfloat16)
        .reshape(tokens_here, 4, head_share)
    )
    owned_pick = owner_pick(group_owner, lax.axis_index("mp"), slots)
    pairs_all, values_all = (
        lax.all_gather(pairs_local, "mp", axis=2, tiled=True),
        lax.all_gather(projected[:, 3], "mp", axis=1, tiled=True),
    )
    tables = slot_tables(owned_pick, HEADS)
    pairs_rows = pairs_all.astype(jnp.float32).reshape(row_count, length, 2, HEADS, FEAT)
    values_rows = values_all.astype(jnp.float32).reshape(row_count, length, HEADS, HV)

    def linear_all(pairs_in, values_in):
        return lax.map(
            lambda operands: linear_row_partial(operands[0], operands[1], operands[2], tables),
            (pairs_in, values_in, doc_ids),
        )

    (numer_rows, denom_rows, row_state), linear_pull = jax.vjp(linear_all, pairs_rows, values_rows)
    state_zero = jnp.zeros_like(row_state)
    numer_part = numer_rows.reshape(tokens_here, HEADS, HV)
    denom_part = denom_rows.reshape(tokens_here, HEADS)
    numer_total, denom_total = lax.psum((numer_part, denom_part), "mp")
    numer_mine = lax.dynamic_slice_in_dim(
        numer_total, lax.axis_index("mp") * heads_here, heads_here, 1
    )
    denom_mine = lax.dynamic_slice_in_dim(
        denom_total, lax.axis_index("mp") * heads_here, heads_here, 1
    )
    linear_mine = numer_mine / denom_mine[:, :, None]
    linear_low = linear_mine.astype(jnp.bfloat16).reshape(tokens_here, head_share)
    window_in = projected[:, :3].reshape(row_count, length, 3, heads_here, HV)

    def window_row(operands):
        return window_forward(operands[0][:, 0], operands[0][:, 1], operands[0][:, 2], operands[1])

    window_rows, log_rows = lax.map(window_row, (window_in, doc_ids))
    window_low = window_rows.astype(jnp.bfloat16).reshape(tokens_here, head_share)
    mixed = branch_total(bf_dot(linear_low, mixer_full[0]) + bf_dot(window_low, mixer_full[1]))
    middle = layer_in + mixed
    normed_two, factor_two = norm_rows(middle, norm_gains[1])
    gate_values = bf_dot(normed_two, gate_full.reshape(D, -1)).reshape(tokens_here, 2, -1)
    gate_part = gate_values[:, 0]
    up_part = gate_values[:, 1]
    sigmoid_gate = jax.nn.sigmoid(gate_part)
    activated = gate_part * sigmoid_gate
    hidden = (activated * up_part).astype(jnp.bfloat16)
    out_y = middle + branch_total(bf_dot(hidden, down_full))
    grad_out_all = gather_rows(out_grad.astype(jnp.bfloat16))
    down_grad = jnp.einsum("tf,td->fd", hidden, grad_out_all, preferred_element_type=jnp.float32)
    hidden_grad = jnp.einsum(
        "td,fd->tf", grad_out_all, down_full, preferred_element_type=jnp.float32
    )
    gate_grad = hidden_grad * up_part * sigmoid_gate * (1.0 + gate_part * (1.0 - sigmoid_gate))
    gate_up_low = jnp.stack([gate_grad, hidden_grad * activated], axis=1).astype(jnp.bfloat16)
    gate_up_full_grad = jnp.einsum(
        "td,tkf->dkf", normed_two, gate_up_low, preferred_element_type=jnp.float32
    )
    normed_two_grad = input_total(
        jnp.einsum("tkf,dkf->td", gate_up_low, gate_full, preferred_element_type=jnp.float32)
    )
    middle_norm_grad, gain_two = norm_backward(middle, factor_two, norm_gains[1], normed_two_grad)
    middle_grad = out_grad + middle_norm_grad
    mixed_all = gather_rows(middle_grad.astype(jnp.bfloat16))
    head_outputs = jnp.stack([linear_low, window_low], axis=1)
    mixer_full_grad = jnp.einsum(
        "tkh,td->khd", head_outputs, mixed_all, preferred_element_type=jnp.float32
    )
    mixer_back = jnp.einsum(
        "td,khd->tkh", mixed_all, mixer_full, preferred_element_type=jnp.float32
    )
    linear_grad = mixer_back[:, 0].reshape(tokens_here, heads_here, HV)
    window_grad = mixer_back[:, 1].astype(jnp.bfloat16).reshape(row_count, length, heads_here, HV)
    numer_grad = (linear_grad / denom_mine[:, :, None]).astype(jnp.bfloat16)
    denom_grad = (-jnp.sum(linear_grad * linear_mine, axis=2) / denom_mine).astype(jnp.bfloat16)
    numer_grad_all, denom_grad_all = (
        lax.all_gather(numer_grad, "mp", axis=1, tiled=True),
        lax.all_gather(denom_grad, "mp", axis=1, tiled=True),
    )
    pairs_grad_rows, values_grad_rows = linear_pull(
        (
            numer_grad_all.astype(jnp.float32).reshape(row_count, length, HEADS, HV),
            denom_grad_all.astype(jnp.float32).reshape(row_count, length, HEADS),
            state_zero,
        )
    )
    pairs_grad, values_grad = (
        lax.psum_scatter(
            pairs_grad_rows.reshape(tokens_here, 2, HEADS * FEAT).astype(jnp.bfloat16),
            "mp",
            scatter_dimension=2,
            tiled=True,
        ).astype(jnp.float32),
        lax.psum_scatter(
            values_grad_rows.reshape(tokens_here, HEADS * HV).astype(jnp.bfloat16),
            "mp",
            scatter_dimension=1,
            tiled=True,
        ).astype(jnp.float32),
    )

    def window_row_back(operands):
        return window_backward(
            operands[0][:, 0],
            operands[0][:, 1],
            operands[0][:, 2],
            operands[1],
            operands[2],
            operands[3],
        )

    query_grad, key_grad, value_grad = lax.map(
        window_row_back, (window_in, doc_ids, log_rows, window_grad)
    )
    projected_grad = jnp.stack(
        [
            query_grad.reshape(tokens_here, head_share),
            key_grad.reshape(tokens_here, head_share),
            value_grad.reshape(tokens_here, head_share),
            values_grad,
        ],
        axis=1,
    ).astype(jnp.bfloat16)
    pairs_low = pairs_grad.astype(jnp.bfloat16)
    feature_full_grad = jnp.einsum(
        "td,tkc->dkc", normed_one, pairs_low, preferred_element_type=jnp.float32
    )
    head_full_grad = jnp.einsum(
        "td,tkc->dkc", normed_one, projected_grad, preferred_element_type=jnp.float32
    )
    normed_one_terms = jnp.einsum(
        "tkc,dkc->td", pairs_low, feature_full, preferred_element_type=jnp.float32
    ) + jnp.einsum("tkc,dkc->td", projected_grad, head_full, preferred_element_type=jnp.float32)
    normed_one_grad = input_total(normed_one_terms)
    input_norm_grad, gain_one = norm_backward(layer_in, factor_one, norm_gains[0], normed_one_grad)
    grad_x = middle_grad + input_norm_grad
    gains_grad = jnp.stack([gain_one, gain_two], axis=0)
    data_index = lax.axis_index("dp")
    summed = (
        lax.psum(feature_full_grad.astype(jnp.bfloat16), "dp").astype(jnp.float32),
        lax.psum(head_full_grad.astype(jnp.bfloat16), "dp").astype(jnp.float32),
        lax.psum(mixer_full_grad.astype(jnp.bfloat16), "dp").astype(jnp.float32),
        lax.psum(gate_up_full_grad.astype(jnp.bfloat16), "dp").astype(jnp.float32),
        lax.psum(down_grad.astype(jnp.bfloat16), "dp").astype(jnp.float32),
        lax.psum(gains_grad.astype(jnp.bfloat16), "dp").astype(jnp.float32),
    )
    feature_sum = own_part(summed[0], 0, data_ways, data_index)
    head_sum = own_part(summed[1], 0, data_ways, data_index)
    mixer_sum = own_part(summed[2], 2, data_ways, data_index)
    gate_sum = own_part(summed[3], 0, data_ways, data_index)
    down_sum = own_part(summed[4], 1, data_ways, data_index)
    gains_sum = summed[5]
    token_total = tokens_here * data_ways
    triples = (
        (norm_gains, norm_gains_moment, norm_gains_average, gains_sum),
        (feature_proj, feature_proj_moment, feature_proj_average, feature_sum),
        (head_proj, head_proj_moment, head_proj_average, head_sum),
        (mixer_out, mixer_out_moment, mixer_out_average, mixer_sum),
        (gate_up, gate_up_moment, gate_up_average, gate_sum),
        (down_proj, down_proj_moment, down_proj_average, down_sum),
    )
    results = [out_y, grad_x, row_state]
    for weight_index in range(6):
        weights, moment, average, gradient = triples[weight_index]
        results.extend(
            momentum_update(
                weights, moment, average, gradient, RATE_FACTORS[weight_index], token_total
            )
        )
    return tuple(results)


def solution(mesh):
    placed = (
        P("dp", "mp"),
        P("dp", "mp"),
        P("dp", None),
        P(),
        P(None, "mp"),
        P(None, "mp"),
        P(None, "mp"),
        P("dp", None, "mp"),
        P("dp", None, "mp"),
        P("dp", None, "mp"),
        P("dp", None, "mp"),
        P("dp", None, "mp"),
        P("dp", None, "mp"),
        P(None, "mp", "dp"),
        P(None, "mp", "dp"),
        P(None, "mp", "dp"),
        P("dp", None, "mp"),
        P("dp", None, "mp"),
        P("dp", None, "mp"),
        P("mp", "dp"),
        P("mp", "dp"),
        P("mp", "dp"),
    )
    return jax.shard_map(
        local,
        mesh=mesh,
        in_specs=placed,
        out_specs=(
            P("dp", "mp"),
            P("dp", "mp"),
            P("dp", "mp", None, None),
            P(None, "mp"),
            P(None, "mp"),
            P(None, "mp"),
            P(None, "mp"),
            P(None, "mp"),
            P("dp", None, "mp"),
            P("dp", None, "mp"),
            P("dp", None, "mp"),
            P("dp", None, "mp"),
            P("dp", None, "mp"),
            P("dp", None, "mp"),
            P("dp", None, "mp"),
            P("dp", None, "mp"),
            P("dp", None, "mp"),
            P("dp", None, "mp"),
            P(None, "mp", "dp"),
            P(None, "mp", "dp"),
            P(None, "mp", "dp"),
            P(None, "mp", "dp"),
            P(None, "mp", "dp"),
            P("dp", None, "mp"),
            P("dp", None, "mp"),
            P("dp", None, "mp"),
            P("dp", None, "mp"),
            P("dp", None, "mp"),
            P("mp", "dp"),
            P("mp", "dp"),
            P("mp", "dp"),
            P("mp", "dp"),
            P("mp", "dp"),
        ),
        check_vma=False,
    )
```

profile of v0, /device:TPU:0, one launch (start us, length us, event | category | flops | bytes accessed | tf_op | source)
XLA Modules:
  0.0 7818.4 jit_solution(10999511888721055593)
XLA Ops:
  44.8 115.6 %all-gather.14.cloned.1.call-done = bf16[2048,2048]{1,0:T(8,128)(2,1)} async-done(((bf16[2048,256]{1,0:T(8,128)(2,1)}), bf16[2048,2048]{1,0:T(8,128)(2,1)}) %all-gather.14.cloned.1.call-update) | async-done | bytes 8388624 | tf_op jit(solution)/shard_map/all_gather | solution.py:38
  420.5 1120.2 %while.150 = (s32[]{:T(128)}, f32[68,17,128]{2,1,0:T(8,128)S(1)}, f32[68,17]{1,0:T(8,128)}, s32[]{:T(128)}, f32[16,128,16,128]{3,1,0,2:T(8,128)}, /*index=5*/f32...) while((s32[]{:T(128)}, f32[68,17,128]{2,1,0:T(8,128)S(1)}, ...), condition=%wide.region_8.9_spmd.clone, body=%wide.region_5.8_spmd.clone.sunk | while | flops 1731968896 | bytes 60174664 | solution.py:148
  1581.9 500.3 %all-reduce.15.cloned.1.call-done = (f32[2048,16]{1,0:T(8,128)}, f32[2048,16,128]{2,0,1:T(8,128)}) async-done(((f32[2048,16]{1,0:T(8,128)}, f32[2048,16,128]{2,0,1:T(8,128)}), (f32[2048,16]{1,0:T(8,128)}, f32[2048,16,128]{2,0,1:T(8,128)})) %all-reduce.15.cloned.1.call-update) | async-done | bytes 16908304 | tf_op jit(solution)/shard_map/psum | solution.py:328
  2122.7 279.5 %reduce-scatter.7.cloned.1.call-done = f32[2048,256]{1,0:T(8,128)} async-done(((f32[2048,2048]{1,0:T(8,128)}), f32[2048,256]{1,0:T(8,128)}) %reduce-scatter.7.cloned.1.call-update) | async-done | bytes 2097168 | tf_op jit(solution)/shard_map/reduce_scatter | solution.py:56
  2446.9 128.2 %all-gather.22.cloned.1.call-done = bf16[2048,2048]{1,0:T(8,128)(2,1)} async-done(((bf16[2048,256]{1,0:T(8,128)(2,1)}), bf16[2048,2048]{1,0:T(8,128)(2,1)}) %all-gather.22.cloned.1.call-update) | async-done | bytes 8388624 | tf_op jit(solution)/shard_map/all_gather | solution.py:38
  2602.5 128.2 %all-gather.28.cloned.1.call-done = bf16[2048,2048]{1,0:T(8,128)(2,1)} async-done(((bf16[2048,256]{1,0:T(8,128)(2,1)}), bf16[2048,2048]{1,0:T(8,128)(2,1)}) %all-gather.28.cloned.1.call-update) | async-done | bytes 8388624 | tf_op jit(solution)/shard_map/all_gather | solution.py:52
  2778.9 267.0 %reduce-scatter.11.cloned.1.call-done = f32[2048,256]{1,0:T(8,128)} async-done(((f32[2048,2048]{1,0:T(8,128)}), f32[2048,256]{1,0:T(8,128)}) %reduce-scatter.11.cloned.1.call-update) | async-done | bytes 2097168 | tf_op jit(solution)/shard_map/reduce_scatter | solution.py:60
  3069.2 262.7 %reduce-scatter.9.cloned.1.call-done = f32[2048,256]{1,0:T(8,128)} async-done(((f32[2048,2048]{1,0:T(8,128)}), f32[2048,256]{1,0:T(8,128)}) %reduce-scatter.9.cloned.1.call-update) | async-done | bytes 2097168 | tf_op jit(solution)/shard_map/reduce_scatter | solution.py:56
  3336.6 124.6 %all-gather.30.cloned.1.call-done = bf16[2048,2048]{1,0:T(8,128)(2,1)} async-done(((bf16[2048,256]{1,0:T(8,128)(2,1)}), bf16[2048,2048]{1,0:T(8,128)(2,1)}) %all-gather.30.cloned.1.call-update) | async-done | bytes 8388624 | tf_op jit(solution)/shard_map/all_gather | solution.py:52
  3480.0 31.1 all-gather.1
  3511.8 89.0 %all-gather.32.cloned.1.call-done = bf16[2048,16,128]{2,0,1:T(8,128)(2,1)} async-done(((bf16[2048,2,128]{2,0,1:T(8,128)(2,1)}), bf16[2048,16,128]{2,0,1:T(8,128)(2,1)}) %all-gather.32.cloned.1.call-update) | async-done | bytes 8388624 | tf_op jit(solution)/shard_map/all_gather | solution.py:382
  3636.6 3289.1 %while.151 = (s32[]{:T(128)}, f32[68,17,128]{2,1,0:T(8,128)}, f32[68,17]{1,0:T(8,128)}, f32[16,128,68,17]{1,0,2,3:T(8,128)}, f32[16,128,68,17]{1,0,2,3:T(8,128)}...) while((s32[]{:T(128)}, f32[68,17,128]{2,1,0:T(8,128)}, ...), condition=%wide.region_24.25_spmd.clone, body=%wide.region_23.24_spmd.clone.sunk | while | flops 3472114688 | bytes 138188176 | solution.py:148
  3735.6 30.2 dynamic_update_slice.170
  3941.0 30.2 dynamic_update_slice.170
  4146.5 30.2 dynamic_update_slice.170
  4351.8 30.2 dynamic_update_slice.170
  4557.2 30.2 dynamic_update_slice.170
  4762.7 30.2 dynamic_update_slice.170
  4968.0 30.2 dynamic_update_slice.170
  5173.5 30.2 dynamic_update_slice.170
  5378.9 30.2 dynamic_update_slice.170
  5584.2 30.2 dynamic_update_slice.170
  5789.7 30.2 dynamic_update_slice.170
  5995.2 30.2 dynamic_update_slice.170
  6200.4 30.2 dynamic_update_slice.170
  6405.9 30.2 dynamic_update_slice.170
  6611.3 30.2 dynamic_update_slice.170
  6816.6 30.2 dynamic_update_slice.170
  7053.1 43.3 while.149
  7133.5 80.3 %reduce-scatter.15.cloned.1.call-done = bf16[2048,256]{1,0:T(8,128)(2,1)} async-done(((bf16[2048,2048]{1,0:T(8,128)(2,1)}), bf16[2048,256]{1,0:T(8,128)(2,1)}) %reduce-scatter.15.cloned.1.call-update) | async-done | bytes 1048592 | tf_op jit(solution)/shard_map/reduce_scatter | solution.py:399
  7257.4 233.7 %all-reduce.17.cloned.1.call-done = (bf16[2048,2,32]{0,2,1:T(8,128)(2,1)}, bf16[2048,4,256]{2,0,1:T(8,128)(2,1)}, bf16[2,256,2048]{2,1,0:T(8,128)(2,1)}, bf16[2048,2,704]{0,2,1:T(8,128)(2,1)}, bf16[704,2048]{1,0:T(8,128)(2,1)}) async-done(((bf16[2048,2,32]{0,2,1:T(8,128)(2,1)}, bf16[2048,4,256]{2,0,1:T(8,128)(2,1)}, bf16[2,256,2048]{2,1,0:T(8,128)(2,1)}, bf16[2048,2,704]{0,2,1:T(8,128)(2,1)}, ...) | async-done | bytes 15204368 | tf_op jit(solution)/shard_map/psum | solution.py:445
  7531.7 246.2 %reduce-scatter.17.cloned.1.call-done = f32[2048,256]{1,0:T(8,128)} async-done(((f32[2048,2048]{1,0:T(8,128)}), f32[2048,256]{1,0:T(8,128)}) %reduce-scatter.17.cloned.1.call-update) | async-done | bytes 2097168 | tf_op jit(solution)/shard_map/reduce_scatter | solution.py:60
  (1939 shorter events, 4767.1 us)
Async XLA Ops:
  7.2 153.2 %all-gather.14.cloned.1.call-start = ((), (), s32[]{:S(2)}) async-start(), calls=%async_computation.6 | async-start | bytes 9437184 | tf_op jit(solution)/shard_map/all_gather | solution.py:38
  37.6 157.7 %all-gather.18.cloned.1.call-start = ((), (), s32[]{:S(2)}) async-start(), calls=%async_computation.8 | async-start | bytes 5242880 | tf_op jit(solution)/shard_map/all_gather | solution.py:293
  39.0 208.4 %all-gather.16.cloned.1.call-start = ((), (), s32[]{:S(2)}) async-start(), calls=%async_computation.7 | async-start | bytes 2359296 | tf_op jit(solution)/shard_map/all_gather | solution.py:311
  167.2 206.2 %all-gather.34.cloned.1.call-start = ((), (), s32[]{:S(2)}) async-start(), calls=%async_computation.22 | async-start | bytes 9437184 | tf_op jit(solution)/shard_map/all_gather | solution.py:312
  217.3 1864.9 %all-reduce.15.cloned.1.call-start = ((), (), s32[]{:S(2)}) async-start(), calls=%async_computation.23 | async-start | bytes 35651584 | tf_op jit(solution)/shard_map/psum | solution.py:328
  1543.2 562.6 %all-gather.20.cloned.1.call-start = ((), (), s32[]{:S(2)}) async-start(), calls=%async_computation.9 | async-start | bytes 2621440 | tf_op jit(solution)/shard_map/all_gather | solution.py:294
  1545.3 857.0 %reduce-scatter.7.cloned.1.call-start = ((), (), s32[]{:S(2)}) async-start(), calls=%async_computation.10 | async-start | bytes 18874368 | tf_op jit(solution)/shard_map/reduce_scatter | solution.py:56
  1579.4 509.6 %copy-start.10 = (bf16[2112,2,128]{2,0,1:T(8,128)(2,1)}, bf16[2112,2,128]{2,0,1:T(8,128)(2,1)S(1)}, u32[]{:S(2)}) copy-start(bf16[2112,2,128]{2,0,1:T(8,128)(2,1)S(1)} %get-tuple-element.2388) | copy-start | bytes 3244036
  1579.5 509.6 %copy-start.12 = (bf16[2048,2,128]{2,0,1:T(8,128)(2,1)}, bf16[2048,2,128]{2,0,1:T(8,128)(2,1)S(1)}, u32[]{:S(2)}) copy-start(bf16[2048,2,128]{2,0,1:T(8,128)(2,1)S(1)} %get-tuple-element.2390) | copy-start | bytes 3145732
  1579.5 509.6 %copy-start.19 = (bf16[4,512,2,128]{1,3,2,0:T(8,128)(2,1)}, bf16[4,512,2,128]{1,3,2,0:T(8,128)(2,1)S(1)}, u32[]{:S(2)}) copy-start(bf16[4,512,2,128]{1,3,2,0:T(8,128)(2,1)S(1)} %get-tuple-element.904) | copy-start | bytes 3145732
  1579.5 509.6 %copy-start.63 = (s32[512]{0:T(512)}, s32[512]{0:T(512)S(1)}, u32[]{:S(2)}) copy-start(s32[512]{0:T(512)S(1)} %get-tuple-element.2449) | copy-start | bytes 6148
  1579.5 509.6 %copy-start.65 = (s32[2112]{0:T(1024)}, s32[2112]{0:T(1024)S(1)}, u32[]{:S(2)}) copy-start(s32[2112]{0:T(1024)S(1)} %get-tuple-element.2450) | copy-start | bytes 25348
  2119.3 282.9 %copy-start.7 = (f32[2048,256]{1,0:T(8,128)S(1)}, f32[2048,256]{1,0:T(8,128)}, u32[]{:S(2)}) copy-start(f32[2048,256]{1,0:T(8,128)} %param.34) | copy-start | bytes 6291460
  2119.4 327.5 %all-gather.24.cloned.1.call-start = ((), (), s32[]{:S(2)}) async-start(), calls=%async_computation.12 | async-start | bytes 7208960 | tf_op jit(solution)/shard_map/all_gather | solution.py:295
  2122.7 308.0 %copy-start.27 = (f32[704,512]{1,0:T(8,128)S(1)}, f32[704,512]{1,0:T(8,128)}, u32[]{:S(2)}) copy-start(f32[704,512]{1,0:T(8,128)} %param.53) | copy-start | bytes 4325380
  2122.7 452.5 %all-gather.22.cloned.1.call-start = ((), (), s32[]{:S(2)}) async-start(), calls=%async_computation.11 | async-start | bytes 9437184 | tf_op jit(solution)/shard_map/all_gather | solution.py:38
  2430.6 171.9 %all-gather.26.cloned.1.call-start = ((), (), s32[]{:S(2)}) async-start(), calls=%async_computation.13 | async-start | bytes 3604480 | tf_op jit(solution)/shard_map/all_gather | solution.py:296
  2431.6 299.1 %all-gather.28.cloned.1.call-start = ((), (), s32[]{:S(2)}) async-start(), calls=%async_computation.15 | async-start | bytes 9437184 | tf_op jit(solution)/shard_map/all_gather | solution.py:52
  2432.8 613.2 %reduce-scatter.11.cloned.1.call-start = ((), (), s32[]{:S(2)}) async-start(), calls=%async_computation.16 | async-start | bytes 18874368 | tf_op jit(solution)/shard_map/reduce_scatter | solution.py:60
  2764.9 567.0 %reduce-scatter.9.cloned.1.call-start = ((), (), s32[]{:S(2)}) async-start(), calls=%async_computation.14 | async-start | bytes 18874368 | tf_op jit(solution)/shard_map/reduce_scatter | solution.py:56
  2778.9 267.1 %copy-start.80 = (f32[1,256]{1,0:T(1,128)S(1)}, f32[1,256]{1,0:T(1,128)}, u32[]{:S(2)}) copy-start(f32[1,256]{1,0:T(1,128)} %get-tuple-element.1758) | copy-start | bytes 3076
  2778.9 290.3 %copy-start.77 = (f32[2048]{0:T(1024)S(1)}, f32[2048]{0:T(1024)}, u32[]{:S(2)}) copy-start(f32[2048]{0:T(1024)} %psum.87) | copy-start | bytes 24580
  2778.9 682.3 %all-gather.30.cloned.1.call-start = ((), (), s32[]{:S(2)}) async-start(), calls=%async_computation.17 | async-start | bytes 9437184 | tf_op jit(solution)/shard_map/all_gather | solution.py:52
  3336.6 264.3 %all-gather.32.cloned.1.call-start = ((), (), s32[]{:S(2)}) async-start(), calls=%async_computation.18 | async-start | bytes 9437184 | tf_op jit(solution)/shard_map/all_gather | solution.py:382
  3476.9 3650.6 %reduce-scatter.13.cloned.1.call-start = ((), (), s32[]{:S(2)}) async-start(), calls=%async_computation.19 | async-start | bytes 2359296 | tf_op jit(solution)/shard_map/reduce_scatter | solution.py:393
  6995.5 218.4 %reduce-scatter.15.cloned.1.call-start = ((), (), s32[]{:S(2)}) async-start(), calls=%async_computation.20 | async-start | bytes 9437184 | tf_op jit(solution)/shard_map/reduce_scatter | solution.py:399
  7019.2 471.8 %all-reduce.17.cloned.1.call-start = ((), (), s32[]{:S(2)}) async-start(), calls=%async_computation.24 | async-start | bytes 30408704 | tf_op jit(solution)/shard_map/psum | solution.py:445
  7227.4 550.5 %reduce-scatter.17.cloned.1.call-start = ((), (), s32[]{:S(2)}) async-start(), calls=%async_computation.21 | async-start | bytes 18874368 | tf_op jit(solution)/shard_map/reduce_scatter | solution.py:60
  7531.7 275.2 %copy-start.76 = (f32[2048]{0:T(1024)S(1)}, f32[2048]{0:T(1024)}, u32[]{:S(2)}) copy-start(f32[2048]{0:T(1024)} %copy-done.75) | copy-start | bytes 24580
  7531.7 275.2 %copy-start.82 = (f32[2,256]{1,0:T(2,128)S(1)}, f32[2,256]{1,0:T(2,128)}, u32[]{:S(2)}) copy-start(f32[2,256]{1,0:T(2,128)} %param.38) | copy-start | bytes 6148
  7531.7 275.2 %copy-start.91 = (f32[2,256]{1,0:T(2,128)S(1)}, f32[2,256]{1,0:T(2,128)}, u32[]{:S(2)}) copy-start(f32[2,256]{1,0:T(2,128)} %param.39) | copy-start | bytes 6148
  7531.7 275.8 %copy-start.89 = (f32[2,256]{1,0:T(2,128)S(1)}, f32[2,256]{1,0:T(2,128)}, u32[]{:S(2)}) copy-start(f32[2,256]{1,0:T(2,128)} %param.40) | copy-start | bytes 6148
  (272 other events, 3708.9 us)
Sparse Core Ops, SparseCore 0:
  37.7 122.6 all-gather.13
  162.6 32.6 all-gather.17
  198.0 49.2 all-gather.15
  249.9 123.4 all-gather.33
  1543.3 538.8 all-reduce.14
  2084.2 21.5 all-gather.19
  2119.5 282.7 reduce-scatter.6
  2404.4 42.4 all-gather.23
  2449.7 125.3 all-gather.21
  2577.2 25.2 all-gather.25
  2605.3 125.3 all-gather.27
  2765.0 280.8 reduce-scatter.10
  3049.7 282.1 reduce-scatter.8
  3336.7 124.4 all-gather.29
  3477.0 123.7 all-gather.31
  6995.6 65.8 reduce-scatter.12
  7065.5 148.3 reduce-scatter.14
  7227.5 263.4 all-reduce.16
  7494.8 283.0 reduce-scatter.16
where the time goes:
time: 7870 us; the launch traced here: 7820 us
  waiting for transfers between devices  2560 us (33%)
  matrix products  2440 us (31%)
  local copies, waits for them, and re-layouts  2170 us (28%)
  other arithmetic  412 us (5%)
  blocking collectives  128 us (2%)
  loops' own time  91.2 us (1%)
    dynamic_update_slice x112, local copies, waits for them, and re-layouts, linear_row_partial(): lax.scan(jax.checkpoint(scan_step), initial, blocked)  1060 us
    reduce_scatter x2, waiting for transfers between devices, branch_total(): return lax.psum_scatter(terms, 'mp', scatter_dimension=1, tiled=True)  542 us
    dot_general x64, matrix products, scan_step(): jnp.einsum('tcf,scf->tsc', query_block, key_block, precision=HIGHEST)  525 us
    reduce_scatter x2, waiting for transfers between devices, input_total(): return lax.psum_scatter(terms, 'mp', scatter_dimension=1, tiled=True)  513 us
    psum x1, waiting for transfers between devices, local(): numer_total, denom_total = lax.psum((numer_part, denom_part), 'mp')  500 us
    dot_general x48, matrix products, scan_step(): jnp.einsum('tcf,cfv->tcv', query_block, state, precision=HIGHEST)  362 us
    dot_general x48, matrix products, scan_step(): jnp.einsum('scf,scv->cfv', key_last, slot_values, precision=HIGHEST)  327 us
    transpose x48, local copies, waits for them, and re-layouts, scan_step(): jnp.einsum('tcf,scf->tsc', query_block, key_block, precision=HIGHEST)  287 us
  transfers between devices with their start and end apart: 19, of which 18 were waited for; matrix products, arithmetic and copies ran while one was open for 6% of the time, Pallas kernels for 0%

commit v1 on v0

v1 whole, which is shorter than its diff:
```python
import functools
import math

import jax
import jax.numpy as jnp
import numpy as np
from jax import lax
from jax.experimental import pallas as pl
from jax.experimental.pallas import tpu as pltpu
from jax.sharding import Mesh, PartitionSpec as P

D = 2048
HEADS = 16
FEAT = 16
HV = 128
WIN = 64
F1 = 17
GROUPS = 272
REACH = 512
QB = 256
WB = 128

EPSILON = 1e-05
MOMENTUM = 0.9
AVERAGE_OLD = 0.99 * 0.01 / (1.0 - 0.99 * 0.99)
AVERAGE_NEW = 0.01 / (1.0 - 0.99 * 0.99)
RATE_FACTORS = (0.03, 0.01, 0.01, 0.28, 0.029, 0.01)
HALF_ROOT = 0.7071067811865476
MASKED = -1e30
SCALE = HV**-0.5
BF = jnp.bfloat16
F32 = jnp.float32
NT = (((1,), (1,)), ((), ()))
TN = (((0,), (0,)), ((), ()))


def mm(left, right):
    return jnp.dot(left, right, preferred_element_type=F32)


def mm_nt(left, right):
    return lax.dot_general(left, right, NT, preferred_element_type=F32)


def mm_tn(left, right):
    return lax.dot_general(left, right, TN, preferred_element_type=F32)


def peer(values, axis, offset):
    ways = lax.axis_size(axis)
    return lax.ppermute(values, axis, [(i, i ^ offset) for i in range(ways)])


def enter(values):
    half = values.shape[0] // 2
    core, side = lax.axis_index("c"), lax.axis_index("s")
    first = lax.dynamic_slice_in_dim(values, side * half, half, 0)
    second = lax.dynamic_slice_in_dim(values, (1 - side) * half, half, 0)
    swap = [(2 * a + b, 2 * b + a) for a in range(2) for b in range(2)]
    turn = [(2 * a + b, 2 * (1 - b) + a) for a in range(2) for b in range(2)]
    same = lax.ppermute(first, ("c", "s"), swap)
    other = lax.ppermute(second, ("c", "s"), turn)
    low = core == 0
    return jnp.concatenate([jnp.where(low, same, other), jnp.where(low, other, same)], axis=1)


def leave(values):
    width = values.shape[1] // 2
    core, side = lax.axis_index("c"), lax.axis_index("s")
    low = core == 0
    same = jnp.where(low, values[:, :width], values[:, width:])
    other = jnp.where(low, values[:, width:], values[:, :width])
    swap = [(2 * a + b, 2 * b + a) for a in range(2) for b in range(2)]
    back = [(2 * (1 - b) + a, 2 * a + b) for a in range(2) for b in range(2)]
    same = lax.ppermute(same, ("c", "s"), swap)
    other = lax.ppermute(other, ("c", "s"), back)
    near = side == 0
    return jnp.concatenate([jnp.where(near, same, other), jnp.where(near, other, same)], axis=0)


def gather_t(piece):
    ways = lax.axis_size("t")
    mine = lax.axis_index("t")
    tokens, both = piece.shape
    width = both // 2
    full = jnp.zeros((tokens, 2 * ways * width), piece.dtype)
    for offset in range(ways):
        part = piece if offset == 0 else peer(piece, "t", offset)
        start = (mine ^ offset) * width
        full = lax.dynamic_update_slice(full, part[:, :width], (0, start))
        full = lax.dynamic_update_slice(full, part[:, width:], (0, ways * width + start))
    return full


def scatter_t(terms):
    ways = lax.axis_size("t")
    mine = lax.axis_index("t")
    half = terms.shape[1] // 2
    width = half // ways

    def piece(offset):
        start = (mine ^ offset) * width
        return jnp.concatenate(
            [
                lax.dynamic_slice_in_dim(terms, start, width, 1),
                lax.dynamic_slice_in_dim(terms, half + start, width, 1),
            ],
            axis=1,
        )

    total = piece(0).astype(F32)
    for offset in range(1, ways):
        total = total + peer(piece(offset).astype(BF), "t", offset).astype(F32)
    return total


def total_t(values):
    total = values
    for offset in range(1, lax.axis_size("t")):
        total = total + peer(values, "t", offset)
    return total


def gather_weight(shard):
    full = lax.all_gather(shard.astype(BF), ("s", "y", "c"), axis=0, tiled=False)
    return full.reshape(2, -1, shard.shape[1])


def scatter_grad(grads):
    stacked = jnp.stack(grads, axis=0).astype(BF)
    flat = stacked.reshape(-1, stacked.shape[2])
    return lax.psum_scatter(flat, ("s", "y", "c"), scatter_dimension=0, tiled=True).astype(F32)


def forward_body(heads, tokens, proj, pairs, far_v, far_p, far_w, docs_c, docs_r, out, den):
    lanes = heads * HV
    for i in range(heads):
        at = i * HV
        qs, ks = i * FEAT, (heads + i) * FEAT
        for b in range(tokens // QB):
            rows = slice(b * QB, (b + 1) * QB)
            q = pairs[0, rows, qs : qs + FEAT]
            docs_q = docs_c[REACH + b * QB : REACH + (b + 1) * QB, :]
            numer = jnp.zeros((QB, HV), F32)
            denom = jnp.zeros((QB, 1), F32)
            for kb in range(b - REACH // QB, b + 1):
                if kb >= 0:
                    keys = slice(kb * QB, (kb + 1) * QB)
                    k = pairs[0, keys, ks : ks + FEAT]
                    v = proj[0, keys, 3 * lanes + at : 3 * lanes + at + HV]
                else:
                    keys = slice(REACH + kb * QB, REACH + (kb + 1) * QB)
                    k = far_p[0, keys, ks : ks + FEAT]
                    v = far_v[0, keys, at : at + HV]
                inner = mm_nt(q, k) * 0.25
                kernel = 1.0 + inner + 0.5 * inner * inner
                allowed = docs_q == docs_r[:, REACH + kb * QB : REACH + (kb + 1) * QB]
                if kb == b:
                    allowed = allowed & (
                        lax.broadcasted_iota(jnp.int32, (QB, QB), 0)
                        >= lax.broadcasted_iota(jnp.int32, (QB, QB), 1)
                    )
                kernel = jnp.where(allowed, kernel, 0.0)
                denom = denom + jnp.sum(kernel, axis=1, keepdims=True)
                numer = numer + mm(kernel.astype(BF), v)
            out[0, rows, at : at + HV] = (numer / denom).astype(BF)
            den[0, rows, i : i + 1] = denom
        for b in range(tokens // WB):
            rows = slice(b * WB, (b + 1) * WB)
            q = proj[0, rows, at : at + HV]
            k, v, allowed = window_block(b, at, lanes, proj, far_w, docs_c, docs_r)
            probs = window_probs(q, k, allowed)
            out[0, rows, lanes + at : lanes + at + HV] = mm(probs.astype(BF), v).astype(BF)


def window_block(b, at, lanes, proj, far_w, docs_c, docs_r):
    if b:
        keys = slice((b - 1) * WB, (b + 1) * WB)
        k = proj[0, keys, lanes + at : lanes + at + HV]
        v = proj[0, keys, 2 * lanes + at : 2 * lanes + at + HV]
    else:
        k = jnp.concatenate(
            [far_w[0, :, at : at + HV], proj[0, :WB, lanes + at : lanes + at + HV]], axis=0
        )
        v = jnp.concatenate(
            [
                far_w[0, :, lanes + at : lanes + at + HV],
                proj[0, :WB, 2 * lanes + at : 2 * lanes + at + HV],
            ],
            axis=0,
        )
    start = REACH + b * WB
    back = (
        lax.broadcasted_iota(jnp.int32, (WB, 2 * WB), 0)
        + WB
        - lax.broadcasted_iota(jnp.int32, (WB, 2 * WB), 1)
    )
    same = docs_c[start : start + WB, :] == docs_r[:, start - WB : start + WB]
    return k, v, same & (back >= 0) & (back < WIN)


def window_probs(q, k, allowed):
    scores = jnp.where(allowed, mm_nt(q, k) * SCALE, MASKED)
    exponent = jnp.exp(scores - jnp.max(scores, axis=1, keepdims=True))
    return exponent / jnp.sum(exponent, axis=1, keepdims=True)


def backward_body(
    heads, tokens, proj, pairs, far_v, far_p, far_w, docs_c, docs_r, out, den, dout,
    dproj, dpairs, dfar_v, dfar_p, dfar_w, acc_v, acc_k, acc_wk, acc_wv,
):
    lanes = heads * HV
    lane_zero = (lax.broadcasted_iota(jnp.int32, (QB, HV), 1) == 0).astype(BF)
    for i in range(heads):
        at = i * HV
        qs, ks = i * FEAT, (heads + i) * FEAT
        acc_v[...] = jnp.zeros_like(acc_v)
        acc_k[...] = jnp.zeros_like(acc_k)
        acc_wk[...] = jnp.zeros_like(acc_wk)
        acc_wv[...] = jnp.zeros_like(acc_wv)
        for b in range(tokens // QB):
            rows = slice(b * QB, (b + 1) * QB)
            q = pairs[0, rows, qs : qs + FEAT]
            docs_q = docs_r[:, REACH + b * QB : REACH + (b + 1) * QB]
            dlin = dout[0, rows, at : at + HV].astype(F32)
            inverse = 1.0 / den[0, rows, i : i + 1]
            mean = jnp.sum(dlin * out[0, rows, at : at + HV].astype(F32), axis=1, keepdims=True)
            dnumer = (dlin * inverse).astype(BF)
            ddenom = (-mean * inverse).astype(BF)
            extended = jnp.concatenate([dnumer, ddenom * lane_zero], axis=1)
            dq = jnp.zeros((QB, FEAT), F32)
            for kb in range(b - REACH // QB, b + 1):
                place = slice(REACH + kb * QB, REACH + (kb + 1) * QB)
                if kb >= 0:
                    keys = slice(kb * QB, (kb + 1) * QB)
                    k = pairs[0, keys, ks : ks + FEAT]
                    v = proj[0, keys, 3 * lanes + at : 3 * lanes + at + HV]
                else:
                    k = far_p[0, place, ks : ks + FEAT]
                    v = far_v[0, place, at : at + HV]
                inner = mm_nt(k, q) * 0.25
                weight = mm_nt(jnp.concatenate([v, lane_zero], axis=1), extended)
                allowed = docs_c[place, :] == docs_q
                if kb == b:
                    allowed = allowed & (
                        lax.broadcasted_iota(jnp.int32, (QB, QB), 0)
                        <= lax.broadcasted_iota(jnp.int32, (QB, QB), 1)
                    )
                kernel = jnp.where(allowed, 1.0 + inner + 0.5 * inner * inner, 0.0).astype(BF)
                slope = jnp.where(allowed, weight * (0.25 + 0.25 * inner), 0.0).astype(BF)
                acc_v[place, :] += mm(kernel, dnumer)
                acc_k[place, :] += mm(slope, q)
                dq = dq + mm_tn(slope, k)
            dpairs[0, rows, qs : qs + FEAT] = dq.astype(BF)
        dfar_v[0, :, at : at + HV] = acc_v[:REACH, :].astype(BF)
        dfar_p[0, :, qs : qs + FEAT] = acc_k[:REACH, :].astype(BF)
        dproj[0, :, 3 * lanes + at : 3 * lanes + at + HV] = acc_v[REACH:, :].astype(BF)
        dpairs[0, :, ks : ks + FEAT] = acc_k[REACH:, :].astype(BF)
        for b in range(tokens // WB):
            rows = slice(b * WB, (b + 1) * WB)
            q = proj[0, rows, at : at + HV]
            k, v, allowed = window_block(b, at, lanes, proj, far_w, docs_c, docs_r)
            probs = window_probs(q, k, allowed)
            upstream = dout[0, rows, lanes + at : lanes + at + HV]
            dprobs = mm_nt(upstream, v)
            dscores = probs * (dprobs - jnp.sum(probs * dprobs, axis=1, keepdims=True))
            dscores = dscores.astype(BF)
            dproj[0, rows, at : at + HV] = (mm(dscores, k) * SCALE).astype(BF)
            span = slice(b * WB, (b + 2) * WB)
            acc_wk[span, :] += mm_tn(dscores, q)
            acc_wv[span, :] += mm_tn(probs.astype(BF), upstream)
        dfar_w[0, :, at : at + HV] = (acc_wk[:WB, :] * SCALE).astype(BF)
        dfar_w[0, :, lanes + at : lanes + at + HV] = acc_wv[:WB, :].astype(BF)
        dproj[0, :, lanes + at : lanes + at + HV] = (acc_wk[WB:, :] * SCALE).astype(BF)
        dproj[0, :, 2 * lanes + at : 2 * lanes + at + HV] = acc_wv[WB:, :].astype(BF)


def per_side(shape):
    return pl.BlockSpec((1,) + tuple(shape[1:]), lambda s: (s,) + (0,) * (len(shape) - 1))


def whole(shape):
    return pl.BlockSpec(tuple(shape), lambda s: (0,) * len(shape))


VMEM = pltpu.CompilerParams(vmem_limit_bytes=56 * 2**20)


def attention_forward(heads, proj, pairs, far_v, far_p, far_w, docs_c, docs_r):
    tokens = proj.shape[1]
    ins = (proj, pairs, far_v, far_p, far_w)
    outs = (
        jax.ShapeDtypeStruct((2, tokens, 2 * heads * HV), BF),
        jax.ShapeDtypeStruct((2, tokens, heads), F32),
    )
    return pl.pallas_call(
        functools.partial(forward_body, heads, tokens),
        grid=(2,),
        in_specs=[per_side(a.shape) for a in ins] + [whole(docs_c.shape), whole(docs_r.shape)],
        out_specs=[per_side(a.shape) for a in outs],
        out_shape=outs,
        compiler_params=VMEM,
        name="attention_forward",
    )(*ins, docs_c, docs_r)


def attention_backward(heads, proj, pairs, far_v, far_p, far_w, docs_c, docs_r, out, den, dout):
    tokens = proj.shape[1]
    ins = (proj, pairs, far_v, far_p, far_w)
    outs = tuple(jax.ShapeDtypeStruct(a.shape, BF) for a in (proj, pairs, far_v))
    outs = outs + (
        jax.ShapeDtypeStruct((2, REACH, heads * FEAT), BF),
        jax.ShapeDtypeStruct(far_w.shape, BF),
    )
    more = (out, den, dout)
    return pl.pallas_call(
        functools.partial(backward_body, heads, tokens),
        grid=(2,),
        in_specs=[per_side(a.shape) for a in ins]
        + [whole(docs_c.shape), whole(docs_r.shape)]
        + [per_side(a.shape) for a in more],
        out_specs=[per_side(a.shape) for a in outs],
        out_shape=outs,
        scratch_shapes=[
            pltpu.VMEM((REACH + tokens, HV), F32),
            pltpu.VMEM((REACH + tokens, FEAT), F32),
            pltpu.VMEM((WB + tokens, HV), F32),
            pltpu.VMEM((WB + tokens, HV), F32),
        ],
        compiler_params=VMEM,
        name="attention_backward",
    )(*ins, docs_c, docs_r, *more)


def feature_tables():
    pick_a = np.zeros((F1, F1 * F1), np.float32)
    pick_b = np.zeros((F1, F1 * F1), np.float32)
    scale = np.ones((F1 * F1,), np.float32)
    for r in range(F1):
        for j in range(F1):
            f = r * F1 + j
            pick_a[r, f] = 1.0
            if r < FEAT:
                scale[f] = HALF_ROOT
                if j < FEAT:
                    pick_b[j, f] = 1.0
            else:
                pick_b[FEAT if j == 0 else j - 1, f] = 1.0
    return pick_a, pick_b, scale


def row_states(heads, keys, values, docs):
    keys, values = keys[:, -REACH:], values[:, -REACH:]
    keys = jnp.swapaxes(keys.reshape(2, REACH, heads, FEAT), 1, 2).reshape(-1, REACH, FEAT)
    values = jnp.swapaxes(values.reshape(2, REACH, heads, HV), 1, 2).reshape(-1, REACH, HV)
    ones = jnp.ones(keys.shape[:2] + (1,), BF)
    extended = jnp.concatenate([keys * BF(0.5), ones], axis=2)
    pick_a, pick_b, scale = feature_tables()
    left = jnp.einsum("bsf,fg->bsg", extended, jnp.asarray(pick_a, BF), preferred_element_type=F32)
    right = jnp.einsum("bsf,fg->bsg", extended, jnp.asarray(pick_b, BF), preferred_element_type=F32)
    in_last = (docs[-REACH:] == docs[-1]).astype(F32)
    features = left * right * scale * in_last[None, :, None]
    return jnp.einsum("bsg,bsv->bgv", features.astype(BF), values, preferred_element_type=F32)


def owned_states(heads, states, owner):
    ways = lax.axis_size("t")
    mine_t, side = lax.axis_index("t"), lax.axis_index("s")
    states = states.astype(BF)
    near = lax.ppermute(states, ("c", "s"), [(2 + s, 2 * s) for s in range(2)])
    far = lax.ppermute(states, ("c", "s"), [(2 + s, 2 * s + 1) for s in range(2)])
    states = jnp.where(side == 0, near, far)
    slots = GROUPS // ways
    groups = jnp.arange(GROUPS, dtype=jnp.int32)
    mine = owner == side * ways + mine_t
    ordinal = jnp.sum((mine[None, :] & (groups[None, :] < groups[:, None])).astype(jnp.int32), axis=1)
    wanted = jnp.arange(slots, dtype=jnp.int32)
    picked = (mine[None, :] & (ordinal[None, :] == wanted[:, None])).astype(BF)
    picked = picked.reshape(slots, 2, ways, heads * F1)
    total = jnp.zeros((slots, F1, HV), F32)
    for offset in range(ways):
        part = states if offset == 0 else peer(states, "t", offset)
        part = part.reshape(2 * heads * F1, F1, HV)
        chosen = lax.dynamic_slice_in_dim(picked, mine_t ^ offset, 1, 2)
        chosen = chosen.reshape(slots, 2 * heads * F1)
        total = total + jnp.einsum("kg,gfv->kfv", chosen, part, preferred_element_type=F32)
    return total[None]


def momentum_update(weights, moment, average, gradient, factor, token_total):
    step_rate = factor / math.sqrt(token_total)
    moment_new = MOMENTUM * moment + gradient
    weights_new = weights - step_rate * (gradient + MOMENTUM * moment_new)
    average_new = AVERAGE_OLD * average + AVERAGE_NEW * weights_new
    return (gradient, weights_new, moment_new, average_new, weights_new.astype(BF))


def norm_back(values, factor, gains, upstream):
    gain_grad = jnp.sum(upstream * values, axis=0)
    inner = total_t(jnp.sum(upstream * gains * values, axis=1))
    scale = (factor * factor * inner / D)[:, None]
    return gains * upstream - values * scale, gain_grad


def local(
    layer_in, out_grad, doc_ids, group_owner,
    norm_gains, norm_gains_moment, norm_gains_average,
    feature_proj, feature_proj_moment, feature_proj_average,
    head_proj, head_proj_moment, head_proj_average,
    mixer_out, mixer_out_moment, mixer_out_average,
    gate_up, gate_up_moment, gate_up_average,
    down_proj, down_proj_moment, down_proj_average,
):
    data_ways = lax.axis_size("y") * 2
    core, side = lax.axis_index("c"), lax.axis_index("s")
    width = layer_in.shape[1]
    tokens = layer_in.shape[0] // 2
    heads = head_proj.shape[2] // HV
    rows = head_proj.shape[0]
    lanes = heads * HV
    token_total = layer_in.shape[0] * data_ways

    feature_full = gather_weight(feature_proj.reshape(rows, -1))
    head_full = gather_weight(head_proj.reshape(rows, -1))
    mixer_full = gather_weight(jnp.transpose(mixer_out, (2, 0, 1)).reshape(rows, -1))
    gate_full = gather_weight(gate_up[:, 0])
    up_full = gather_weight(gate_up[:, 1])
    down_full = gather_weight(jnp.transpose(down_proj))

    other_gains = lax.ppermute(norm_gains, "s", [(0, 1), (1, 0)])
    gains = jnp.where(
        side == 0,
        jnp.concatenate([norm_gains, other_gains], axis=1),
        jnp.concatenate([other_gains, norm_gains], axis=1),
    )

    x = enter(layer_in.astype(BF)).astype(F32)
    dy_mine = enter(out_grad.astype(BF))
    docs = lax.ppermute(doc_ids, ("c", "s"), [(2 * a + b, 2 * b + a) for a in range(2) for b in range(2)])
    docs = jnp.concatenate([jnp.full((1, REACH), -1, jnp.int32), docs], axis=1)
    docs_r = lax.dynamic_slice_in_dim(docs, core * tokens, REACH + tokens, 1)
    docs_c = jnp.reshape(docs_r, (REACH + tokens, 1))

    factor_one = lax.rsqrt(total_t(jnp.sum(x * x, axis=1)) / D + EPSILON)
    scaled_one = gather_t((x * gains[0]).astype(BF))
    proj = jnp.stack([(mm(scaled_one, head_full[s]) * factor_one[:, None]).astype(BF) for s in range(2)])
    pairs = jnp.stack([(mm(scaled_one, feature_full[s]) * factor_one[:, None]).astype(BF) for s in range(2)])

    ahead = [(0, 1)]
    far_v = lax.ppermute(proj[:, -REACH:, 3 * lanes :], "c", ahead)
    far_p = lax.ppermute(pairs[:, -REACH:], "c", ahead)
    far_w = lax.ppermute(proj[:, -WB:, lanes : 3 * lanes], "c", ahead)
    attended, denom = attention_forward(heads, proj, pairs, far_v, far_p, far_w, docs_c, docs_r)
    states = row_states(heads, pairs[:, :, heads * FEAT :], proj[:, :, 3 * lanes :], docs_r[0])
    row_state = owned_states(heads, states, group_owner)

    mixed = scatter_t(mm_nt(attended[0], mixer_full[0]) + mm_nt(attended[1], mixer_full[1]))
    middle = x + mixed
    factor_two = lax.rsqrt(total_t(jnp.sum(middle * middle, axis=1)) / D + EPSILON)
    scaled_two = gather_t((middle * gains[1]).astype(BF))

    dy = gather_t(dy_mine)
    hidden, dgate, dup = [], [], []
    for s in range(2):
        back = mm(dy, down_full[s])
        gate = mm(scaled_two, gate_full[s]) * factor_two[:, None]
        up = mm(scaled_two, up_full[s]) * factor_two[:, None]
        sigmoid = jax.nn.sigmoid(gate)
        active = gate * sigmoid
        hidden.append((active * up).astype(BF))
        slope = back * up * sigmoid * (1.0 + gate * (1.0 - sigmoid))
        dgate.append((slope * factor_two[:, None]).astype(BF))
        dup.append((back * active * factor_two[:, None]).astype(BF))
    terms_two = sum(mm_nt(dgate[s], gate_full[s]) + mm_nt(dup[s], up_full[s]) for s in range(2))
    upstream_two = scatter_t(terms_two)
    branch = scatter_t(mm_nt(hidden[0], down_full[0]) + mm_nt(hidden[1], down_full[1]))
    out_y = layer_in + leave((mixed + branch).astype(BF)).astype(F32)
    back_two, gain_two = norm_back(middle, factor_two, gains[1], upstream_two)
    dmixed = gather_t((dy_mine.astype(F32) + back_two).astype(BF))

    down_sum = scatter_grad([mm_tn(dy, hidden[s]) for s in range(2)])
    gate_sum = scatter_grad([mm_tn(scaled_two, dgate[s]) for s in range(2)])
    up_sum = scatter_grad([mm_tn(scaled_two, dup[s]) for s in range(2)])

    dattended = jnp.stack([mm(dmixed, mixer_full[s]).astype(BF) for s in range(2)])
    mixer_sum = scatter_grad([mm_tn(dmixed, attended[s]) for s in range(2)])
    dproj, dpairs, dfar_v, dfar_p, dfar_w = attention_backward(
        heads, proj, pairs, far_v, far_p, far_w, docs_c, docs_r, attended, denom, dattended
    )
    behind = [(1, 0)]
    dfar_v = lax.ppermute(dfar_v, "c", behind).astype(F32)
    dfar_p = lax.ppermute(dfar_p, "c", behind).astype(F32)
    dfar_w = lax.ppermute(dfar_w, "c", behind).astype(F32)
    dproj = (
        dproj.astype(F32)
        + jnp.pad(dfar_v, ((0, 0), (tokens - REACH, 0), (3 * lanes, 0)))
        + jnp.pad(dfar_w, ((0, 0), (tokens - WB, 0), (lanes, lanes)))
    )
    dpairs = dpairs.astype(F32) + jnp.pad(dfar_p, ((0, 0), (tokens - REACH, 0), (heads * FEAT, 0)))
    dproj = (dproj * factor_one[None, :, None]).astype(BF)
    dpairs = (dpairs * factor_one[None, :, None]).astype(BF)
    head_sum = scatter_grad([mm_tn(scaled_one, dproj[s]) for s in range(2)])
    feature_sum = scatter_grad([mm_tn(scaled_one, dpairs[s]) for s in range(2)])
    terms_one = sum(mm_nt(dproj[s], head_full[s]) + mm_nt(dpairs[s], feature_full[s]) for s in range(2))
    upstream_one = scatter_t(terms_one)
    back_one, gain_one = norm_back(x, factor_one, gains[0], upstream_one)
    grad_x = out_grad + leave((back_one + back_two).astype(BF)).astype(F32)

    both = jnp.stack([gain_one, gain_two], axis=0)
    gains_sum = lax.dynamic_slice_in_dim(both, side * width, width, 1)
    holders = 2 * data_ways
    for offset in range(1, holders):
        theirs = lax.dynamic_slice_in_dim(both, (side ^ (offset & 1)) * width, width, 1)
        gains_sum = gains_sum + lax.ppermute(
            theirs, ("y", "c", "s"), [(i, i ^ offset) for i in range(holders)]
        )

    mixer_sum = jnp.transpose(mixer_sum.reshape(rows, 2, lanes), (1, 2, 0))
    triples = (
        (norm_gains, norm_gains_moment, norm_gains_average, gains_sum),
        (feature_proj, feature_proj_moment, feature_proj_average, feature_sum.reshape(feature_proj.shape)),
        (head_proj, head_proj_moment, head_proj_average, head_sum.reshape(head_proj.shape)),
        (mixer_out, mixer_out_moment, mixer_out_average, mixer_sum),
        (gate_up, gate_up_moment, gate_up_average, jnp.stack([gate_sum, up_sum], axis=1)),
        (down_proj, down_proj_moment, down_proj_average, jnp.transpose(down_sum)),
    )
    results = [out_y, grad_x, row_state]
    for index, triple in enumerate(triples):
        results.extend(momentum_update(*triple, RATE_FACTORS[index], token_total))
    return tuple(results)


def solution(mesh):
    data_ways, model_ways = mesh.shape["dp"], mesh.shape["mp"]
    grid = Mesh(mesh.devices.reshape(data_ways // 2, 2, 2, model_ways // 2), ("y", "c", "s", "t"))
    dp, mp = ("y", "c"), ("s", "t")
    gains = (P(None, mp),)
    rows_cols = (P(dp, None, mp),)
    mixer = (P(None, mp, dp),)
    down = (P(mp, dp),)
    tokens = (P(dp, mp),)
    return jax.shard_map(
        local,
        mesh=grid,
        in_specs=tokens * 2
        + (P(dp, None), P())
        + gains * 3
        + rows_cols * 6
        + mixer * 3
        + rows_cols * 3
        + down * 3,
        out_specs=tokens * 2
        + (P(dp, mp, None, None),)
        + gains * 5
        + rows_cols * 10
        + mixer * 5
        + rows_cols * 5
        + down * 5,
        check_vma=False,
    )
```

time: 7870 us -> 1200 us (0.15)
  matrix products: 2440 us -> 207 us
  local copies, waits for them, and re-layouts: 2170 us -> 90.2 us
  waiting for transfers between devices: 2560 us -> 545 us
  other arithmetic: 412 us -> 86.3 us
  starting transfers between devices: 0.96 us -> 104 us
  loops' own time: 91.2 us -> 0 us
    dot_general x452 -> x42, matrix products: 2440 us -> 207 us  [the longest x12 77.6 us: mm_nt(): return lax.dot_general(left, right, NT, preferred_element_type=F32)]
    dynamic_update_slice x112 -> x30, local copies, waits for them, and re-layouts: 1060 us -> 19.7 us  [the longest x15 9.92 us: gather_t(): lax.dynamic_update_slice(full, part[:, width:], (0, ways * width + start))]
    reduce_scatter x6, waiting for transfers between devices: 1140 us -> 177 us  [scatter_grad(): lax.psum_scatter(flat, ('s', 'y', 'c'), scatter_dimension=0, tiled=True)]
    psum x2 -> x0, waiting for transfers between devices: 734 us -> none  [the longest x1 500 us: local(): numer_total, denom_total = lax.psum((numer_part, denom_part), 'mp')]
    all_gather x11 -> x5, waiting for transfers between devices: 689 us -> 0.01 us  [gather_weight(): lax.all_gather(shard.astype(BF), ('s', 'y', 'c'), axis=0, tiled=False)]
    transpose x84 -> x1, local copies, waits for them, and re-layouts: 414 us -> 1.25 us  [local(): mixer_sum = jnp.transpose(mixer_sum.reshape(rows, 2, lanes), (1, 2, 0))]
    ppermute x0 -> x64, waiting for transfers between devices: none -> 369 us  [the longest x39 356 us: peer(): return lax.ppermute(values, axis, [(i, i ^ offset) for i in range(ways)])]
    dynamic_slice x122 -> x8, local copies, waits for them, and re-layouts: 212 us -> 7.28 us  [the longest x4 4.58 us: piece(): lax.dynamic_slice_in_dim(terms, start, width, 1)]
  transfers between devices with their start and end apart: 19 -> 75, of which waited for: 18 -> 28; matrix products, arithmetic and copies ran while one was open for 6% -> 23% of each run, Pallas kernels for 0% -> 1%
where the time goes in v1:
time: 1200 us; the launch traced here: 1190 us
  waiting for transfers between devices  545 us (45%)
  matrix products  207 us (17%)
  starting transfers between devices  104 us (9%)
  blocking collectives  94 us (8%)
  local copies, waits for them, and re-layouts  90.2 us (8%)
  other arithmetic  86.3 us (7%)
  Pallas kernels  50.5 us (4%)
  between operations  16.5 us (1%)
    ppermute x39, waiting for transfers between devices, peer(): return lax.ppermute(values, axis, [(i, i ^ offset) for i in range(ways)])  356 us
    reduce_scatter x6, waiting for transfers between devices, scatter_grad(): lax.psum_scatter(flat, ('s', 'y', 'c'), scatter_dimension=0, tiled=True)  177 us
    all_gather x1, blocking collectives, gather_weight(): lax.all_gather(shard.astype(BF), ('s', 'y', 'c'), axis=0, tiled=False)  94 us
    dot_general x12, matrix products, mm_nt(): return lax.dot_general(left, right, NT, preferred_element_type=F32)  77.6 us
    dot_general x12, matrix products, mm(): return jnp.dot(left, right, preferred_element_type=F32)  67.6 us
    dot_general x12, matrix products, mm_tn(): return lax.dot_general(left, right, TN, preferred_element_type=F32)  55.7 us
    ppermute x39, starting transfers between devices, peer(): return lax.ppermute(values, axis, [(i, i ^ offset) for i in range(ways)])  48.6 us
    pallas_call x1, Pallas kernels, attention_backward(): pl.pallas_call(functools.partial(backward_body, heads, tokens), grid=(2,)...  35.7 us
  transfers between devices with their start and end apart: 75, of which 28 were waited for; matrix products, arithmetic and copies ran while one was open for 23% of the time, Pallas kernels for 1%

profile of v1, /device:TPU:0, one launch (start us, length us, event | category | flops | bytes accessed | tf_op | source)
XLA Modules:
  0.0 1193.5 jit_solution(7729612239310460872)
XLA Ops:
  30.1 94.0 %all_gather.27 = bf16[8,512,64]{1,2,0:T(8,128)(2,1)S(1)} all-gather(bf16[1,512,64]{1,2,0:T(8,128)(2,1)S(1)} %bitcast.230), channel_id=1, replica_groups=mesh['y'=2,'c'=2,'s'=2,'t'=4] {'s','y','c'}, dimensions={0}, use_global_device_ids=true | all-gather | bytes 589824 | tf_op jit(solution)/shard_map/all_gather | solution.py:125
  156.7 14.0 %collective-permute-done.4 = bf16[1024,512]{1,0:T(8,128)(2,1)S(1)} collective-permute-done((bf16[1024,512]{1,0:T(8,128)(2,1)S(1)}, bf16[1024,512]{1,0:T(8,128)(2,1)S(1)}, u32[]{:S(2)}, u32[]{:S(2)}) %collective-permute-start.4) | collective-permute-done | bytes 1048608 | tf_op jit(solution)/shard_map/ppermute | solution.py:51
  170.8 34.4 %collective-permute-done.5 = bf16[1024,512]{1,0:T(8,128)(2,1)S(1)} collective-permute-done((bf16[1024,512]{1,0:T(8,128)(2,1)S(1)}, bf16[1024,512]{1,0:T(8,128)(2,1)S(1)}, u32[]{:S(2)}, u32[]{:S(2)}) %collective-permute-start.5) | collective-permute-done | bytes 1048608 | tf_op jit(solution)/shard_map/ppermute | solution.py:51
  241.2 14.8 %attention_forward.1 = (bf16[2,1024,512]{2,1,0:T(8,128)(2,1)}, f32[2,1024,2]{2,1,0:T(8,128)}) custom-call(bf16[2,1024,1024]{2,1,0:T(8,128)(2,1)} %pad_maximum_fusion.1.proj, bf16[2,1024,64]{2,1,0:T(8,128)(2,1)} %pad_maximum_fusion.18.pairs, bf16[2,512,256]{2,1,0:T(8,128)(2,1)} %collective-permute-done.9.far_v, bf16[2,512,64]{2,1,0:T(8,128)(2,1)} %copy-done.80, ...), custom_call_target="tpu_custom_call" | custom-call | tf_op jit(solution)/shard_map/attention_forward/pallas_call | solution.py:296
  277.6 25.1 %collective-permute-done.14 = bf16[1024,512]{1,0:T(8,128)(2,1)S(1)} collective-permute-done((bf16[1024,512]{1,0:T(8,128)(2,1)S(1)}, bf16[1024,512]{1,0:T(8,128)(2,1)S(1)}, u32[]{:S(2)}, u32[]{:S(2)}) %collective-permute-start.14) | collective-permute-done | bytes 1048608 | tf_op jit(solution)/shard_map/ppermute | solution.py:51
  302.7 38.6 %collective-permute-done.15 = bf16[1024,512]{1,0:T(8,128)(2,1)S(1)} collective-permute-done((bf16[1024,512]{1,0:T(8,128)(2,1)S(1)}, bf16[1024,512]{1,0:T(8,128)(2,1)S(1)}, u32[]{:S(2)}, u32[]{:S(2)}) %collective-permute-start.15) | collective-permute-done | bytes 1048608 | tf_op jit(solution)/shard_map/ppermute | solution.py:51
  343.8 8.3 fusion.22
  372.3 26.7 %collective-permute-done.17 = bf16[1024,512]{1,0:T(8,128)(2,1)S(1)} collective-permute-done((bf16[1024,512]{1,0:T(8,128)(2,1)S(1)}, bf16[1024,512]{1,0:T(8,128)(2,1)S(1)}, u32[]{:S(2)}, u32[]{:S(2)}) %collective-permute-start.17) | collective-permute-done | bytes 1048608 | tf_op jit(solution)/shard_map/ppermute | solution.py:51
  400.7 22.3 %collective-permute-done.18 = bf16[1024,512]{1,0:T(8,128)(2,1)S(1)} collective-permute-done((bf16[1024,512]{1,0:T(8,128)(2,1)S(1)}, bf16[1024,512]{1,0:T(8,128)(2,1)S(1)}, u32[]{:S(2)}, u32[]{:S(2)}) %collective-permute-start.18) | collective-permute-done | bytes 1048608 | tf_op jit(solution)/shard_map/ppermute | solution.py:51
  424.7 8.2 fusion.16
  432.9 6.9 fusion.13
  439.8 8.0 fusion.15
  447.8 7.1 fusion.11
  454.9 12.6 %multiply_convert_fusion.3 = (bf16[1024,704]{0,1:T(8,128)(2,1)S(1)}, bf16[1024,704]{0,1:T(8,128)(2,1)}, bf16[1024,704]{0,1:T(8,128)(2,1)S(1)}, bf16[1024,704]{0,...) fusion(f32[1024]{0:T(1024)S(1)} %add_rsqrt_fusion, f32[1024,704]{0,1:T(8,128)} %fusion.15, ...), kind=kOutput, calls=%fused_computation.50 | convolution fusion | flops 2980184064 | bytes 30150656 | tf_op jit(solution)/shard_map/dot_general | solution.py:38
  473.6 7.7 fusion.10
  496.8 11.9 add_add_fusion.1
  518.0 22.0 %collective-permute-done.33 = bf16[1024,512]{1,0:T(8,128)(2,1)S(1)} collective-permute-done((bf16[1024,512]{1,0:T(8,128)(2,1)S(1)}, bf16[1024,512]{1,0:T(8,128)(2,1)S(1)}, u32[]{:S(2)}, u32[]{:S(2)}) %collective-permute-start.33) | collective-permute-done | bytes 1048608 | tf_op jit(solution)/shard_map/ppermute | solution.py:51
  540.0 20.8 %collective-permute-done.34 = bf16[1024,512]{1,0:T(8,128)(2,1)S(1)} collective-permute-done((bf16[1024,512]{1,0:T(8,128)(2,1)S(1)}, bf16[1024,512]{1,0:T(8,128)(2,1)S(1)}, u32[]{:S(2)}, u32[]{:S(2)}) %collective-permute-start.34) | collective-permute-done | bytes 1048608 | tf_op jit(solution)/shard_map/ppermute | solution.py:51
  575.0 21.2 %collective-permute-done.38 = bf16[1024,512]{1,0:T(8,128)(2,1)S(1)} collective-permute-done((bf16[1024,512]{1,0:T(8,128)(2,1)S(1)}, bf16[1024,512]{1,0:T(8,128)(2,1)S(1)}, u32[]{:S(2)}, u32[]{:S(2)}) %collective-permute-start.38) | collective-permute-done | bytes 1048608 | tf_op jit(solution)/shard_map/ppermute | solution.py:51
  598.0 16.2 %collective-permute-done.40 = bf16[1024,512]{1,0:T(8,128)(2,1)S(1)} collective-permute-done((bf16[1024,512]{1,0:T(8,128)(2,1)S(1)}, bf16[1024,512]{1,0:T(8,128)(2,1)S(1)}, u32[]{:S(2)}, u32[]{:S(2)}) %collective-permute-start.40) | collective-permute-done | bytes 1048608 | tf_op jit(solution)/shard_map/ppermute | solution.py:51
  621.2 35.7 %attention_backward.1 = (bf16[2,1024,1024]{2,1,0:T(8,128)(2,1)}, bf16[2,1024,64]{2,1,0:T(8,128)(2,1)}, bf16[2,512,256]{2,1,0:T(8,128)(2,1)}, bf16[2,512,32]{2,1,0:T(8,128)(2,1)}, bf16[2,128,512]{2,1,0:T(8,128)(2,1)}) custom-call(bf16[2,1024,1024]{2,1,0:T(8,128)(2,1)} %pad_maximum_fusion.1.proj, bf16[2,1024,64]{2,1,0:T(8,128)(2,1)} %pad_maximum_fusion.18.pairs, ...), custom_call_target="tpu_custom_call" | custom-call | tf_op jit(solution)/shard_map/attention_backward/pallas_call | solution.py:316
  745.3 18.0 %collective-permute-done.55 = bf16[4,289,128]{2,1,0:T(8,128)(2,1)} collective-permute-done((bf16[4,289,128]{2,1,0:T(8,128)(2,1)S(1)}, bf16[4,289,128]{2,1,0:T(8,128)(2,1)}, u32[]{:S(2)}, u32[]{:S(2)}) %collective-permute-start.55) | collective-permute-done | bytes 295968 | tf_op jit(solution)/shard_map/ppermute | solution.py:51
  791.5 6.7 pad_maximum_fusion
  805.0 17.9 %collective-permute-done.23 = bf16[1024,512]{1,0:T(8,128)(2,1)} collective-permute-done((bf16[1024,512]{1,0:T(8,128)(2,1)}, bf16[1024,512]{1,0:T(8,128)(2,1)}, u32[]{:S(2)}, u32[]{:S(2)}) %collective-permute-start.23) | collective-permute-done | bytes 1048608 | tf_op jit(solution)/shard_map/ppermute | solution.py:51
  828.5 16.1 %collective-permute-start.26 = (bf16[1024,256]{1,0:T(8,128)(2,1)S(1)}, bf16[1024,256]{1,0:T(8,128)(2,1)S(1)}, u32[]{:S(2)}, u32[]{:S(2)}) collective-permute-start(bf16[1024,256]{1,0:T(8,128)(2,1)S(1)} %get-tuple-element.301), channel_id=1, source_target_pairs={{8,0},{0,4},{12,8},{4,12},{9,1},{1,5},{13,9},{5,13},{10,2},{2,6},{... | collective-permute-start | bytes 1572872 | tf_op jit(solution)/shard_map/ppermute | solution.py:76
  855.6 6.9 fusion.43
  862.6 13.5 %add_add_fusion = f32[1024,2048]{1,0:T(8,128)} fusion(f32[1024,2048]{1,0:T(8,128)} %fusion.84, f32[1024,2048]{1,0:T(8,128)} %fusion.43, f32[1024,2048]{1,0:T(8,128)} %fusion.83, bf16[2048,1024]{1,0:T(8,128)(2,1)S(1)} %bitcast.209, bf16[2,1024,1024]{2,1,0:T(8,128)(2,1)} %copy-done.22), kind=kOutput, calls=%fused_computation.1 | convolution fusion | flops 4301258752 | bytes 39845888 | tf_op jit(solution)/shard_map/dot_general | solution.py:42
  891.6 15.6 %collective-permute-done.45 = bf16[1024,512]{1,0:T(8,128)(2,1)} collective-permute-done((bf16[1024,512]{1,0:T(8,128)(2,1)}, bf16[1024,512]{1,0:T(8,128)(2,1)}, u32[]{:S(2)}, u32[]{:S(2)}) %collective-permute-start.45) | collective-permute-done | bytes 1048608 | tf_op jit(solution)/shard_map/ppermute | solution.py:51
  907.2 37.1 %collective-permute-done.46 = bf16[1024,512]{1,0:T(8,128)(2,1)} collective-permute-done((bf16[1024,512]{1,0:T(8,128)(2,1)}, bf16[1024,512]{1,0:T(8,128)(2,1)}, u32[]{:S(2)}, u32[]{:S(2)}) %collective-permute-start.46) | collective-permute-done | bytes 1048608 | tf_op jit(solution)/shard_map/ppermute | solution.py:51
  967.1 8.2 collective-permute-done.51
  989.0 78.2 %reduce-scatter.15.cloned.1.call-done = bf16[512,704]{0,1:T(8,128)(2,1)} async-done(((bf16[4096,704]{0,1:T(8,128)(2,1)}), bf16[512,704]{0,1:T(8,128)(2,1)}) %reduce-scatter.15.cloned.1.call-update) | async-done | bytes 720912 | tf_op jit(solution)/shard_map/reduce_scatter | solution.py:132
  1077.4 98.4 %reduce-scatter.9.cloned.1.call-done = bf16[512,1024]{1,0:T(8,128)(2,1)} async-done(((bf16[4096,1024]{1,0:T(8,128)(2,1)}), bf16[512,1024]{1,0:T(8,128)(2,1)}) %reduce-scatter.9.cloned.1.call-update) | async-done | bytes 1048592 | tf_op jit(solution)/shard_map/reduce_scatter | solution.py:132
  (584 shorter events, 404.2 us)
Async XLA Ops:
  7.2 206.8 %all-gather.9.cloned.1.call-start = ((), (), s32[]{:S(2)}) async-start(), calls=%async_computation.6 | async-start | bytes 9437184 | tf_op jit(solution)/shard_map/all_gather | solution.py:125
  10.8 223.1 %all-gather.11.cloned.1.call-start = ((), (), s32[]{:S(2)}) async-start(), calls=%async_computation.7 | async-start | bytes 4718592 | tf_op jit(solution)/shard_map/all_gather | solution.py:125
  13.3 330.5 %all-gather.17.cloned.1.call-start = ((), (), s32[]{:S(2)}) async-start(), calls=%async_computation.16 | async-start | bytes 6488064 | tf_op jit(solution)/shard_map/all_gather | solution.py:125
  15.7 409.0 %all-gather.15.cloned.1.call-start = ((), (), s32[]{:S(2)}) async-start(), calls=%async_computation.15 | async-start | bytes 6488064 | tf_op jit(solution)/shard_map/all_gather | solution.py:125
  17.2 422.6 %all-gather.13.cloned.1.call-start = ((), (), s32[]{:S(2)}) async-start(), calls=%async_computation.14 | async-start | bytes 6488064 | tf_op jit(solution)/shard_map/all_gather | solution.py:125
  17.3 107.0 %collective-permute-start.2 = (f32[2,256]{1,0:T(2,128)S(1)}, f32[2,256]{1,0:T(2,128)S(1)}, u32[]{:S(2)}, u32[]{:S(2)}) collective-permute-start(f32[2,256]{1,0:T(2,128)S(1)} %copy-done.98), channel_id=1, source_target_pairs={{0,4},{4,0},{1,5},{5,1},{2,6},{6,2},{3,7},{7,3},{8,12},{12,8},{9,1... | collective-permute-start | bytes 6152 | tf_op jit(solution)/shard_map/ppermute | solution.py:430
  21.4 104.6 %collective-permute-start.12 = (s32[1,2048]{1,0:T(1,128)S(1)}, s32[1,2048]{1,0:T(1,128)S(1)}, u32[]{:S(2)}, u32[]{:S(2)}) collective-permute-start(s32[1,2048]{1,0:T(1,128)S(1)} %copy-done.106), channel_id=1, source_target_pairs={{0,0},{4,8},{8,4},{12,12},{1,1},{5,9},{9,5},{13,13},{2,2},{6,10},{... | collective-permute-start | bytes 24584 | tf_op jit(solution)/shard_map/ppermute | solution.py:439
  23.2 104.6 %collective-permute-start = (bf16[1024,256]{1,0:T(8,128)(2,1)}, bf16[1024,256]{1,0:T(8,128)(2,1)S(1)}, u32[]{:S(2)}, u32[]{:S(2)}) collective-permute-start(bf16[1024,256]{1,0:T(8,128)(2,1)} %get-tuple-element.306), channel_id=1, source_target_pairs={{0,0},{4,8},{8,4},{12,12},{1,1},{5,9},{9,5},{13,13},{2,2},{6,10},{... | collective-permute-start | bytes 1572872 | tf_op jit(solution)/shard_map/ppermute | solution.py:61
  25.0 102.8 %collective-permute-start.1 = (bf16[1024,256]{1,0:T(8,128)(2,1)}, bf16[1024,256]{1,0:T(8,128)(2,1)}, u32[]{:S(2)}, u32[]{:S(2)}) collective-permute-start(bf16[1024,256]{1,0:T(8,128)(2,1)} %get-tuple-element.307), channel_id=1, source_target_pairs={{0,8},{4,0},{8,12},{12,4},{1,9},{5,1},{9,13},{13,5},{2,10},{6,2},{... | collective-permute-start | bytes 1572872 | tf_op jit(solution)/shard_map/ppermute | solution.py:62
  29.9 103.0 %collective-permute-start.28 = (bf16[1024,256]{1,0:T(8,128)(2,1)}, bf16[1024,256]{1,0:T(8,128)(2,1)S(1)}, u32[]{:S(2)}, u32[]{:S(2)}) collective-permute-start(bf16[1024,256]{1,0:T(8,128)(2,1)} %get-tuple-element.296), channel_id=1, source_target_pairs={{0,8},{4,0},{8,12},{12,4},{1,9},{5,1},{9,13},{13,5},{2,10},{6,2},{... | collective-permute-start | bytes 1572872 | tf_op jit(solution)/shard_map/ppermute | solution.py:62
  30.0 860.0 %reduce-scatter.7.cloned.1.call-start = ((), (), s32[]{:S(2)}) async-start(), calls=%async_computation.8 | async-start | bytes 589824 | tf_op jit(solution)/shard_map/reduce_scatter | solution.py:132
  140.7 64.5 %collective-permute-start.5 = (bf16[1024,512]{1,0:T(8,128)(2,1)S(1)}, bf16[1024,512]{1,0:T(8,128)(2,1)S(1)}, u32[]{:S(2)}, u32[]{:S(2)}) collective-permute-start(bf16[1024,512]{1,0:T(8,128)(2,1)S(1)} %get-tuple-element.302), channel_id=1, source_target_pairs={{0,3},{1,2},{2,1},{3,0},{4,7},{5,6},{6,5},{7,4},{8,11},{9,10},{10,... | collective-permute-start | bytes 3145736 | tf_op jit(solution)/shard_map/ppermute | solution.py:51
  142.6 124.0 %collective-permute-start.30 = (bf16[1024,512]{1,0:T(8,128)(2,1)}, bf16[1024,512]{1,0:T(8,128)(2,1)}, u32[]{:S(2)}, u32[]{:S(2)}) collective-permute-start(bf16[1024,512]{1,0:T(8,128)(2,1)} %pad_maximum_fusion.11), channel_id=1, source_target_pairs={{0,2},{1,3},{2,0},{3,1},{4,6},{5,7},{6,4},{7,5},{8,10},{9,11},{10,... | collective-permute-start | bytes 3145736 | tf_op jit(solution)/shard_map/ppermute | solution.py:51
  142.7 69.6 %collective-permute-start.29 = (bf16[1024,512]{1,0:T(8,128)(2,1)}, bf16[1024,512]{1,0:T(8,128)(2,1)S(1)}, u32[]{:S(2)}, u32[]{:S(2)}) collective-permute-start(bf16[1024,512]{1,0:T(8,128)(2,1)} %pad_maximum_fusion.11), channel_id=1, source_target_pairs={{0,1},{1,0},{2,3},{3,2},{4,5},{5,4},{6,7},{7,6},{8,9},{9,8},{10,11... | collective-permute-start | bytes 3145736 | tf_op jit(solution)/shard_map/ppermute | solution.py:51
  150.7 122.8 %collective-permute-start.31 = (bf16[1024,512]{1,0:T(8,128)(2,1)}, bf16[1024,512]{1,0:T(8,128)(2,1)}, u32[]{:S(2)}, u32[]{:S(2)}) collective-permute-start(bf16[1024,512]{1,0:T(8,128)(2,1)} %pad_maximum_fusion.11), channel_id=1, source_target_pairs={{0,3},{1,2},{2,1},{3,0},{4,7},{5,6},{6,5},{7,4},{8,11},{9,10},{10,... | collective-permute-start | bytes 3145736 | tf_op jit(solution)/shard_map/ppermute | solution.py:51
  262.9 78.5 %collective-permute-start.15 = (bf16[1024,512]{1,0:T(8,128)(2,1)S(1)}, bf16[1024,512]{1,0:T(8,128)(2,1)S(1)}, u32[]{:S(2)}, u32[]{:S(2)}) collective-permute-start(bf16[1024,512]{1,0:T(8,128)(2,1)S(1)} %pad_maximum_fusion.7), channel_id=1, source_target_pairs={{0,3},{1,2},{2,1},{3,0},{4,7},{5,6},{6,5},{7,4},{8,11},{9,10},{10,... | collective-permute-start | bytes 3145736 | tf_op jit(solution)/shard_map/ppermute | solution.py:51
  265.3 76.0 %collective-permute-start.13 = (bf16[1024,512]{1,0:T(8,128)(2,1)S(1)}, bf16[1024,512]{1,0:T(8,128)(2,1)S(1)}, u32[]{:S(2)}, u32[]{:S(2)}) collective-permute-start(bf16[1024,512]{1,0:T(8,128)(2,1)S(1)} %pad_maximum_fusion.5), channel_id=1, source_target_pairs={{0,1},{1,0},{2,3},{3,2},{4,5},{5,4},{6,7},{7,6},{8,9},{9,8},{10,11... | collective-permute-start | bytes 3145736 | tf_op jit(solution)/shard_map/ppermute | solution.py:51
  359.9 63.0 %collective-permute-start.18 = (bf16[1024,512]{1,0:T(8,128)(2,1)S(1)}, bf16[1024,512]{1,0:T(8,128)(2,1)S(1)}, u32[]{:S(2)}, u32[]{:S(2)}) collective-permute-start(bf16[1024,512]{1,0:T(8,128)(2,1)S(1)} %multiply_convert_fusion.10), channel_id=1, source_target_pairs={{0,3},{1,2},{2,1},{3,0},{4,7},{5,6},{6,5},{7,4},{8,11},{9,10},{10,... | collective-permute-start | bytes 3145736 | tf_op jit(solution)/shard_map/ppermute | solution.py:51
  514.0 46.8 %collective-permute-start.34 = (bf16[1024,512]{1,0:T(8,128)(2,1)S(1)}, bf16[1024,512]{1,0:T(8,128)(2,1)S(1)}, u32[]{:S(2)}, u32[]{:S(2)}) collective-permute-start(bf16[1024,512]{1,0:T(8,128)(2,1)S(1)} %pad_maximum_fusion.14), channel_id=1, source_target_pairs={{0,3},{1,2},{2,1},{3,0},{4,7},{5,6},{6,5},{7,4},{8,11},{9,10},{10,... | collective-permute-start | bytes 3145736 | tf_op jit(solution)/shard_map/ppermute | solution.py:51
  516.3 46.1 %collective-permute-start.32 = (bf16[1024,512]{1,0:T(8,128)(2,1)S(1)}, bf16[1024,512]{1,0:T(8,128)(2,1)S(1)}, u32[]{:S(2)}, u32[]{:S(2)}) collective-permute-start(bf16[1024,512]{1,0:T(8,128)(2,1)S(1)} %pad_maximum_fusion.12), channel_id=1, source_target_pairs={{0,1},{1,0},{2,3},{3,2},{4,5},{5,4},{6,7},{7,6},{8,9},{9,8},{10,11... | collective-permute-start | bytes 3145736 | tf_op jit(solution)/shard_map/ppermute | solution.py:51
  665.3 311.6 %reduce-scatter.11.cloned.1.call-start = ((), (), s32[]{:S(2)}) async-start(), calls=%async_computation.10 | async-start | bytes 4718592 | tf_op jit(solution)/shard_map/reduce_scatter | solution.py:132
  672.5 310.4 %reduce-scatter.17.cloned.1.call-start = ((), (), s32[]{:S(2)}) async-start(), calls=%async_computation.13 | async-start | bytes 6488064 | tf_op jit(solution)/shard_map/reduce_scatter | solution.py:132
  688.7 300.3 %reduce-scatter.13.cloned.1.call-start = ((), (), s32[]{:S(2)}) async-start(), calls=%async_computation.11 | async-start | bytes 6488064 | tf_op jit(solution)/shard_map/reduce_scatter | solution.py:132
  704.1 363.1 %reduce-scatter.15.cloned.1.call-start = ((), (), s32[]{:S(2)}) async-start(), calls=%async_computation.12 | async-start | bytes 6488064 | tf_op jit(solution)/shard_map/reduce_scatter | solution.py:132
  720.7 455.0 %reduce-scatter.9.cloned.1.call-start = ((), (), s32[]{:S(2)}) async-start(), calls=%async_computation.9 | async-start | bytes 9437184 | tf_op jit(solution)/shard_map/reduce_scatter | solution.py:132
  739.1 60.4 %collective-permute-start.54 = (bf16[4,289,128]{2,1,0:T(8,128)(2,1)S(1)}, bf16[4,289,128]{2,1,0:T(8,128)(2,1)}, u32[]{:S(2)}, u32[]{:S(2)}) collective-permute-start(bf16[4,289,128]{2,1,0:T(8,128)(2,1)S(1)} %broadcast_select_fusion.12), channel_id=1, source_target_pairs={{0,1},{1,0},{2,3},{3,2},{4,5},{5,4},{6,7},{7,6},{8,9},{9,8},{10,11... | collective-permute-start | bytes 887816 | tf_op jit(solution)/shard_map/ppermute | solution.py:51
  771.2 51.7 %collective-permute-start.23 = (bf16[1024,512]{1,0:T(8,128)(2,1)}, bf16[1024,512]{1,0:T(8,128)(2,1)}, u32[]{:S(2)}, u32[]{:S(2)}) collective-permute-start(bf16[1024,512]{1,0:T(8,128)(2,1)} %pad_maximum_fusion.9), channel_id=1, source_target_pairs={{0,2},{1,3},{2,0},{3,1},{4,6},{5,7},{6,4},{7,5},{8,10},{9,11},{10,... | collective-permute-start | bytes 3145736 | tf_op jit(solution)/shard_map/ppermute | solution.py:51
  775.4 47.5 %collective-permute-start.22 = (bf16[1024,512]{1,0:T(8,128)(2,1)}, bf16[1024,512]{1,0:T(8,128)(2,1)}, u32[]{:S(2)}, u32[]{:S(2)}) collective-permute-start(bf16[1024,512]{1,0:T(8,128)(2,1)} %pad_maximum_fusion.8), channel_id=1, source_target_pairs={{0,1},{1,0},{2,3},{3,2},{4,5},{5,4},{6,7},{7,6},{8,9},{9,8},{10,11... | collective-permute-start | bytes 3145736 | tf_op jit(solution)/shard_map/ppermute | solution.py:51
  826.9 59.7 %collective-permute-start.25 = (bf16[1024,256]{1,0:T(8,128)(2,1)}, bf16[1024,256]{1,0:T(8,128)(2,1)S(1)}, u32[]{:S(2)}, u32[]{:S(2)}) collective-permute-start(bf16[1024,256]{1,0:T(8,128)(2,1)} %get-tuple-element.300), channel_id=1, source_target_pairs={{0,0},{4,8},{8,4},{12,12},{1,1},{5,9},{9,5},{13,13},{2,2},{6,10},{... | collective-permute-start | bytes 1572872 | tf_op jit(solution)/shard_map/ppermute | solution.py:75
  828.5 58.0 %collective-permute-start.26 = (bf16[1024,256]{1,0:T(8,128)(2,1)S(1)}, bf16[1024,256]{1,0:T(8,128)(2,1)S(1)}, u32[]{:S(2)}, u32[]{:S(2)}) collective-permute-start(bf16[1024,256]{1,0:T(8,128)(2,1)S(1)} %get-tuple-element.301), channel_id=1, source_target_pairs={{8,0},{0,4},{12,8},{4,12},{9,1},{1,5},{13,9},{5,13},{10,2},{2,6},{... | collective-permute-start | bytes 1572872 | tf_op jit(solution)/shard_map/ppermute | solution.py:76
  884.0 60.3 %collective-permute-start.46 = (bf16[1024,512]{1,0:T(8,128)(2,1)}, bf16[1024,512]{1,0:T(8,128)(2,1)}, u32[]{:S(2)}, u32[]{:S(2)}) collective-permute-start(bf16[1024,512]{1,0:T(8,128)(2,1)} %pad_maximum_fusion.17), channel_id=1, source_target_pairs={{0,3},{1,2},{2,1},{3,0},{4,7},{5,6},{6,5},{7,4},{8,11},{9,10},{10,... | collective-permute-start | bytes 3145736 | tf_op jit(solution)/shard_map/ppermute | solution.py:51
  885.0 59.2 %collective-permute-start.44 = (bf16[1024,512]{1,0:T(8,128)(2,1)}, bf16[1024,512]{1,0:T(8,128)(2,1)}, u32[]{:S(2)}, u32[]{:S(2)}) collective-permute-start(bf16[1024,512]{1,0:T(8,128)(2,1)} %pad_maximum_fusion.15), channel_id=1, source_target_pairs={{0,1},{1,0},{2,3},{3,2},{4,5},{5,4},{6,7},{7,6},{8,9},{9,8},{10,11... | collective-permute-start | bytes 3145736 | tf_op jit(solution)/shard_map/ppermute | solution.py:51
  (167 other events, 3548.4 us)
Sparse Core Ops, SparseCore 0:
  10.9 129.5 all-gather.8
  143.0 52.6 all-gather.10
  198.1 68.6 all-gather.16
  269.1 67.5 all-gather.14
  339.1 66.5 all-gather.12
  665.4 34.4 reduce-scatter.6
  703.6 75.0 reduce-scatter.10
  782.2 100.5 reduce-scatter.16
  886.6 94.9 reduce-scatter.12
  984.9 82.2 reduce-scatter.14
  1071.0 104.6 reduce-scatter.8

commit v2 on v1

v2 whole, which is shorter than its diff:
```python
import functools
import math

import jax
import jax.numpy as jnp
import numpy as np
from jax import lax
from jax.experimental import pallas as pl
from jax.experimental.pallas import tpu as pltpu
from jax.sharding import Mesh, PartitionSpec as P

D = 2048
HEADS = 16
FEAT = 16
HV = 128
WIN = 64
F1 = 17
GROUPS = 272
REACH = 512
QB = 256
WB = 128

EPSILON = 1e-05
MOMENTUM = 0.9
AVERAGE_OLD = 0.99 * 0.01 / (1.0 - 0.99 * 0.99)
AVERAGE_NEW = 0.01 / (1.0 - 0.99 * 0.99)
RATE_FACTORS = (0.03, 0.01, 0.01, 0.28, 0.029, 0.01)
HALF_ROOT = 0.7071067811865476
MASKED = -1e30
SCALE = HV**-0.5
BF = jnp.bfloat16
F32 = jnp.float32


def cost(matmul_flops):
    return pl.CostEstimate(flops=int(0.4 * matmul_flops), bytes_accessed=1, transcendentals=0)


CHEAP = cost(0)
NT = (((1,), (1,)), ((), ()))
TN = (((0,), (0,)), ((), ()))


def mm(left, right):
    return jnp.dot(left, right, preferred_element_type=F32)


def mm_nt(left, right):
    return lax.dot_general(left, right, NT, preferred_element_type=F32)


def mm_tn(left, right):
    return lax.dot_general(left, right, TN, preferred_element_type=F32)


def peer(values, axis, offset):
    ways = lax.axis_size(axis)
    return lax.ppermute(values, axis, [(i, i ^ offset) for i in range(ways)])


def shift(values, step, first):
    ways = lax.axis_size("t")
    places = range(first, ways - 1) if step > 0 else range(1, ways - first)
    return lax.ppermute(values, "t", [(i, i + step) for i in places])


SWAP = [(2 * a + b, 2 * b + a) for a in range(2) for b in range(2)]
TURN = [(2 * a + b, 2 * (1 - b) + a) for a in range(2) for b in range(2)]
BACK = [(2 * (1 - b) + a, 2 * a + b) for a in range(2) for b in range(2)]


def told(flag, *earlier):
    flag = flag.astype(jnp.int32).reshape(1, 1)
    return (hold(flag, *earlier) if earlier else flag)[0, 0] == 1


def enter(values, *earlier):
    half = values.shape[0] // 2
    near = told(lax.axis_index("s") == 0, *earlier)
    first = jnp.where(near, values[:half], values[half:]).astype(BF)
    second = jnp.where(near, values[half:], values[:half]).astype(BF)
    same = lax.ppermute(first, ("c", "s"), SWAP)
    other = lax.ppermute(second, ("c", "s"), TURN)
    low = lax.axis_index("c") == 0
    return jnp.concatenate([jnp.where(low, same, other), jnp.where(low, other, same)], axis=1)


def leave(values):
    width = values.shape[1] // 2
    low = lax.axis_index("c") == 0
    same = jnp.where(low, values[:, :width], values[:, width:])
    other = jnp.where(low, values[:, width:], values[:, :width])
    same = lax.ppermute(same, ("c", "s"), SWAP)
    other = lax.ppermute(other, ("c", "s"), BACK)
    near = lax.axis_index("s") == 0
    return jnp.concatenate([jnp.where(near, same, other), jnp.where(near, other, same)], axis=0)


def line():
    return lax.axis_size("t") == 4


def send_t(piece):
    ways = lax.axis_size("t")
    if not line():
        return [piece] + [peer(piece, "t", offset) for offset in range(1, ways)]
    parts = [piece]
    up = down = piece
    for step in range(ways - 1):
        up, down = shift(up, 1, step), shift(down, -1, step)
        parts += [up, down]
    return parts


def where_from(mine, place):
    if not line():
        return mine ^ place
    return 0 if mine == place else 2 * abs(mine - place) - (1 if place < mine else 0)


def anywhere(count):
    return [pl.BlockSpec(memory_space=pl.ANY)] * count


def hold(values, *earlier):
    def body(*refs):
        pass

    return pl.pallas_call(
        body,
        out_shape=jax.ShapeDtypeStruct(values.shape, values.dtype),
        in_specs=anywhere(1 + len(earlier)),
        out_specs=pl.BlockSpec(memory_space=pl.ANY),
        input_output_aliases={0: 0},
        cost_estimate=CHEAP,
        name="hold",
    )(values, *earlier)


def join_body(ways, mine, *refs):
    parts, out = refs, refs[-1]
    width = parts[0].shape[1]
    for d in range(ways):

        @pl.when(mine[0] == d)
        def _():
            for place in range(ways):
                out[:, place * width : (place + 1) * width] = parts[where_from(d, place)][...]


def join_t(parts, *earlier):
    ways = lax.axis_size("t")
    tokens, width = parts[0].shape
    rows = min(256, tokens)
    return pl.pallas_call(
        functools.partial(join_body, ways),
        grid_spec=pltpu.PrefetchScalarGridSpec(
            num_scalar_prefetch=1,
            grid=(tokens // rows,),
            in_specs=[pl.BlockSpec((rows, width), lambda i, mine: (i, 0))] * len(parts)
            + anywhere(len(earlier)),
            out_specs=pl.BlockSpec((rows, ways * width), lambda i, mine: (i, 0)),
        ),
        out_shape=jax.ShapeDtypeStruct((tokens, ways * width), parts[0].dtype),
        cost_estimate=cost(5e9),
        name="join",
    )(lax.axis_index("t").astype(jnp.int32).reshape(1), *parts, *earlier)


def terms_body(count, pieces, dests, *refs):
    lefts, rights, outs = refs[:count], refs[count : 2 * count], refs[-pieces:]
    total = None
    for left, right in zip(lefts, rights):
        if len(right.shape) == 4:
            product = mm(left[...], right[0, 0])
        else:
            product = mm_nt(left[...], right[0])
        total = product if total is None else total + product
    for i in range(pieces):

        @pl.when(pl.program_id(0) == i)
        def _():
            outs[i][...] = total.astype(outs[i].dtype)


def terms_t(lefts, rights, dests, dtypes, *earlier):
    tokens = lefts[0].shape[0]
    count, pieces = len(lefts), len(dtypes)
    width = D // lax.axis_size("t")

    def right_spec(weight, s):
        if len(weight.shape) == 4:
            return pl.BlockSpec((1, 1) + weight.shape[2:], lambda i, dests: (s, dests[i], 0, 0))
        return pl.BlockSpec((1, width, weight.shape[2]), lambda i, dests: (s, dests[i], 0))

    return pl.pallas_call(
        functools.partial(terms_body, count, pieces),
        grid_spec=pltpu.PrefetchScalarGridSpec(
            num_scalar_prefetch=1,
            grid=(pieces,),
            in_specs=[pl.BlockSpec(a.shape, lambda i, dests: (0, 0)) for a in lefts]
            + [right_spec(*right) for right in rights]
            + anywhere(len(earlier)),
            out_specs=[pl.BlockSpec((tokens, width), lambda i, dests: (0, 0))] * pieces,
        ),
        out_shape=[jax.ShapeDtypeStruct((tokens, width), dtype) for dtype in dtypes],
        compiler_params=pltpu.CompilerParams(vmem_limit_bytes=48 * 2**20),
        cost_estimate=cost(2 * pieces * tokens * width * sum(a.shape[1] for a in lefts)),
        name="terms",
    )(dests, *lefts, *[weight for weight, s in rights], *earlier)


def hop(values, step, count):
    places = range(count) if step > 0 else range(3, 3 - count, -1)
    return lax.ppermute(values, "t", [(i, i + step) for i in places])


def both_s(weight):
    return [(weight, 0), (weight, 1)]


def spread_t(lefts, rights, *earlier):
    ways, mine = lax.axis_size("t"), lax.axis_index("t")
    if not line():
        dests = jnp.stack([mine ^ offset for offset in range(ways)]).astype(jnp.int32)
        parts = terms_t(lefts, rights, dests, [F32] + [BF] * (ways - 1), *earlier)
        return [parts[0]] + [peer(part, "t", offset) for offset, part in enumerate(parts) if offset], parts
    order = jnp.asarray(np.array([[3, 2, 1, 0], [3, 2, 0, 1], [0, 1, 3, 2], [0, 1, 2, 3]], np.int32))
    dests = lax.dynamic_index_in_dim(order, mine, 0, False)
    [first] = terms_t(lefts, rights, dests[:1], [BF], *earlier)
    up, down = hop(first, 1, 1), hop(first, -1, 1)
    second, third, own = terms_t(lefts, rights, dests[1:], [BF, BF, F32], first)
    wide = lambda a: a.astype(F32)
    up2 = (jnp.where(mine == 0, wide(second), wide(first)) + wide(up)).astype(BF)
    down2 = (jnp.where(mine == 3, wide(second), wide(first)) + wide(down)).astype(BF)
    up, down = hop(up2, 1, 2), hop(down2, -1, 2)
    up3 = (jnp.where(mine == 1, wide(second), wide(third)) + wide(up)).astype(BF)
    down3 = (jnp.where(mine == 2, wide(second), wide(third)) + wide(down)).astype(BF)
    return [own, hop(up3, 1, 3), hop(down3, -1, 3)], [up2, down2, up3, down3]


def add_up(parts):
    total = parts[0].astype(F32)
    for part in parts[1:]:
        total = total + part.astype(F32)
    return total


def total_t(values):
    total = values
    for offset in range(1, lax.axis_size("t")):
        total = total + peer(values, "t", offset)
    return total


def gather_weight(shard, *earlier):
    flag = told(lax.axis_index("s") >= 0, *earlier)
    shard = jnp.where(flag, shard, 0.0).astype(BF)
    full = lax.all_gather(shard, ("s", "y", "c"), axis=0, tiled=False)
    return full.reshape((2, -1) + shard.shape)


def rows_of(full):
    return full.reshape(2, -1, full.shape[3])


def pack(pair):
    cut = pair.shape[2] // HV * HV
    return jnp.concatenate([pair[:, 0, :cut], pair[:, 1, :cut], pair[:, 0, cut:], pair[:, 1, cut:]], axis=1)


def unpack(packed):
    columns = packed.shape[1] // 2
    cut = columns // HV * HV
    left = 2 * cut
    more = columns - cut
    gate = jnp.concatenate([packed[:, :cut], packed[:, left : left + more]], axis=1)
    return gate, jnp.concatenate([packed[:, cut:left], packed[:, left + more :]], axis=1)


def grads_body(count, *refs):
    turned, out = refs[0][...].T, refs[-1]
    for i in range(count):
        out[i] = mm(turned, refs[1 + i][...]).astype(BF)


def grads(left, rights, *earlier):
    tokens, width = left.shape[0], min(256, left.shape[1])
    count, columns = len(rights), rights[0].shape[1]
    return pl.pallas_call(
        functools.partial(grads_body, count),
        grid=(left.shape[1] // width,),
        in_specs=[pl.BlockSpec((tokens, width), lambda i: (0, i))]
        + [pl.BlockSpec(right.shape, lambda i: (0, 0)) for right in rights]
        + anywhere(len(earlier)),
        out_specs=pl.BlockSpec((count, width, columns), lambda i: (0, i, 0)),
        out_shape=jax.ShapeDtypeStruct((count, left.shape[1], columns), BF),
        compiler_params=pltpu.CompilerParams(vmem_limit_bytes=40 * 2**20),
        cost_estimate=cost(2 * count * tokens * left.shape[1] * columns),
        name="grads",
    )(left, *rights, *earlier)


def down_grads_body(count, *refs):
    block, out = refs[0][...], refs[-1]
    for i in range(count):
        out[i, 0] = mm_tn(refs[1 + i][...], block).astype(BF)


def down_grads(upstream, hidden, *earlier):
    ways = lax.axis_size("t")
    tokens, width = upstream.shape[0], upstream.shape[1] // ways
    count, columns = len(hidden), hidden[0].shape[1]
    return pl.pallas_call(
        functools.partial(down_grads_body, count),
        grid=(ways,),
        in_specs=[pl.BlockSpec((tokens, width), lambda i: (0, i))]
        + [pl.BlockSpec(left.shape, lambda i: (0, 0)) for left in hidden]
        + anywhere(len(earlier)),
        out_specs=pl.BlockSpec((count, 1, columns, width), lambda i: (0, i, 0, 0)),
        out_shape=jax.ShapeDtypeStruct((count, ways, columns, width), BF),
        compiler_params=pltpu.CompilerParams(vmem_limit_bytes=40 * 2**20),
        cost_estimate=cost(2 * count * tokens * upstream.shape[1] * columns),
        name="down_grads",
    )(upstream, *hidden, *earlier)


def scatter_grad(stacked):
    flat = stacked.reshape((-1,) + stacked.shape[2:])
    return lax.psum_scatter(flat, ("s", "y", "c"), scatter_dimension=0, tiled=True)


def back_body(upstream, weight, out):
    width = weight.shape[3]
    total = mm_nt(upstream[:, :width], weight[0, 0])
    for i in range(1, weight.shape[1]):
        total = total + mm_nt(upstream[:, i * width : (i + 1) * width], weight[0, i])
    out[...] = total.astype(BF)


def back_hidden(upstream, weight, s):
    tokens = upstream.shape[0]
    rows = min(256, tokens)
    return pl.pallas_call(
        back_body,
        grid=(tokens // rows,),
        in_specs=[
            pl.BlockSpec((rows, upstream.shape[1]), lambda i: (i, 0)),
            pl.BlockSpec((1,) + weight.shape[1:], lambda i: (s, 0, 0, 0)),
        ],
        out_specs=pl.BlockSpec((rows, weight.shape[2]), lambda i: (i, 0)),
        out_shape=jax.ShapeDtypeStruct((tokens, weight.shape[2]), BF),
        compiler_params=pltpu.CompilerParams(vmem_limit_bytes=40 * 2**20),
        cost_estimate=cost(2 * tokens * upstream.shape[1] * weight.shape[2]),
        name="back_hidden",
    )(upstream, weight)


def project_body(count, left, factor, *refs):
    for right, out in zip(refs[:count], refs[-count:]):
        out[...] = (mm(left[...], right[0]) * factor[...]).astype(BF)


def project(left, weights, factor):
    tokens = left.shape[0]
    rows = min(256, tokens)
    by_rows = lambda n: pl.BlockSpec((rows, n), lambda i: (i, 0))
    return pl.pallas_call(
        functools.partial(project_body, len(weights)),
        grid=(tokens // rows,),
        in_specs=[by_rows(left.shape[1]), by_rows(1)]
        + [pl.BlockSpec((1,) + w.shape[1:], lambda i, s=s: (s, 0, 0)) for w, s in weights],
        out_specs=[by_rows(w.shape[2]) for w, s in weights],
        out_shape=[jax.ShapeDtypeStruct((tokens, w.shape[2]), BF) for w, s in weights],
        compiler_params=pltpu.CompilerParams(vmem_limit_bytes=40 * 2**20),
        cost_estimate=cost(2 * tokens * left.shape[1] * sum(w.shape[2] for w, s in weights)),
        name="project",
    )(left, factor, *[w for w, s in weights])


def feed_body(scaled, factor, back, weight, hidden, dboth):
    scale = factor[...]
    gate, up = unpack(mm(scaled[...], weight[0]) * scale)
    upstream = back[...].astype(F32)
    sigmoid = 1.0 / (1.0 + jnp.exp(-gate))
    active = gate * sigmoid
    hidden[...] = (active * up).astype(BF)
    slope = upstream * up * sigmoid * (1.0 + gate * (1.0 - sigmoid))
    dgate, dup = (slope * scale).astype(BF), (upstream * active * scale).astype(BF)
    cut = dgate.shape[1] // HV * HV
    dboth[:, :cut] = dgate[:, :cut]
    dboth[:, cut : 2 * cut] = dup[:, :cut]
    dboth[:, 2 * cut :] = jnp.concatenate([dgate[:, cut:], dup[:, cut:]], axis=1)


def feed_forward(scaled, factor, back, weight, s):
    tokens, columns = back.shape
    rows = min(256, tokens)
    by_rows = lambda n: pl.BlockSpec((rows, n), lambda i: (i, 0))
    return pl.pallas_call(
        feed_body,
        grid=(tokens // rows,),
        in_specs=[
            by_rows(scaled.shape[1]),
            by_rows(1),
            by_rows(columns),
            pl.BlockSpec((1,) + weight.shape[1:], lambda i: (s, 0, 0)),
        ],
        out_specs=[by_rows(columns), by_rows(2 * columns)],
        out_shape=[jax.ShapeDtypeStruct((tokens, n), BF) for n in (columns, 2 * columns)],
        compiler_params=pltpu.CompilerParams(vmem_limit_bytes=40 * 2**20),
        cost_estimate=cost(4 * tokens * scaled.shape[1] * columns),
        name="feed_forward",
    )(scaled, factor, back, weight)


def forward_body(heads, tokens, wqk, rest, far_v, far_w, docs_c, docs_r, out, den):
    lanes = heads * HV
    for i in range(heads):
        at = i * HV
        qs, ks = 2 * lanes + i * FEAT, 2 * lanes + (heads + i) * FEAT
        fs = lanes + (heads + i) * FEAT
        for b in range(tokens // QB):
            rows = slice(b * QB, (b + 1) * QB)
            q = rest[rows, qs : qs + FEAT]
            docs_q = docs_c[REACH + b * QB : REACH + (b + 1) * QB, :]
            numer = jnp.zeros((QB, HV), F32)
            denom = jnp.zeros((QB, 1), F32)
            for kb in range(b - REACH // QB, b + 1):
                if kb >= 0:
                    keys = slice(kb * QB, (kb + 1) * QB)
                    k = rest[keys, ks : ks + FEAT]
                    v = rest[keys, lanes + at : lanes + at + HV]
                else:
                    keys = slice(REACH + kb * QB, REACH + (kb + 1) * QB)
                    k = far_v[keys, fs : fs + FEAT]
                    v = far_v[keys, at : at + HV]
                inner = mm_nt(q, k) * 0.25
                kernel = 1.0 + inner + 0.5 * inner * inner
                allowed = docs_q == docs_r[:, REACH + kb * QB : REACH + (kb + 1) * QB]
                if kb == b:
                    allowed = allowed & (
                        lax.broadcasted_iota(jnp.int32, (QB, QB), 0)
                        >= lax.broadcasted_iota(jnp.int32, (QB, QB), 1)
                    )
                kernel = jnp.where(allowed, kernel, 0.0)
                denom = denom + jnp.sum(kernel, axis=1, keepdims=True)
                numer = numer + mm(kernel.astype(BF), v)
            out[rows, at : at + HV] = (numer / denom).astype(BF)
            den[rows, i : i + 1] = denom
        for b in range(tokens // WB):
            rows = slice(b * WB, (b + 1) * WB)
            q = wqk[rows, at : at + HV]
            k, v, allowed = window_block(b, at, lanes, wqk, rest, far_w, docs_c, docs_r)
            probs = window_probs(q, k, allowed)
            out[rows, lanes + at : lanes + at + HV] = mm(probs.astype(BF), v).astype(BF)


def window_block(b, at, lanes, wqk, rest, far_w, docs_c, docs_r):
    if b:
        keys = slice((b - 1) * WB, (b + 1) * WB)
        k = wqk[keys, lanes + at : lanes + at + HV]
        v = rest[keys, at : at + HV]
    else:
        k = jnp.concatenate(
            [far_w[:, at : at + HV], wqk[:WB, lanes + at : lanes + at + HV]], axis=0
        )
        v = jnp.concatenate(
            [
                far_w[:, lanes + at : lanes + at + HV],
                rest[:WB, at : at + HV],
            ],
            axis=0,
        )
    start = REACH + b * WB
    back = (
        lax.broadcasted_iota(jnp.int32, (WB, 2 * WB), 0)
        + WB
        - lax.broadcasted_iota(jnp.int32, (WB, 2 * WB), 1)
    )
    same = docs_c[start : start + WB, :] == docs_r[:, start - WB : start + WB]
    return k, v, same & (back >= 0) & (back < WIN)


def window_probs(q, k, allowed):
    scores = jnp.where(allowed, mm_nt(q, k) * SCALE, MASKED)
    exponent = jnp.exp(scores - jnp.max(scores, axis=1, keepdims=True))
    return exponent / jnp.sum(exponent, axis=1, keepdims=True)


def backward_body(
    heads, tokens, wqk, rest, far_v, far_w, docs_c, docs_r, out, den, dout,
    *rest_refs,
):
    dwqk, drest, dfar_v, dfar_w, acc_v, acc_k, acc_wk, acc_wv = rest_refs[-8:]
    lanes = heads * HV
    lane_zero = (lax.broadcasted_iota(jnp.int32, (QB, HV), 1) == 0).astype(BF)
    dfar_v[:, lanes:] = jnp.zeros((REACH, dfar_v.shape[1] - lanes), BF)
    drest[:, 2 * lanes :] = jnp.zeros((tokens, drest.shape[1] - 2 * lanes), BF)
    for i in range(heads):
        at = i * HV
        qs, ks = 2 * lanes + i * FEAT, 2 * lanes + (heads + i) * FEAT
        fs = lanes + (heads + i) * FEAT
        acc_v[...] = jnp.zeros_like(acc_v)
        acc_k[...] = jnp.zeros_like(acc_k)
        acc_wk[...] = jnp.zeros_like(acc_wk)
        acc_wv[...] = jnp.zeros_like(acc_wv)
        for b in range(tokens // QB):
            rows = slice(b * QB, (b + 1) * QB)
            q = rest[rows, qs : qs + FEAT]
            docs_q = docs_r[:, REACH + b * QB : REACH + (b + 1) * QB]
            dlin = dout[rows, at : at + HV].astype(F32)
            inverse = 1.0 / den[rows, i : i + 1]
            mean = jnp.sum(dlin * out[rows, at : at + HV].astype(F32), axis=1, keepdims=True)
            dnumer = (dlin * inverse).astype(BF)
            ddenom = (-mean * inverse).astype(BF)
            extended = jnp.concatenate([dnumer, ddenom * lane_zero], axis=1)
            dq = jnp.zeros((QB, FEAT), F32)
            for kb in range(b - REACH // QB, b + 1):
                place = slice(REACH + kb * QB, REACH + (kb + 1) * QB)
                if kb >= 0:
                    keys = slice(kb * QB, (kb + 1) * QB)
                    k = rest[keys, ks : ks + FEAT]
                    v = rest[keys, lanes + at : lanes + at + HV]
                else:
                    k = far_v[place, fs : fs + FEAT]
                    v = far_v[place, at : at + HV]
                inner = mm_nt(k, q) * 0.25
                weight = mm_nt(jnp.concatenate([v, lane_zero], axis=1), extended)
                allowed = docs_c[place, :] == docs_q
                if kb == b:
                    allowed = allowed & (
                        lax.broadcasted_iota(jnp.int32, (QB, QB), 0)
                        <= lax.broadcasted_iota(jnp.int32, (QB, QB), 1)
                    )
                kernel = jnp.where(allowed, 1.0 + inner + 0.5 * inner * inner, 0.0).astype(BF)
                slope = jnp.where(allowed, weight * (0.25 + 0.25 * inner), 0.0).astype(BF)
                acc_v[place, :] += mm(kernel, dnumer)
                acc_k[place, :] += mm(slope, q)
                dq = dq + mm_tn(slope, k)
            drest[rows, qs : qs + FEAT] = dq.astype(BF)
        dfar_v[:, at : at + HV] = acc_v[:REACH, :].astype(BF)
        dfar_v[:, fs : fs + FEAT] = acc_k[:REACH, :].astype(BF)
        drest[:, lanes + at : lanes + at + HV] = acc_v[REACH:, :].astype(BF)
        drest[:, ks : ks + FEAT] = acc_k[REACH:, :].astype(BF)
        for b in range(tokens // WB):
            rows = slice(b * WB, (b + 1) * WB)
            q = wqk[rows, at : at + HV]
            k, v, allowed = window_block(b, at, lanes, wqk, rest, far_w, docs_c, docs_r)
            probs = window_probs(q, k, allowed)
            upstream = dout[rows, lanes + at : lanes + at + HV]
            dprobs = mm_nt(upstream, v)
            dscores = probs * (dprobs - jnp.sum(probs * dprobs, axis=1, keepdims=True))
            dscores = dscores.astype(BF)
            dwqk[rows, at : at + HV] = (mm(dscores, k) * SCALE).astype(BF)
            span = slice(b * WB, (b + 2) * WB)
            acc_wk[span, :] += mm_tn(dscores, q)
            acc_wv[span, :] += mm_tn(probs.astype(BF), upstream)
        dfar_w[:, at : at + HV] = (acc_wk[:WB, :] * SCALE).astype(BF)
        dfar_w[:, lanes + at : lanes + at + HV] = acc_wv[:WB, :].astype(BF)
        dwqk[:, lanes + at : lanes + at + HV] = (acc_wk[WB:, :] * SCALE).astype(BF)
        drest[:, at : at + HV] = acc_wv[WB:, :].astype(BF)


VMEM = pltpu.CompilerParams(vmem_limit_bytes=28 * 2**20)


def attention_forward(heads, wqk, rest, far_v, far_w, docs_c, docs_r):
    tokens = wqk.shape[0]
    outs = (
        jax.ShapeDtypeStruct((tokens, 2 * heads * HV), BF),
        jax.ShapeDtypeStruct((tokens, heads), F32),
    )
    return pl.pallas_call(
        functools.partial(forward_body, heads, tokens),
        out_shape=outs,
        compiler_params=VMEM,
        cost_estimate=cost(6e9),
        name="attention_forward",
    )(wqk, rest, far_v, far_w, docs_c, docs_r)


def attention_backward(heads, wqk, rest, far_v, far_w, docs_c, docs_r, out, den, dout, *earlier):
    tokens = wqk.shape[0]
    ins = (wqk, rest, far_v, far_w, docs_c, docs_r, out, den, dout)
    return pl.pallas_call(
        functools.partial(backward_body, heads, tokens),
        in_specs=[pl.BlockSpec(memory_space=pltpu.VMEM)] * len(ins) + anywhere(len(earlier)),
        out_shape=tuple(jax.ShapeDtypeStruct(a.shape, BF) for a in (wqk, rest, far_v, far_w)),
        scratch_shapes=[
            pltpu.VMEM((REACH + tokens, HV), F32),
            pltpu.VMEM((REACH + tokens, FEAT), F32),
            pltpu.VMEM((WB + tokens, HV), F32),
            pltpu.VMEM((WB + tokens, HV), F32),
        ],
        compiler_params=VMEM,
        cost_estimate=cost(17e9),
        name="attention_backward",
    )(*ins, *earlier)


def feature_tables():
    pick_a = np.zeros((F1, F1 * F1), np.float32)
    pick_b = np.zeros((F1, F1 * F1), np.float32)
    scale = np.ones((F1 * F1,), np.float32)
    for r in range(F1):
        for j in range(F1):
            f = r * F1 + j
            pick_a[r, f] = 1.0
            if r < FEAT:
                scale[f] = HALF_ROOT
                if j < FEAT:
                    pick_b[j, f] = 1.0
            else:
                pick_b[FEAT if j == 0 else j - 1, f] = 1.0
    return pick_a, pick_b, scale


def row_states(heads, keys, values, docs):
    keys, values = keys[:, -REACH:], values[:, -REACH:]
    keys = jnp.swapaxes(keys.reshape(2, REACH, heads, FEAT), 1, 2).reshape(-1, REACH, FEAT)
    values = jnp.swapaxes(values.reshape(2, REACH, heads, HV), 1, 2).reshape(-1, REACH, HV)
    ones = jnp.ones(keys.shape[:2] + (1,), BF)
    extended = jnp.concatenate([keys * BF(0.5), ones], axis=2)
    pick_a, pick_b, scale = feature_tables()
    left = jnp.einsum("bsf,fg->bsg", extended, jnp.asarray(pick_a, BF), preferred_element_type=F32)
    right = jnp.einsum("bsf,fg->bsg", extended, jnp.asarray(pick_b, BF), preferred_element_type=F32)
    in_last = (docs[-REACH:] == docs[-1]).astype(F32)
    features = left * right * scale * in_last[None, :, None]
    return jnp.einsum("bsg,bsv->bgv", features.astype(BF), values, preferred_element_type=F32)


def owned_states(heads, states, owner):
    ways = lax.axis_size("t")
    mine_t, side = lax.axis_index("t"), lax.axis_index("s")
    states = lax.all_gather(states.astype(BF), ("c", "s", "t"), axis=0, tiled=False)
    states = lax.dynamic_slice_in_dim(states, (2 + lax.axis_index("c")) * ways, ways, 0)
    states = states.reshape(GROUPS, F1, HV)
    slots = GROUPS // ways
    groups = jnp.arange(GROUPS, dtype=jnp.int32)
    mine = owner == 2 * mine_t + side
    ordinal = jnp.sum((mine[None, :] & (groups[None, :] < groups[:, None])).astype(jnp.int32), axis=1)
    wanted = jnp.arange(slots, dtype=jnp.int32)
    picked = (mine[None, :] & (ordinal[None, :] == wanted[:, None])).astype(BF)
    return jnp.einsum("kg,gfv->kfv", picked, states, preferred_element_type=F32)[None]


def momentum_update(weights, moment, average, gradient, factor, token_total):
    step_rate = factor / math.sqrt(token_total)
    moment_new = MOMENTUM * moment + gradient
    weights_new = weights - step_rate * (gradient + MOMENTUM * moment_new)
    average_new = AVERAGE_OLD * average + AVERAGE_NEW * weights_new
    return (gradient, weights_new, moment_new, average_new, weights_new.astype(BF))


def norm_back(values, factor, gains, upstream):
    gain_grad = jnp.sum(upstream * values, axis=0)
    inner = total_t(jnp.sum(upstream * gains * values, axis=1))
    scale = factor * factor * inner[:, None] / D
    return gains * upstream - values * scale, gain_grad


def local(
    layer_in, out_grad, doc_ids, group_owner,
    norm_gains, norm_gains_moment, norm_gains_average,
    feature_proj, feature_proj_moment, feature_proj_average,
    head_proj, head_proj_moment, head_proj_average,
    mixer_out, mixer_out_moment, mixer_out_average,
    gate_up, gate_up_moment, gate_up_average,
    down_proj, down_proj_moment, down_proj_average,
):
    data_ways = lax.axis_size("y") * 2
    core, side = lax.axis_index("c"), lax.axis_index("s")
    width = layer_in.shape[1]
    tokens = layer_in.shape[0] // 2
    heads = head_proj.shape[2] // HV
    rows = head_proj.shape[0]
    lanes = heads * HV
    token_total = layer_in.shape[0] * data_ways

    x_low = enter(layer_in)
    x = x_low.astype(F32)
    other_gains = lax.ppermute(norm_gains, "s", [(0, 1), (1, 0)])
    gains = jnp.where(
        side == 0,
        jnp.concatenate([norm_gains, other_gains], axis=1),
        jnp.concatenate([other_gains, norm_gains], axis=1),
    )
    docs = lax.ppermute(doc_ids, ("c", "s"), SWAP)
    docs = jnp.concatenate([jnp.full((1, REACH), -1, jnp.int32), docs], axis=1)
    docs_r = lax.dynamic_slice_in_dim(docs, core * tokens, REACH + tokens, 1)
    docs_c = jnp.reshape(docs_r, (REACH + tokens, 1))

    scaled_mine = (x * gains[0]).astype(BF)
    wqk_shard = head_proj[:, :2].reshape(rows, -1)
    extra = -(2 * heads * FEAT) % HV
    rest_shard = jnp.concatenate(
        [head_proj[:, 2:].reshape(rows, -1), feature_proj.reshape(rows, -1), jnp.zeros((rows, extra), F32)], axis=1
    )
    parts = send_t(scaled_mine)
    wqk_full = rows_of(gather_weight(wqk_shard, x_low))
    rest_full = rows_of(gather_weight(rest_shard, x_low))
    begun = parts[3:5]
    mixer_full = rows_of(gather_weight(jnp.transpose(mixer_out, (2, 0, 1)).reshape(rows, -1), *begun))
    both_full = rows_of(gather_weight(pack(gate_up), *begun))
    down_full = gather_weight(down_proj, *begun)
    factor_one = lax.rsqrt(total_t(jnp.sum(x * x, axis=1)) / D + EPSILON)[:, None]
    scaled_one = join_t(parts)
    dy_mine = enter(out_grad, *begun)
    dy = lax.all_gather(dy_mine, "t", axis=1, tiled=True)
    wqk, rest = [], []
    for s in range(2):
        one, two = project(scaled_one, [(wqk_full, s), (rest_full, s)], factor_one)
        wqk.append(one)
        rest.append(two)

    ahead, behind = [(0, 1)], [(1, 0)]
    far_v = [lax.ppermute(p[-REACH:, lanes:], "c", ahead) for p in rest]
    far_w = [
        lax.ppermute(jnp.concatenate([a[-WB:, lanes:], b[-WB:, :lanes]], axis=1), "c", ahead)
        for a, b in zip(wqk, rest)
    ]
    attended, denom = [], []
    for s in range(2):
        one, two = attention_forward(heads, wqk[s], rest[s], far_v[s], far_w[s], docs_c, docs_r)
        attended.append(one)
        denom.append(two)

    mixed = add_up(spread_t(attended, both_s(mixer_full))[0])
    middle = x + mixed
    factor_two = lax.rsqrt(total_t(jnp.sum(middle * middle, axis=1)) / D + EPSILON)[:, None]
    scaled_mine = (middle * gains[1]).astype(BF)
    parts = send_t(scaled_mine)
    dhidden = [back_hidden(dy, down_full, s) for s in range(2)]
    last = jnp.stack([p[-REACH:, lanes:] for p in rest])
    states = row_states(heads, last[:, :, lanes + heads * FEAT : lanes + 2 * heads * FEAT], last[:, :, :lanes], docs_r[0])
    row_state = owned_states(heads, states, group_owner)
    scaled_two = join_t(parts, *dhidden)

    hidden, dboth = [], []
    for s in range(2):
        one, two = feed_forward(scaled_two, factor_two, dhidden[s], both_full, s)
        hidden.append(one)
        dboth.append(two)
    parts, second = spread_t(dboth, both_s(both_full), row_state)
    for_down = down_grads(dy, hidden, *second[:2])
    upstream_two = add_up([hold(parts[0], for_down)] + parts[1:])
    back_two, gain_two = norm_back(middle, factor_two, gains[1], upstream_two)
    dmixed_mine = (dy_mine.astype(F32) + back_two).astype(BF)
    parts = send_t(dmixed_mine)
    for_both = grads(scaled_two, dboth, *parts[1:3])
    branch_parts, second = spread_t(hidden, both_s(down_full), for_both, *parts[3:5])
    dmixed = join_t(parts, for_both)
    down_sum, both_sum = scatter_grad(for_down), scatter_grad(for_both)

    branch = add_up(branch_parts)
    out_y = layer_in + leave((mixed + branch).astype(BF)).astype(F32)
    dattended = project(dmixed, both_s(mixer_full), jnp.ones((tokens, 1), F32))
    mixer_sum = scatter_grad(hold(grads(dmixed, attended, *dattended), both_sum))
    dwqk, drest = [], []
    for s in range(2):
        one, two, three, four = attention_backward(
            heads, wqk[s], rest[s], far_v[s], far_w[s], docs_c, docs_r, attended[s], denom[s], dattended[s], *second[2 * s : 2 * s + 2]
        )
        far_three = lax.ppermute(three, "c", behind).astype(F32)
        far_four = lax.ppermute(four, "c", behind).astype(F32)
        one = one.astype(F32) + jnp.pad(far_four[:, :lanes], ((tokens - WB, 0), (lanes, 0)))
        two = (
            two.astype(F32)
            + jnp.pad(far_three, ((tokens - REACH, 0), (lanes, 0)))
            + jnp.pad(far_four[:, lanes:], ((tokens - WB, 0), (0, rest[s].shape[1] - lanes)))
        )
        dwqk.append((one * factor_one).astype(BF))
        drest.append((two * factor_one).astype(BF))
    parts, second = spread_t(dwqk + drest, both_s(wqk_full) + both_s(rest_full), down_sum, both_sum, branch)
    rest_sum = scatter_grad(grads(scaled_one, drest, *second[:2]))
    wqk_sum = scatter_grad(grads(scaled_one, dwqk, *second[:2]))
    upstream_one = add_up([hold(parts[0], mixer_sum)] + parts[1:])
    back_one, gain_one = norm_back(x, factor_one, gains[0], upstream_one)
    grad_x = out_grad + leave((back_one + back_two).astype(BF)).astype(F32)
    wqk_sum, rest_sum, mixer_sum, both_sum = [a.astype(F32) for a in (wqk_sum, rest_sum, mixer_sum, both_sum)]
    down_sum = down_sum[0].astype(F32)
    head_sum = jnp.concatenate([wqk_sum, rest_sum[:, : 2 * lanes]], axis=1)
    feature_sum = rest_sum[:, 2 * lanes : 2 * lanes + 2 * heads * FEAT]

    both = jnp.stack([gain_one, gain_two], axis=0)
    both = both + peer(both, "c", 1)
    step = 1
    while step < data_ways // 2:
        both = both + peer(both, "y", step)
        step *= 2
    low, high = both[:, :width], both[:, width:]
    gains_sum = jnp.where(side == 0, low, high) + peer(jnp.where(side == 0, high, low), "s", 1)

    mixer_sum = jnp.transpose(mixer_sum.reshape(rows, 2, lanes), (1, 2, 0))
    triples = (
        (norm_gains, norm_gains_moment, norm_gains_average, gains_sum),
        (feature_proj, feature_proj_moment, feature_proj_average, feature_sum.reshape(feature_proj.shape)),
        (head_proj, head_proj_moment, head_proj_average, head_sum.reshape(head_proj.shape)),
        (mixer_out, mixer_out_moment, mixer_out_average, mixer_sum),
        (gate_up, gate_up_moment, gate_up_average, jnp.stack(unpack(both_sum), axis=1)),
        (down_proj, down_proj_moment, down_proj_average, down_sum),
    )
    results = [out_y, grad_x, row_state]
    for index, triple in enumerate(triples):
        results.extend(momentum_update(*triple, RATE_FACTORS[index], token_total))
    return tuple(results)


def solution(mesh):
    data_ways, model_ways = mesh.shape["dp"], mesh.shape["mp"]
    grid = Mesh(mesh.devices.reshape(data_ways // 2, 2, model_ways // 2, 2), ("y", "c", "t", "s"))
    dp, mp = ("y", "c"), ("t", "s")
    gains = (P(None, mp),)
    rows_cols = (P(dp, None, mp),)
    mixer = (P(None, mp, dp),)
    down = (P(mp, dp),)
    tokens = (P(dp, mp),)
    return jax.shard_map(
        local,
        mesh=grid,
        in_specs=tokens * 2
        + (P(dp, None), P())
        + gains * 3
        + rows_cols * 6
        + mixer * 3
        + rows_cols * 3
        + down * 3,
        out_specs=tokens * 2
        + (P(dp, mp, None, None),)
        + gains * 5
        + rows_cols * 10
        + mixer * 5
        + rows_cols * 5
        + down * 5,
        check_vma=False,
    )
```

time: 1200 us -> 969 us (0.81)
  waiting for transfers between devices: 545 us -> 336 us
  matrix products: 207 us -> 7.27 us
  Pallas kernels: 50.5 us -> 226 us
  blocking collectives: 94 us -> 0 us
  starting transfers between devices: 104 us -> 174 us
  local copies, waits for them, and re-layouts: 90.2 us -> 112 us
    ppermute x39 -> x15, waiting for transfers between devices: 356 us -> 30.9 us  [peer(): return lax.ppermute(values, axis, [(i, i ^ offset) for i in range(ways)])]
    ppermute x24 -> x59, waiting for transfers between devices: 12.8 us -> 283 us  [the longest x18 132 us: shift(): return lax.ppermute(values, 't', [(i, i + step) for i in places])]
    dot_general x40 -> x1, matrix products: 202 us -> 1.98 us  [owned_states(): jnp.einsum('kg,gfv->kfv', picked, states, preferred_element_type=F32)[None]]
    pallas_call x2 -> x33, Pallas kernels: 50.5 us -> 226 us  [the longest x8 65.2 us: terms_t(): pl.pallas_call(functools.partial(terms_body, count, pieces), grid_spec=pl...]
    reduce_scatter x6 -> x5, waiting for transfers between devices: 177 us -> 17.2 us  [scatter_grad(): lax.psum_scatter(flat, ('s', 'y', 'c'), scatter_dimension=0, tiled=True)]
    ppermute x24 -> x59, starting transfers between devices: 50.3 us -> 152 us  [the longest x24 84 us: hop(): return lax.ppermute(values, 't', [(i, i + step) for i in places])]
    all_gather x1 -> x0, blocking collectives: 94 us -> none  [gather_weight(): lax.all_gather(shard.astype(BF), ('s', 'y', 'c'), axis=0, tiled=False)]
    unnamed x250 -> x317, local copies, waits for them, and re-layouts: 16.4 us -> 80.7 us
  transfers between devices with their start and end apart: 75 -> 87, of which waited for: 28 -> 31; matrix products, arithmetic and copies ran while one was open for 23% -> 13% of each run, Pallas kernels for 1% -> 19%
where the time goes in v2:
time: 969 us; the launch traced here: 957 us
  waiting for transfers between devices  336 us (35%)
  Pallas kernels  226 us (23%)
  starting transfers between devices  174 us (18%)
  local copies, waits for them, and re-layouts  112 us (12%)
  other arithmetic  82.9 us (9%)
  between operations  18.7 us (2%)
    ppermute x18, waiting for transfers between devices, shift(): return lax.ppermute(values, 't', [(i, i + step) for i in places])  132 us
    ppermute x24, waiting for transfers between devices, hop(): return lax.ppermute(values, 't', [(i, i + step) for i in places])  119 us
    ppermute x24, starting transfers between devices, hop(): return lax.ppermute(values, 't', [(i, i + step) for i in places])  84 us
    unnamed x317, local copies, waits for them, and re-layouts  80.7 us
    pallas_call x8, Pallas kernels, terms_t(): pl.pallas_call(functools.partial(terms_body, count, pieces), grid_spec=pl...  65.2 us
    pallas_call x4, Pallas kernels, grads(): pl.pallas_call(functools.partial(grads_body, count), grid=(left.shape[1]...  39 us
    ppermute x18, starting transfers between devices, shift(): return lax.ppermute(values, 't', [(i, i + step) for i in places])  34.8 us
    pallas_call x2, Pallas kernels, attention_backward(): pl.pallas_call(functools.partial(backward_body, heads, tokens), in_specs=...  31.5 us
  transfers between devices with their start and end apart: 87, of which 31 were waited for; matrix products, arithmetic and copies ran while one was open for 13% of the time, Pallas kernels for 19%

profile of v2, /device:TPU:0, one launch (start us, length us, event | category | flops | bytes accessed | tf_op | source)
XLA Modules:
  0.0 957.3 jit_solution(1262133847629869286)
XLA Ops:
  16.9 11.1 %collective-permute-done.1 = bf16[1024,256]{1,0:T(8,128)(2,1)} collective-permute-done((bf16[1024,256]{1,0:T(8,128)(2,1)}, bf16[1024,256]{1,0:T(8,128)(2,1)}, u32[]{:S(2)}, u32[]{:S(2)}) %collective-permute-start.1) | collective-permute-done | bytes 524320 | tf_op jit(solution)/shard_map/ppermute | solution.py:83
  44.5 19.6 %collective-permute-done.3.refs_1_ = bf16[1024,512]{1,0:T(8,128)(2,1)S(1)} collective-permute-done((bf16[1024,512]{1,0:T(8,128)(2,1)S(1)}, bf16[1024,512]{1,0:T(8,128)(2,1)S(1)}, u32[]{:S(2)}, u32[]{:S(2)}) %collective-permute-start.3) | collective-permute-done | bytes 1048608 | tf_op jit(solution)/shard_map/ppermute | solution.py:64
  69.6 23.0 %collective-permute-done.6.refs_4_.refs_2_ = bf16[1024,512]{1,0:T(8,128)(2,1)S(1)} collective-permute-done((bf16[1024,512]{1,0:T(8,128)(2,1)S(1)}, bf16[1024,512]{1,0:T(8,128)(2,1)S(1)}, u32[]{:S(2)}, u32[]{:S(2)}) %collective-permute-start.6) | collective-permute-done | bytes 1048608 | tf_op jit(solution)/shard_map/ppermute | solution.py:64
  104.2 19.2 %collective-permute-done.30 = bf16[1024,256]{1,0:T(8,128)(2,1)S(1)} collective-permute-done((bf16[1024,256]{1,0:T(8,128)(2,1)S(1)}, bf16[1024,256]{1,0:T(8,128)(2,1)S(1)}, u32[]{:S(2)}, u32[]{:S(2)}) %collective-permute-start.30) | collective-permute-done | bytes 524320 | tf_op jit(solution)/shard_map/ppermute | solution.py:83
  140.3 14.7 %collective-permute-done.9 = f32[1024]{0:T(1024)S(1)} collective-permute-done((f32[1024]{0:T(1024)S(1)}, f32[1024]{0:T(1024)S(1)}, u32[]{:S(2)}, u32[]{:S(2)}) %collective-permute-start.9) | collective-permute-done | bytes 4128 | tf_op jit(solution)/shard_map/ppermute | solution.py:58
  174.2 8.3 project.4
  250.5 9.3 collective-permute-done.17
  268.2 17.9 %collective-permute-done.18 = bf16[1024,512]{1,0:T(8,128)(2,1)S(1)} collective-permute-done((bf16[1024,512]{1,0:T(8,128)(2,1)}, bf16[1024,512]{1,0:T(8,128)(2,1)S(1)}, u32[]{:S(2)}, u32[]{:S(2)}) %collective-permute-start.18) | collective-permute-done | bytes 1048608 | tf_op jit(solution)/shard_map/ppermute | solution.py:215
  289.8 8.8 collective-permute-start.19
  298.6 26.0 %collective-permute-done.22 = bf16[1024,512]{1,0:T(8,128)(2,1)S(1)} collective-permute-done((bf16[1024,512]{1,0:T(8,128)(2,1)S(1)}, bf16[1024,512]{1,0:T(8,128)(2,1)S(1)}, u32[]{:S(2)}, u32[]{:S(2)}) %collective-permute-start.22) | collective-permute-done | bytes 1048608 | tf_op jit(solution)/shard_map/ppermute | solution.py:215
  324.6 9.2 collective-permute-done.19
  336.4 10.0 %collective-permute-start.23 = (bf16[1024,512]{1,0:T(8,128)(2,1)S(1)}, bf16[1024,512]{1,0:T(8,128)(2,1)S(1)}, u32[]{:S(2)}, u32[]{:S(2)}) collective-permute-start(bf16[1024,512]{1,0:T(8,128)(2,1)S(1)} %multiply_convert_fusion.5.refs_0_), channel_id=1, source_target_pairs={{0,2},{2,4},{4,6},{1,3},{3,5},{5,7},{8,10},{10,12},{12,14},{9,11},... | collective-permute-start | bytes 3145736 | tf_op jit(solution)/shard_map/ppermute | solution.py:64
  347.7 19.7 %collective-permute-done.23.refs_1_ = bf16[1024,512]{1,0:T(8,128)(2,1)S(1)} collective-permute-done((bf16[1024,512]{1,0:T(8,128)(2,1)S(1)}, bf16[1024,512]{1,0:T(8,128)(2,1)S(1)}, u32[]{:S(2)}, u32[]{:S(2)}) %collective-permute-start.23) | collective-permute-done | bytes 1048608 | tf_op jit(solution)/shard_map/ppermute | solution.py:64
  372.0 23.6 %collective-permute-done.26.refs_4_ = bf16[1024,512]{1,0:T(8,128)(2,1)} collective-permute-done((bf16[1024,512]{1,0:T(8,128)(2,1)S(1)}, bf16[1024,512]{1,0:T(8,128)(2,1)}, u32[]{:S(2)}, u32[]{:S(2)}) %collective-permute-start.26) | collective-permute-done | bytes 1048608 | tf_op jit(solution)/shard_map/ppermute | solution.py:64
  433.3 10.8 %feed_forward.2 = (bf16[1024,704]{1,0:T(8,128)(2,1)S(1)}, bf16[1024,1408]{1,0:T(8,128)(2,1)S(1)}) custom-call(bf16[1024,2048]{1,0:T(8,128)(2,1)S(1)} %copy-done.6, f32[1024,1]{1,0:T(8,128)S(1)} %copy-done.38, bf16[1024,704]{1,0:T(8,128)(2,1)S(1)} %copy-done.24, bf16[2,2048,1408]{2,1,0:T(8,128)(2,1)} %bitcast.102), custom_call_target="tpu_custom_call" | custom-call | flops 2362232064 | bytes 1 | tf_op jit(solution)/shard_map/feed_forward/pallas_call | solution.py:400
  444.1 11.7 %feed_forward.3 = (bf16[1024,704]{1,0:T(8,128)(2,1)S(1)}, bf16[1024,1408]{1,0:T(8,128)(2,1)S(1)}) custom-call(bf16[1024,2048]{1,0:T(8,128)(2,1)S(1)} %copy-done.6, f32[1024,1]{1,0:T(8,128)S(1)} %copy-done.39, bf16[1024,704]{1,0:T(8,128)(2,1)S(1)} %copy-done.26, bf16[2,2048,1408]{2,1,0:T(8,128)(2,1)} %bitcast.103), custom_call_target="tpu_custom_call" | custom-call | flops 2362232064 | bytes 1 | tf_op jit(solution)/shard_map/feed_forward/pallas_call | solution.py:400
  468.7 14.9 %terms.11 = (bf16[1024,512]{1,0:T(8,128)(2,1)S(1)}, bf16[1024,512]{1,0:T(8,128)(2,1)S(1)}, f32[1024,512]{1,0:T(8,128)S(1)}) custom-call(s32[3]{0:T(128)S(1)} %slice_bitcast_fusion.4.dests, bf16[1024,1408]{1,0:T(8,128)(2,1)} %copy-done.13, bf16[1024,1408]{1,0:T(8,128)(2,1)} %copy-done.15, bf16[2,2048,1408]{2,1,0:T(8,128)(2,1)} %bitcast.106, ...), custom_call_target="tpu_custom_call" | custom-call | flops 3543347968 | bytes 1 | tf_op jit(solution)/shard_map/terms/pallas_call | solution.py:196
  492.3 15.7 %collective-permute-done.36 = bf16[1024,512]{1,0:T(8,128)(2,1)S(1)} collective-permute-done((bf16[1024,512]{1,0:T(8,128)(2,1)S(1)}, bf16[1024,512]{1,0:T(8,128)(2,1)S(1)}, u32[]{:S(2)}, u32[]{:S(2)}) %collective-permute-start.36) | collective-permute-done | bytes 1048608 | tf_op jit(solution)/shard_map/ppermute | solution.py:215
  511.3 10.3 %collective-permute-start.37 = (bf16[1024,512]{1,0:T(8,128)(2,1)}, bf16[1024,512]{1,0:T(8,128)(2,1)}, u32[]{:S(2)}, u32[]{:S(2)}) collective-permute-start(bf16[1024,512]{1,0:T(8,128)(2,1)} %get-tuple-element.308), channel_id=1, source_target_pairs={{0,2},{2,4},{4,6},{1,3},{3,5},{5,7},{8,10},{10,12},{12,14},{9,11},... | collective-permute-start | bytes 3145736 | tf_op jit(solution)/shard_map/ppermute | solution.py:215
  521.6 8.2 down_grads.1.refs_1_
  554.8 13.0 %collective-permute-done.43.refs_3_.refs_1_ = bf16[1024,512]{1,0:T(8,128)(2,1)S(1)} collective-permute-done((bf16[1024,512]{1,0:T(8,128)(2,1)S(1)}, bf16[1024,512]{1,0:T(8,128)(2,1)S(1)}, u32[]{:S(2)}, u32[]{:S(2)}) %collective-permute-start.43) | collective-permute-done | bytes 1048608 | tf_op jit(solution)/shard_map/ppermute | solution.py:64
  572.3 16.4 %grads.4.refs_4_.refs_7_ = bf16[2,2048,1408]{2,1,0:T(8,128)(2,1)} custom-call(bf16[1024,2048]{1,0:T(8,128)(2,1)S(1)} %copy-done.7, bf16[1024,1408]{1,0:T(8,128)(2,1)S(1)} %copy-done.14, bf16[1024,1408]{1,0:T(8,128)(2,1)S(1)} %copy-done.16, bf16[1024,512]{1,0:T(8,128)(2,1)S(1)} %collective-permute-done.43.refs_3_.refs_1_, ...), custom_call_target="tpu_custom_call" | custom-call | flops 4724464128 | bytes 1 | tf_op jit(solution)/shard_map/grads/pallas_call | solution.py:290
  592.4 22.7 %collective-permute-done.46.refs_6_.refs_4_ = bf16[1024,512]{1,0:T(8,128)(2,1)S(1)} collective-permute-done((bf16[1024,512]{1,0:T(8,128)(2,1)}, bf16[1024,512]{1,0:T(8,128)(2,1)S(1)}, u32[]{:S(2)}, u32[]{:S(2)}) %collective-permute-start.46) | collective-permute-done | bytes 1048608 | tf_op jit(solution)/shard_map/ppermute | solution.py:64
  657.9 17.2 %reduce-scatter.8.cloned.1.call-done.refs_9_.refs_1_ = bf16[512,1408]{1,0:T(8,128)(2,1)} async-done(((bf16[4096,1408]{1,0:T(8,128)(2,1)}), bf16[512,1408]{1,0:T(8,128)(2,1)}) %reduce-scatter.8.cloned.1.call-update) | async-done | bytes 1441808 | tf_op jit(solution)/shard_map/reduce_scatter | solution.py:330
  675.2 9.5 terms.13
  692.7 15.3 %attention_backward.2 = (bf16[1024,512]{1,0:T(8,128)(2,1)S(1)}, bf16[1024,640]{1,0:T(8,128)(2,1)S(1)}, bf16[512,384]{1,0:T(8,128)(2,1)S(1)}, bf16[128,512]{1,0:T(8,128)(2,1)S(1)}) custom-call(bf16[1024,512]{1,0:T(8,128)(2,1)S(1)} %copy-done.69, bf16[1024,640]{1,0:T(8,128)(2,1)S(1)} %copy-done.63, bf16[512,384]{1,0:T(8,128)(2,1)S(1)} %copy-done.72, ...), custom_call_target="tpu_custom_call" | custom-call | flops 6800000000 | bytes 1 | tf_op jit(solution)/shard_map/attention_backward/pallas_call | solution.py:586
  723.8 16.2 %attention_backward.3 = (bf16[1024,512]{1,0:T(8,128)(2,1)S(1)}, bf16[1024,640]{1,0:T(8,128)(2,1)S(1)}, bf16[512,384]{1,0:T(8,128)(2,1)S(1)}, bf16[128,512]{1,0:T(8,128)(2,1)S(1)}) custom-call(bf16[1024,512]{1,0:T(8,128)(2,1)S(1)} %copy-done.66, bf16[1024,640]{1,0:T(8,128)(2,1)S(1)} %copy-done.60, bf16[512,384]{1,0:T(8,128)(2,1)} %collective-permute-done.15.far_v, ...), custom_call_target="tpu_custom_call" | custom-call | flops 6800000000 | bytes 1 | tf_op jit(solution)/shard_map/attention_backward/pallas_call | solution.py:586
  762.4 14.1 %terms.15 = (bf16[1024,512]{1,0:T(8,128)(2,1)S(1)}, bf16[1024,512]{1,0:T(8,128)(2,1)S(1)}, f32[1024,512]{1,0:T(8,128)}) custom-call(s32[3]{0:T(128)S(1)} %slice_bitcast_fusion.4.dests, bf16[1024,512]{1,0:T(8,128)(2,1)S(1)} %get-tuple-element.353.refs_0_.refs_1_, bf16[1024,512]{1,0:T(8,128)(2,1)S(1)} %get-tuple-element.352.refs_1_.refs_2_, ...), custom_call_target="tpu_custom_call" | custom-call | flops 2899102976 | bytes 1 | tf_op jit(solution)/shard_map/terms/pallas_call | solution.py:196
  816.1 9.1 grads.6
  842.3 19.8 %collective-permute-done.62 = bf16[1024,512]{1,0:T(8,128)(2,1)S(1)} collective-permute-done((bf16[1024,512]{1,0:T(8,128)(2,1)S(1)}, bf16[1024,512]{1,0:T(8,128)(2,1)S(1)}, u32[]{:S(2)}, u32[]{:S(2)}) %collective-permute-start.62) | collective-permute-done | bytes 1048608 | tf_op jit(solution)/shard_map/ppermute | solution.py:215
  865.7 8.7 collective-permute-start.63
  920.9 10.9 %collective-permute-done.74 = f32[2,256]{1,0:T(2,128)S(1)} collective-permute-done((f32[2,256]{1,0:T(2,128)S(1)}, f32[2,256]{1,0:T(2,128)S(1)}, u32[]{:S(2)}, u32[]{:S(2)}) %collective-permute-start.74) | collective-permute-done | bytes 2080 | tf_op jit(solution)/shard_map/ppermute | solution.py:58
  (617 shorter events, 473.8 us)
Async XLA Ops:
  7.2 153.5 %all-gather.10.cloned.1.call-start = ((), (), s32[]{:S(2)}) async-start(), calls=%async_computation.5 | async-start | bytes 4718592 | tf_op jit(solution)/shard_map/all_gather | solution.py:259
  32.7 128.1 %all-gather.12.cloned.1.call-start = ((), (), s32[]{:S(2)}) async-start(), calls=%async_computation.6 | async-start | bytes 5898240 | tf_op jit(solution)/shard_map/all_gather | solution.py:259
  34.9 201.3 %all-gather.14.cloned.1.call-start = ((), (), s32[]{:S(2)}) async-start(), calls=%async_computation.7 | async-start | bytes 4718592 | tf_op jit(solution)/shard_map/all_gather | solution.py:259
  97.2 300.1 %all-gather.16.cloned.1.call-start = ((), (), s32[]{:S(2)}) async-start(), calls=%async_computation.8 | async-start | bytes 5242880 | tf_op jit(solution)/shard_map/all_gather | solution.py:710
  125.5 271.8 %all-gather.20.cloned.1.call-start = ((), (), s32[]{:S(2)}) async-start(), calls=%async_computation.15 | async-start | bytes 6488064 | tf_op jit(solution)/shard_map/all_gather | solution.py:259
  128.1 296.1 %all-gather.22.cloned.1.call-start = ((), (), s32[]{:S(2)}) async-start(), calls=%async_computation.16 | async-start | bytes 5152768 | tf_op jit(solution)/shard_map/all_gather | solution.py:636
  128.2 27.1 %collective-permute-start.7 = (bf16[1024,512]{1,0:T(8,128)(2,1)S(1)}, bf16[1024,512]{1,0:T(8,128)(2,1)}, u32[]{:S(2)}, u32[]{:S(2)}) collective-permute-start(bf16[1024,512]{1,0:T(8,128)(2,1)S(1)} %copy-done.93), channel_id=1, source_target_pairs={{4,6},{5,7},{12,14},{13,15},{20,22},{21,23},{28,30},{29,31}} | collective-permute-start | bytes 3145736 | tf_op jit(solution)/shard_map/ppermute | solution.py:64
  194.8 235.2 %all-gather.18.cloned.1.call-start = ((), (), s32[]{:S(2)}) async-start(), calls=%async_computation.9 | async-start | bytes 12976128 | tf_op jit(solution)/shard_map/all_gather | solution.py:259
  208.4 466.7 %reduce-scatter.8.cloned.1.call-start = ((), (), s32[]{:S(2)}) async-start(), calls=%async_computation.11 | async-start | bytes 12976128 | tf_op jit(solution)/shard_map/reduce_scatter | solution.py:330
  288.5 36.1 %collective-permute-start.22 = (bf16[1024,512]{1,0:T(8,128)(2,1)S(1)}, bf16[1024,512]{1,0:T(8,128)(2,1)S(1)}, u32[]{:S(2)}, u32[]{:S(2)}) collective-permute-start(bf16[1024,512]{1,0:T(8,128)(2,1)S(1)} %get-tuple-element.315), channel_id=1, source_target_pairs={{6,4},{4,2},{2,0},{7,5},{5,3},{3,1},{14,12},{12,10},{10,8},{15,13}... | collective-permute-start | bytes 3145736 | tf_op jit(solution)/shard_map/ppermute | solution.py:215
  289.8 44.0 %collective-permute-start.19 = (bf16[1024,512]{1,0:T(8,128)(2,1)S(1)}, bf16[1024,512]{1,0:T(8,128)(2,1)S(1)}, u32[]{:S(2)}, u32[]{:S(2)}) collective-permute-start(bf16[1024,512]{1,0:T(8,128)(2,1)S(1)} %get-tuple-element.314), channel_id=1, source_target_pairs={{0,2},{2,4},{4,6},{1,3},{3,5},{5,7},{8,10},{10,12},{12,14},{9,11},... | collective-permute-start | bytes 3145736 | tf_op jit(solution)/shard_map/ppermute | solution.py:215
  336.4 31.0 %collective-permute-start.23 = (bf16[1024,512]{1,0:T(8,128)(2,1)S(1)}, bf16[1024,512]{1,0:T(8,128)(2,1)S(1)}, u32[]{:S(2)}, u32[]{:S(2)}) collective-permute-start(bf16[1024,512]{1,0:T(8,128)(2,1)S(1)} %multiply_convert_fusion.5.refs_0_), channel_id=1, source_target_pairs={{0,2},{2,4},{4,6},{1,3},{3,5},{5,7},{8,10},{10,12},{12,14},{9,11},... | collective-permute-start | bytes 3145736 | tf_op jit(solution)/shard_map/ppermute | solution.py:64
  369.0 26.6 %collective-permute-start.26 = (bf16[1024,512]{1,0:T(8,128)(2,1)S(1)}, bf16[1024,512]{1,0:T(8,128)(2,1)}, u32[]{:S(2)}, u32[]{:S(2)}) collective-permute-start(bf16[1024,512]{1,0:T(8,128)(2,1)S(1)} %collective-permute-done.24.refs_2_), channel_id=1, source_target_pairs={{2,0},{4,2},{3,1},{5,3},{10,8},{12,10},{11,9},{13,11},{18,16},{20,... | collective-permute-start | bytes 3145736 | tf_op jit(solution)/shard_map/ppermute | solution.py:64
  370.3 48.5 %collective-permute-start.27 = (bf16[1024,512]{1,0:T(8,128)(2,1)}, bf16[1024,512]{1,0:T(8,128)(2,1)}, u32[]{:S(2)}, u32[]{:S(2)}) collective-permute-start(bf16[1024,512]{1,0:T(8,128)(2,1)} %collective-permute-done.25.refs_3_), channel_id=1, source_target_pairs={{4,6},{5,7},{12,14},{13,15},{20,22},{21,23},{28,30},{29,31}} | collective-permute-start | bytes 3145736 | tf_op jit(solution)/shard_map/ppermute | solution.py:64
  509.9 26.7 %collective-permute-start.39 = (bf16[1024,512]{1,0:T(8,128)(2,1)}, bf16[1024,512]{1,0:T(8,128)(2,1)}, u32[]{:S(2)}, u32[]{:S(2)}) collective-permute-start(bf16[1024,512]{1,0:T(8,128)(2,1)} %get-tuple-element.309), channel_id=1, source_target_pairs={{6,4},{4,2},{2,0},{7,5},{5,3},{3,1},{14,12},{12,10},{10,8},{15,13}... | collective-permute-start | bytes 3145736 | tf_op jit(solution)/shard_map/ppermute | solution.py:215
  511.3 26.4 %collective-permute-start.37 = (bf16[1024,512]{1,0:T(8,128)(2,1)}, bf16[1024,512]{1,0:T(8,128)(2,1)}, u32[]{:S(2)}, u32[]{:S(2)}) collective-permute-start(bf16[1024,512]{1,0:T(8,128)(2,1)} %get-tuple-element.308), channel_id=1, source_target_pairs={{0,2},{2,4},{4,6},{1,3},{3,5},{5,7},{8,10},{10,12},{12,14},{9,11},... | collective-permute-start | bytes 3145736 | tf_op jit(solution)/shard_map/ppermute | solution.py:215
  588.8 162.5 %reduce-scatter.6.cloned.1.call-start = ((), (), s32[]{:S(2)}) async-start(), calls=%async_computation.10 | async-start | bytes 6488064 | tf_op jit(solution)/shard_map/reduce_scatter | solution.py:330
  589.5 307.1 %reduce-scatter.10.cloned.1.call-start = ((), (), s32[]{:S(2)}) async-start(), calls=%async_computation.12 | async-start | bytes 4718592 | tf_op jit(solution)/shard_map/reduce_scatter | solution.py:330
  591.7 37.5 %collective-permute-start.55 = (bf16[1024,512]{1,0:T(8,128)(2,1)S(1)}, bf16[1024,512]{1,0:T(8,128)(2,1)S(1)}, u32[]{:S(2)}, u32[]{:S(2)}) collective-permute-start(bf16[1024,512]{1,0:T(8,128)(2,1)S(1)} %collective-permute-done.45.refs_5_.refs_3_), channel_id=1, source_target_pairs={{4,6},{5,7},{12,14},{13,15},{20,22},{21,23},{28,30},{29,31}} | collective-permute-start | bytes 3145736 | tf_op jit(solution)/shard_map/ppermute | solution.py:64
  621.0 63.6 %collective-permute-start.47 = (bf16[1024,512]{1,0:T(8,128)(2,1)}, bf16[1024,512]{1,0:T(8,128)(2,1)}, u32[]{:S(2)}, u32[]{:S(2)}) collective-permute-start(bf16[1024,512]{1,0:T(8,128)(2,1)} %terms.12.refs_4_), channel_id=1, source_target_pairs={{0,2},{1,3},{8,10},{9,11},{16,18},{17,19},{24,26},{25,27}} | collective-permute-start | bytes 3145736 | tf_op jit(solution)/shard_map/ppermute | solution.py:215
  627.5 57.2 %collective-permute-start.50 = (bf16[1024,512]{1,0:T(8,128)(2,1)}, bf16[1024,512]{1,0:T(8,128)(2,1)}, u32[]{:S(2)}, u32[]{:S(2)}) collective-permute-start(bf16[1024,512]{1,0:T(8,128)(2,1)} %terms.12.refs_4_), channel_id=1, source_target_pairs={{6,4},{7,5},{14,12},{15,13},{22,20},{23,21},{30,28},{31,29}} | collective-permute-start | bytes 3145736 | tf_op jit(solution)/shard_map/ppermute | solution.py:215
  675.1 259.5 %reduce-scatter.14.cloned.1.call-start = ((), (), s32[]{:S(2)}) async-start(), calls=%async_computation.14 | async-start | bytes 4718592 | tf_op jit(solution)/shard_map/reduce_scatter | solution.py:330
  707.9 33.4 %collective-permute-start.57 = (bf16[128,512]{1,0:T(8,128)(2,1)S(1)}, bf16[128,512]{1,0:T(8,128)(2,1)S(1)}, u32[]{:S(2)}, u32[]{:S(2)}) collective-permute-start(bf16[128,512]{1,0:T(8,128)(2,1)S(1)} %get-tuple-element.89), channel_id=1, source_target_pairs={{8,0},{9,1},{10,2},{11,3},{12,4},{13,5},{14,6},{15,7},{24,16},{25,... | collective-permute-start | bytes 393224 | tf_op jit(solution)/shard_map/ppermute | solution.py:766
  709.2 34.5 %collective-permute-start.59 = (bf16[512,384]{1,0:T(8,128)(2,1)S(1)}, bf16[512,384]{1,0:T(8,128)(2,1)S(1)}, u32[]{:S(2)}, u32[]{:S(2)}) collective-permute-start(bf16[512,384]{1,0:T(8,128)(2,1)S(1)} %get-tuple-element.95), channel_id=1, source_target_pairs={{8,0},{9,1},{10,2},{11,3},{12,4},{13,5},{14,6},{15,7},{24,16},{25,... | collective-permute-start | bytes 1179656 | tf_op jit(solution)/shard_map/ppermute | solution.py:765
  714.2 34.5 %collective-permute-start.52 = (bf16[1024,512]{1,0:T(8,128)(2,1)S(1)}, bf16[1024,512]{1,0:T(8,128)(2,1)S(1)}, u32[]{:S(2)}, u32[]{:S(2)}) collective-permute-start(bf16[1024,512]{1,0:T(8,128)(2,1)S(1)} %get-tuple-element.305.rest_refs_1_), channel_id=1, source_target_pairs={{6,4},{4,2},{2,0},{7,5},{5,3},{3,1},{14,12},{12,10},{10,8},{15,13}... | collective-permute-start | bytes 3145736 | tf_op jit(solution)/shard_map/ppermute | solution.py:215
  715.6 33.1 %collective-permute-start.49 = (bf16[1024,512]{1,0:T(8,128)(2,1)S(1)}, bf16[1024,512]{1,0:T(8,128)(2,1)S(1)}, u32[]{:S(2)}, u32[]{:S(2)}) collective-permute-start(bf16[1024,512]{1,0:T(8,128)(2,1)S(1)} %get-tuple-element.304.rest_refs_0_), channel_id=1, source_target_pairs={{0,2},{2,4},{4,6},{1,3},{3,5},{5,7},{8,10},{10,12},{12,14},{9,11},... | collective-permute-start | bytes 3145736 | tf_op jit(solution)/shard_map/ppermute | solution.py:215
  757.7 26.5 %collective-permute-start.61 = (bf16[1024,512]{1,0:T(8,128)(2,1)S(1)}, bf16[1024,512]{1,0:T(8,128)(2,1)S(1)}, u32[]{:S(2)}, u32[]{:S(2)}) collective-permute-start(bf16[1024,512]{1,0:T(8,128)(2,1)S(1)} %terms.14.refs_8_), channel_id=1, source_target_pairs={{0,2},{1,3},{8,10},{9,11},{16,18},{17,19},{24,26},{25,27}} | collective-permute-start | bytes 3145736 | tf_op jit(solution)/shard_map/ppermute | solution.py:215
  796.0 139.8 %reduce-scatter.12.cloned.1.call-start = ((), (), s32[]{:S(2)}) async-start(), calls=%async_computation.13 | async-start | bytes 5898240 | tf_op jit(solution)/shard_map/reduce_scatter | solution.py:330
  798.3 29.4 %collective-permute-start.53 = (bf16[1024,256]{1,0:T(8,128)(2,1)}, bf16[1024,256]{1,0:T(8,128)(2,1)}, u32[]{:S(2)}, u32[]{:S(2)}) collective-permute-start(bf16[1024,256]{1,0:T(8,128)(2,1)} %get-tuple-element.336), channel_id=1, source_target_pairs={{0,0},{1,8},{8,1},{9,9},{2,2},{3,10},{10,3},{11,11},{4,4},{5,12},{... | collective-permute-start | bytes 1572872 | tf_op jit(solution)/shard_map/ppermute | solution.py:93
  834.8 27.3 %collective-permute-start.62 = (bf16[1024,512]{1,0:T(8,128)(2,1)S(1)}, bf16[1024,512]{1,0:T(8,128)(2,1)S(1)}, u32[]{:S(2)}, u32[]{:S(2)}) collective-permute-start(bf16[1024,512]{1,0:T(8,128)(2,1)S(1)} %copy-done.35), channel_id=1, source_target_pairs={{0,2},{2,4},{1,3},{3,5},{8,10},{10,12},{9,11},{11,13},{16,18},{18,... | collective-permute-start | bytes 3145736 | tf_op jit(solution)/shard_map/ppermute | solution.py:215
  864.1 32.5 %collective-permute-start.66 = (bf16[1024,512]{1,0:T(8,128)(2,1)}, bf16[1024,512]{1,0:T(8,128)(2,1)}, u32[]{:S(2)}, u32[]{:S(2)}) collective-permute-start(bf16[1024,512]{1,0:T(8,128)(2,1)} %get-tuple-element.301), channel_id=1, source_target_pairs={{6,4},{4,2},{2,0},{7,5},{5,3},{3,1},{14,12},{12,10},{10,8},{15,13}... | collective-permute-start | bytes 3145736 | tf_op jit(solution)/shard_map/ppermute | solution.py:215
  865.7 31.0 %collective-permute-start.63 = (bf16[1024,512]{1,0:T(8,128)(2,1)}, bf16[1024,512]{1,0:T(8,128)(2,1)}, u32[]{:S(2)}, u32[]{:S(2)}) collective-permute-start(bf16[1024,512]{1,0:T(8,128)(2,1)} %get-tuple-element.300), channel_id=1, source_target_pairs={{0,2},{2,4},{4,6},{1,3},{3,5},{5,7},{8,10},{10,12},{12,14},{9,11},... | collective-permute-start | bytes 3145736 | tf_op jit(solution)/shard_map/ppermute | solution.py:215
  (208 other events, 2324.8 us)
Sparse Core Ops, SparseCore 0:
  32.9 37.3 all-gather.9
  72.7 44.2 all-gather.11
  119.5 37.6 all-gather.13
  159.2 80.7 all-gather.15
  242.3 41.8 all-gather.19
  286.9 67.1 all-gather.21
  356.6 68.5 all-gather.17
  588.9 86.1 reduce-scatter.7
  678.5 59.0 reduce-scatter.5
  741.2 51.3 reduce-scatter.9
  796.2 51.7 reduce-scatter.13
  851.6 56.5 reduce-scatter.11

commit v3 on v2

--- a/solution.py
+++ b/solution.py
@@ -33,7 +33,7 @@
 
 
 def cost(matmul_flops):
-    return pl.CostEstimate(flops=int(0.4 * matmul_flops), bytes_accessed=1, transcendentals=0)
+    return pl.CostEstimate(flops=int(0.05 * matmul_flops), bytes_accessed=1, transcendentals=0)
 
 
 CHEAP = cost(0)
@@ -210,6 +210,10 @@
     )(dests, *lefts, *[weight for weight, s in rights], *earlier)
 
 
+def pieces_t(lefts, rights, *earlier):
+    return terms_t(lefts, rights, line_order(), [BF, BF, BF, F32], *earlier)
+
+
 def hop(values, step, count):
     places = range(count) if step > 0 else range(3, 3 - count, -1)
     return lax.ppermute(values, "t", [(i, i + step) for i in places])
@@ -225,11 +229,19 @@
         dests = jnp.stack([mine ^ offset for offset in range(ways)]).astype(jnp.int32)
         parts = terms_t(lefts, rights, dests, [F32] + [BF] * (ways - 1), *earlier)
         return [parts[0]] + [peer(part, "t", offset) for offset, part in enumerate(parts) if offset], parts
+    dests = line_order()
+    [first] = terms_t(lefts, rights, dests[:1], [BF], *earlier)
+    return along_line(first, *terms_t(lefts, rights, dests[1:], [BF, BF, F32], first))
+
+
+def line_order():
     order = jnp.asarray(np.array([[3, 2, 1, 0], [3, 2, 0, 1], [0, 1, 3, 2], [0, 1, 2, 3]], np.int32))
-    dests = lax.dynamic_index_in_dim(order, mine, 0, False)
-    [first] = terms_t(lefts, rights, dests[:1], [BF], *earlier)
+    return lax.dynamic_index_in_dim(order, lax.axis_index("t"), 0, False)
+
+
+def along_line(first, second, third, own):
+    mine = lax.axis_index("t")
     up, down = hop(first, 1, 1), hop(first, -1, 1)
-    second, third, own = terms_t(lefts, rights, dests[1:], [BF, BF, F32], first)
     wide = lambda a: a.astype(F32)
     up2 = (jnp.where(mine == 0, wide(second), wide(first)) + wide(up)).astype(BF)
     down2 = (jnp.where(mine == 3, wide(second), wide(first)) + wide(down)).astype(BF)
@@ -253,10 +265,13 @@
     return total
 
 
-def gather_weight(shard, *earlier):
+def rounded(shard, *earlier):
     flag = told(lax.axis_index("s") >= 0, *earlier)
-    shard = jnp.where(flag, shard, 0.0).astype(BF)
-    full = lax.all_gather(shard, ("s", "y", "c"), axis=0, tiled=False)
+    return jnp.where(flag, shard, 0.0).astype(BF)
+
+
+def gather_weight(shard):
+    full = lax.all_gather(shard.astype(BF), ("s", "y", "c"), axis=0, tiled=False)
     return full.reshape((2, -1) + shard.shape)
 
 
@@ -264,9 +279,28 @@
     return full.reshape(2, -1, full.shape[3])
 
 
-def pack(pair):
+def pack_body(pair, *refs):
+    out = refs[-1]
     cut = pair.shape[2] // HV * HV
-    return jnp.concatenate([pair[:, 0, :cut], pair[:, 1, :cut], pair[:, 0, cut:], pair[:, 1, cut:]], axis=1)
+    gate, up = pair[:, 0, :].astype(BF), pair[:, 1, :].astype(BF)
+    out[:, :cut] = gate[:, :cut]
+    out[:, cut : 2 * cut] = up[:, :cut]
+    out[:, 2 * cut :] = jnp.concatenate([gate[:, cut:], up[:, cut:]], axis=1)
+
+
+def packed_rounded(pair, *earlier):
+    rows, ways, columns = pair.shape
+    step = min(128, rows)
+    return pl.pallas_call(
+        pack_body,
+        grid=(rows // step,),
+        in_specs=[pl.BlockSpec((step, ways, columns), lambda i: (i, 0, 0))] + anywhere(len(earlier)),
+        out_specs=pl.BlockSpec((step, ways * columns), lambda i: (i, 0)),
+        out_shape=jax.ShapeDtypeStruct((rows, ways * columns), BF),
+        compiler_params=pltpu.CompilerParams(vmem_limit_bytes=40 * 2**20),
+        cost_estimate=CHEAP,
+        name="pack",
+    )(pair, *earlier)
 
 
 def unpack(packed):
@@ -361,7 +395,7 @@
         out[...] = (mm(left[...], right[0]) * factor[...]).astype(BF)
 
 
-def project(left, weights, factor):
+def project(left, weights, factor, *earlier):
     tokens = left.shape[0]
     rows = min(256, tokens)
     by_rows = lambda n: pl.BlockSpec((rows, n), lambda i: (i, 0))
@@ -369,13 +403,14 @@
         functools.partial(project_body, len(weights)),
         grid=(tokens // rows,),
         in_specs=[by_rows(left.shape[1]), by_rows(1)]
-        + [pl.BlockSpec((1,) + w.shape[1:], lambda i, s=s: (s, 0, 0)) for w, s in weights],
+        + [pl.BlockSpec((1,) + w.shape[1:], lambda i, s=s: (s, 0, 0)) for w, s in weights]
+        + anywhere(len(earlier)),
         out_specs=[by_rows(w.shape[2]) for w, s in weights],
         out_shape=[jax.ShapeDtypeStruct((tokens, w.shape[2]), BF) for w, s in weights],
         compiler_params=pltpu.CompilerParams(vmem_limit_bytes=40 * 2**20),
         cost_estimate=cost(2 * tokens * left.shape[1] * sum(w.shape[2] for w, s in weights)),
         name="project",
-    )(left, factor, *[w for w, s in weights])
+    )(left, factor, *[w for w, s in weights], *earlier)
 
 
 def feed_body(scaled, factor, back, weight, hidden, dboth):
@@ -414,7 +449,8 @@
     )(scaled, factor, back, weight)
 
 
-def forward_body(heads, tokens, wqk, rest, far_v, far_w, docs_c, docs_r, out, den):
+def forward_body(heads, tokens, wqk, rest, far_v, far_w, docs_c, docs_r, *rest_refs):
+    out, den = rest_refs[-2:]
     lanes = heads * HV
     for i in range(heads):
         at = i * HV
@@ -565,19 +601,21 @@
 VMEM = pltpu.CompilerParams(vmem_limit_bytes=28 * 2**20)
 
 
-def attention_forward(heads, wqk, rest, far_v, far_w, docs_c, docs_r):
+def attention_forward(heads, wqk, rest, far_v, far_w, docs_c, docs_r, *earlier):
     tokens = wqk.shape[0]
+    ins = (wqk, rest, far_v, far_w, docs_c, docs_r)
     outs = (
         jax.ShapeDtypeStruct((tokens, 2 * heads * HV), BF),
         jax.ShapeDtypeStruct((tokens, heads), F32),
     )
     return pl.pallas_call(
         functools.partial(forward_body, heads, tokens),
+        in_specs=[pl.BlockSpec(memory_space=pltpu.VMEM)] * len(ins) + anywhere(len(earlier)),
         out_shape=outs,
         compiler_params=VMEM,
         cost_estimate=cost(6e9),
         name="attention_forward",
-    )(wqk, rest, far_v, far_w, docs_c, docs_r)
+    )(*ins, *earlier)
 
 
 def attention_backward(heads, wqk, rest, far_v, far_w, docs_c, docs_r, out, den, dout, *earlier):
@@ -633,9 +671,9 @@
 def owned_states(heads, states, owner):
     ways = lax.axis_size("t")
     mine_t, side = lax.axis_index("t"), lax.axis_index("s")
-    states = lax.all_gather(states.astype(BF), ("c", "s", "t"), axis=0, tiled=False)
-    states = lax.dynamic_slice_in_dim(states, (2 + lax.axis_index("c")) * ways, ways, 0)
-    states = states.reshape(GROUPS, F1, HV)
+    states = lax.all_gather(states.astype(BF), ("c", "s"), axis=0, tiled=False)
+    states = lax.dynamic_index_in_dim(states, 2 + lax.axis_index("c"), 0, False)
+    states = lax.all_gather(states, "t", axis=0, tiled=False).reshape(GROUPS, F1, HV)
     slots = GROUPS // ways
     groups = jnp.arange(GROUPS, dtype=jnp.int32)
     mine = owner == 2 * mine_t + side
@@ -698,15 +736,18 @@
         [head_proj[:, 2:].reshape(rows, -1), feature_proj.reshape(rows, -1), jnp.zeros((rows, extra), F32)], axis=1
     )
     parts = send_t(scaled_mine)
-    wqk_full = rows_of(gather_weight(wqk_shard, x_low))
-    rest_full = rows_of(gather_weight(rest_shard, x_low))
-    begun = parts[3:5]
-    mixer_full = rows_of(gather_weight(jnp.transpose(mixer_out, (2, 0, 1)).reshape(rows, -1), *begun))
-    both_full = rows_of(gather_weight(pack(gate_up), *begun))
-    down_full = gather_weight(down_proj, *begun)
+    wqk_full = rows_of(gather_weight(rounded(wqk_shard, x_low)))
+    rest_full = rows_of(gather_weight(rounded(rest_shard, x_low)))
+    begun = parts[1:3]
+    mixer_shard = rounded(jnp.transpose(mixer_out, (2, 0, 1)).reshape(rows, -1), *begun)
+    down_shard = rounded(down_proj, *begun)
+    both_shard = packed_rounded(gate_up, *begun)
+    mixer_full = rows_of(gather_weight(mixer_shard))
+    down_full = gather_weight(down_shard)
+    both_full = rows_of(gather_weight(both_shard))
     factor_one = lax.rsqrt(total_t(jnp.sum(x * x, axis=1)) / D + EPSILON)[:, None]
-    scaled_one = join_t(parts)
-    dy_mine = enter(out_grad, *begun)
+    scaled_one = join_t(parts, mixer_shard, down_shard, both_shard)
+    dy_mine = hold(enter(out_grad, *begun), scaled_one)
     dy = lax.all_gather(dy_mine, "t", axis=1, tiled=True)
     wqk, rest = [], []
     for s in range(2):
@@ -726,41 +767,48 @@
         attended.append(one)
         denom.append(two)
 
-    mixed = add_up(spread_t(attended, both_s(mixer_full))[0])
+    parts, second = spread_t(attended, both_s(mixer_full))
+    dhidden = [back_hidden(dy, down_full, s) for s in range(2)]
+    mixed = add_up([hold(parts[0], *dhidden)] + parts[1:])
     middle = x + mixed
     factor_two = lax.rsqrt(total_t(jnp.sum(middle * middle, axis=1)) / D + EPSILON)[:, None]
     scaled_mine = (middle * gains[1]).astype(BF)
     parts = send_t(scaled_mine)
-    dhidden = [back_hidden(dy, down_full, s) for s in range(2)]
-    last = jnp.stack([p[-REACH:, lanes:] for p in rest])
+    last = hold(jnp.stack([p[-REACH:, lanes:] for p in rest]), *second[:2])
     states = row_states(heads, last[:, :, lanes + heads * FEAT : lanes + 2 * heads * FEAT], last[:, :, :lanes], docs_r[0])
-    row_state = owned_states(heads, states, group_owner)
-    scaled_two = join_t(parts, *dhidden)
+    scaled_two = join_t(parts, states)
+    row_state = owned_states(heads, hold(states, scaled_two), group_owner)
 
     hidden, dboth = [], []
     for s in range(2):
         one, two = feed_forward(scaled_two, factor_two, dhidden[s], both_full, s)
         hidden.append(one)
         dboth.append(two)
-    parts, second = spread_t(dboth, both_s(both_full), row_state)
+    parts, second = spread_t(dboth, both_s(both_full))
     for_down = down_grads(dy, hidden, *second[:2])
-    upstream_two = add_up([hold(parts[0], for_down)] + parts[1:])
+    pieces = pieces_t(hidden, both_s(down_full), *second[:2]) if line() else []
+    upstream_two = add_up([hold(parts[0], for_down, *pieces)] + parts[1:])
     back_two, gain_two = norm_back(middle, factor_two, gains[1], upstream_two)
     dmixed_mine = (dy_mine.astype(F32) + back_two).astype(BF)
     parts = send_t(dmixed_mine)
     for_both = grads(scaled_two, dboth, *parts[1:3])
-    branch_parts, second = spread_t(hidden, both_s(down_full), for_both, *parts[3:5])
+    if line():
+        first = hold(pieces[0], *parts[3:5])
+        branch_parts, second = along_line(first, *pieces[1:])
+        second = [first] + second
+    else:
+        branch_parts, second = spread_t(hidden, both_s(down_full))
     dmixed = join_t(parts, for_both)
     down_sum, both_sum = scatter_grad(for_down), scatter_grad(for_both)
 
     branch = add_up(branch_parts)
     out_y = layer_in + leave((mixed + branch).astype(BF)).astype(F32)
-    dattended = project(dmixed, both_s(mixer_full), jnp.ones((tokens, 1), F32))
-    mixer_sum = scatter_grad(hold(grads(dmixed, attended, *dattended), both_sum))
+    dattended = project(dmixed, both_s(mixer_full), jnp.ones((tokens, 1), F32), *second[1:3])
+    mixer_sum = scatter_grad(grads(dmixed, attended, *dattended))
     dwqk, drest = [], []
     for s in range(2):
         one, two, three, four = attention_backward(
-            heads, wqk[s], rest[s], far_v[s], far_w[s], docs_c, docs_r, attended[s], denom[s], dattended[s], *second[2 * s : 2 * s + 2]
+            heads, wqk[s], rest[s], far_v[s], far_w[s], docs_c, docs_r, attended[s], denom[s], dattended[s], *([row_state] if s else second[3:5])
         )
         far_three = lax.ppermute(three, "c", behind).astype(F32)
         far_four = lax.ppermute(four, "c", behind).astype(F32)
@@ -772,12 +820,16 @@
         )
         dwqk.append((one * factor_one).astype(BF))
         drest.append((two * factor_one).astype(BF))
-    parts, second = spread_t(dwqk + drest, both_s(wqk_full) + both_s(rest_full), down_sum, both_sum, branch)
-    rest_sum = scatter_grad(grads(scaled_one, drest, *second[:2]))
-    wqk_sum = scatter_grad(grads(scaled_one, dwqk, *second[:2]))
-    upstream_one = add_up([hold(parts[0], mixer_sum)] + parts[1:])
+    for_rest = grads(scaled_one, drest, branch)
+    for_wqk = grads(scaled_one, dwqk, for_rest)
+    rest_sum, wqk_sum = scatter_grad(for_rest), scatter_grad(for_wqk)
+    parts, second = spread_t(dwqk + drest, both_s(wqk_full) + both_s(rest_full), for_wqk, both_sum)
+    upstream_one = add_up(parts)
     back_one, gain_one = norm_back(x, factor_one, gains[0], upstream_one)
-    grad_x = out_grad + leave((back_one + back_two).astype(BF)).astype(F32)
+    back = (back_one + back_two).astype(BF)
+    grad_x = out_grad + leave(back).astype(F32)
+    both_sum, down_sum = [hold(a, *second[:1]) for a in (both_sum, down_sum)]
+    wqk_sum, rest_sum, mixer_sum = [hold(a, back) for a in (wqk_sum, rest_sum, mixer_sum)]
     wqk_sum, rest_sum, mixer_sum, both_sum = [a.astype(F32) for a in (wqk_sum, rest_sum, mixer_sum, both_sum)]
     down_sum = down_sum[0].astype(F32)
     head_sum = jnp.concatenate([wqk_sum, rest_sum[:, : 2 * lanes]], axis=1)

time: 969 us -> 965 us (level)
  starting transfers between devices: 174 us -> 159 us
    ppermute x2, waiting for transfers between devices: 30.2 us -> 11.1 us  [enter(): other = lax.ppermute(second, ('c', 's'), TURN)]
    all_gather x6 -> x7, waiting for transfers between devices: 0.05 us -> 16.2 us  [the longest x5 16.2 us: gather_weight(): lax.all_gather(shard.astype(BF), ('s', 'y', 'c'), axis=0, tiled=False)]
    ppermute x24, starting transfers between devices: 84 us -> 70.1 us  [hop(): return lax.ppermute(values, 't', [(i, i + step) for i in places])]
    unnamed x317 -> x343, local copies, waits for them, and re-layouts: 80.7 us -> 90.5 us
    pallas_call x8 -> x7, Pallas kernels: 65.2 us -> 63.6 us  [terms_t(): pl.pallas_call(functools.partial(terms_body, count, pieces), grid_spec=pl...]
  transfers between devices with their start and end apart: 87 -> 88, of which waited for: 31 -> 34; matrix products, arithmetic and copies ran while one was open for 13% -> 16% of each run, Pallas kernels for 19% -> 21%
where the time goes in v3:
time: 965 us; the launch traced here: 953 us
  waiting for transfers between devices  333 us (35%)
  Pallas kernels  228 us (24%)
  starting transfers between devices  159 us (16%)
  local copies, waits for them, and re-layouts  119 us (12%)
  other arithmetic  91.3 us (9%)
  between operations  18.7 us (2%)
    ppermute x18, waiting for transfers between devices, shift(): return lax.ppermute(values, 't', [(i, i + step) for i in places])  132 us
    ppermute x24, waiting for transfers between devices, hop(): return lax.ppermute(values, 't', [(i, i + step) for i in places])  126 us
    unnamed x343, local copies, waits for them, and re-layouts  90.5 us
    ppermute x24, starting transfers between devices, hop(): return lax.ppermute(values, 't', [(i, i + step) for i in places])  70.1 us
    pallas_call x7, Pallas kernels, terms_t(): pl.pallas_call(functools.partial(terms_body, count, pieces), grid_spec=pl...  63.6 us
    pallas_call x4, Pallas kernels, grads(): pl.pallas_call(functools.partial(grads_body, count), grid=(left.shape[1]...  38.9 us
    ppermute x18, starting transfers between devices, shift(): return lax.ppermute(values, 't', [(i, i + step) for i in places])  31.4 us
    pallas_call x2, Pallas kernels, attention_backward(): pl.pallas_call(functools.partial(backward_body, heads, tokens), in_specs=...  30.5 us
  transfers between devices with their start and end apart: 88, of which 34 were waited for; matrix products, arithmetic and copies ran while one was open for 16% of the time, Pallas kernels for 21%

profile of v3, /device:TPU:0, one launch (start us, length us, event | category | flops | bytes accessed | tf_op | source)
XLA Modules:
  0.0 952.5 jit_solution(13270535887472566002)
XLA Ops:
  16.9 11.1 %collective-permute-done.1 = bf16[1024,256]{1,0:T(8,128)(2,1)} collective-permute-done((bf16[1024,256]{1,0:T(8,128)(2,1)}, bf16[1024,256]{1,0:T(8,128)(2,1)}, u32[]{:S(2)}, u32[]{:S(2)}) %collective-permute-start.1) | collective-permute-done | bytes 524320 | tf_op jit(solution)/shard_map/ppermute | solution.py:83
  44.5 19.6 %collective-permute-done.3.refs_1_.refs_0_ = bf16[1024,512]{1,0:T(8,128)(2,1)S(1)} collective-permute-done((bf16[1024,512]{1,0:T(8,128)(2,1)S(1)}, bf16[1024,512]{1,0:T(8,128)(2,1)S(1)}, u32[]{:S(2)}, u32[]{:S(2)}) %collective-permute-start.3) | collective-permute-done | bytes 1048608 | tf_op jit(solution)/shard_map/ppermute | solution.py:64
  78.8 22.5 %collective-permute-done.6.refs_4_ = bf16[1024,512]{1,0:T(8,128)(2,1)} collective-permute-done((bf16[1024,512]{1,0:T(8,128)(2,1)S(1)}, bf16[1024,512]{1,0:T(8,128)(2,1)}, u32[]{:S(2)}, u32[]{:S(2)}) %collective-permute-start.6) | collective-permute-done | bytes 1048608 | tf_op jit(solution)/shard_map/ppermute | solution.py:64
  152.1 7.9 project.4
  165.8 8.1 project.3
  206.9 7.3 terms.8
  214.3 34.9 %collective-permute-done.19 = bf16[1024,512]{1,0:T(8,128)(2,1)} collective-permute-done((bf16[1024,512]{1,0:T(8,128)(2,1)S(1)}, bf16[1024,512]{1,0:T(8,128)(2,1)}, u32[]{:S(2)}, u32[]{:S(2)}) %collective-permute-start.19) | collective-permute-done | bytes 1048608 | tf_op jit(solution)/shard_map/ppermute | solution.py:219
  257.6 20.4 %collective-permute-done.20 = bf16[1024,512]{1,0:T(8,128)(2,1)S(1)} collective-permute-done((bf16[1024,512]{1,0:T(8,128)(2,1)S(1)}, bf16[1024,512]{1,0:T(8,128)(2,1)S(1)}, u32[]{:S(2)}, u32[]{:S(2)}) %collective-permute-start.20) | collective-permute-done | bytes 1048608 | tf_op jit(solution)/shard_map/ppermute | solution.py:219
  281.8 6.9 collective-permute-start.21
  290.1 16.1 %all-gather.22.cloned.1.call-done = bf16[5632,512]{1,0:T(8,128)(2,1)} async-done(((bf16[704,512]{1,0:T(8,128)(2,1)}), bf16[5632,512]{1,0:T(8,128)(2,1)}) %all-gather.22.cloned.1.call-update) | async-done | bytes 5767184 | tf_op jit(solution)/shard_map/all_gather | solution.py:274
  331.9 21.4 %collective-permute-done.25.refs_1_ = bf16[1024,512]{1,0:T(8,128)(2,1)S(1)} collective-permute-done((bf16[1024,512]{1,0:T(8,128)(2,1)S(1)}, bf16[1024,512]{1,0:T(8,128)(2,1)S(1)}, u32[]{:S(2)}, u32[]{:S(2)}) %collective-permute-start.25) | collective-permute-done | bytes 1048608 | tf_op jit(solution)/shard_map/ppermute | solution.py:64
  365.3 19.5 %collective-permute-done.28.refs_4_ = bf16[1024,512]{1,0:T(8,128)(2,1)} collective-permute-done((bf16[1024,512]{1,0:T(8,128)(2,1)S(1)}, bf16[1024,512]{1,0:T(8,128)(2,1)}, u32[]{:S(2)}, u32[]{:S(2)}) %collective-permute-start.28) | collective-permute-done | bytes 1048608 | tf_op jit(solution)/shard_map/ppermute | solution.py:64
  395.5 15.4 %collective-permute-done.31 = f32[1024]{0:T(1024)S(1)} collective-permute-done((f32[1024]{0:T(1024)S(1)}, f32[1024]{0:T(1024)S(1)}, u32[]{:S(2)}, u32[]{:S(2)}) %collective-permute-start.31) | collective-permute-done | bytes 4128 | tf_op jit(solution)/shard_map/ppermute | solution.py:58
  418.9 10.7 %feed_forward.3 = (bf16[1024,704]{1,0:T(8,128)(2,1)S(1)}, bf16[1024,1408]{1,0:T(8,128)(2,1)S(1)}) custom-call(bf16[1024,2048]{1,0:T(8,128)(2,1)S(1)} %copy-done.4, f32[1024,1]{1,0:T(8,128)S(1)} %copy.203.factor, bf16[1024,704]{1,0:T(8,128)(2,1)S(1)} %copy-done.43, bf16[2,2048,1408]{2,1,0:T(8,128)(2,1)} %bitcast.95), custom_call_target="tpu_custom_call" | custom-call | flops 295279008 | bytes 1 | tf_op jit(solution)/shard_map/feed_forward/pallas_call | solution.py:435
  432.4 10.6 %feed_forward.2 = (bf16[1024,704]{1,0:T(8,128)(2,1)S(1)}, bf16[1024,1408]{1,0:T(8,128)(2,1)S(1)}) custom-call(bf16[1024,2048]{1,0:T(8,128)(2,1)S(1)} %copy-done.4, f32[1024,1]{1,0:T(8,128)S(1)} %copy.203.factor, bf16[1024,704]{1,0:T(8,128)(2,1)S(1)} %copy-done.41, bf16[2,2048,1408]{2,1,0:T(8,128)(2,1)} %bitcast.96), custom_call_target="tpu_custom_call" | custom-call | flops 295279008 | bytes 1 | tf_op jit(solution)/shard_map/feed_forward/pallas_call | solution.py:435
  444.2 7.2 terms.9.refs_4_
  453.6 14.9 %terms.10 = (bf16[1024,512]{1,0:T(8,128)(2,1)S(1)}, bf16[1024,512]{1,0:T(8,128)(2,1)S(1)}, f32[1024,512]{1,0:T(8,128)S(1)}) custom-call(s32[3]{0:T(128)S(1)} %slice_bitcast_fusion.dests, bf16[1024,1408]{1,0:T(8,128)(2,1)} %copy-done.15, bf16[1024,1408]{1,0:T(8,128)(2,1)} %copy-done.13, bf16[2,2048,1408]{2,1,0:T(8,128)(2,1)} %bitcast.99, ...), custom_call_target="tpu_custom_call" | custom-call | flops 442918496 | bytes 1 | tf_op jit(solution)/shard_map/terms/pallas_call | solution.py:196
  482.8 15.0 %collective-permute-done.36 = bf16[1024,512]{1,0:T(8,128)(2,1)} collective-permute-done((bf16[1024,512]{1,0:T(8,128)(2,1)S(1)}, bf16[1024,512]{1,0:T(8,128)(2,1)}, u32[]{:S(2)}, u32[]{:S(2)}) %collective-permute-start.36) | collective-permute-done | bytes 1048608 | tf_op jit(solution)/shard_map/ppermute | solution.py:219
  501.6 7.4 collective-permute-start.37
  512.5 12.2 %terms.11 = (bf16[1024,512]{1,0:T(8,128)(2,1)S(1)}, bf16[1024,512]{1,0:T(8,128)(2,1)S(1)}, bf16[1024,512]{1,0:T(8,128)(2,1)S(1)}, f32[1024,512]{1,0:T(8,128)}) custom-call(s32[4]{0:T(128)S(1)} %get-tuple-element.356.dests, bf16[1024,704]{1,0:T(8,128)(2,1)} %copy-done.57, bf16[1024,704]{1,0:T(8,128)(2,1)} %copy-done.55, bf16[2,4,704,512]{3,2,1,0:T(8,128)(2,1)} %bitcast.83, ...), custom_call_target="tpu_custom_call" | custom-call | flops 295279008 | bytes 1 | tf_op jit(solution)/shard_map/terms/pallas_call | solution.py:196
  525.7 8.2 down_grads.1.refs_1_
  539.0 12.2 %collective-permute-done.39 = bf16[1024,512]{1,0:T(8,128)(2,1)} collective-permute-done((bf16[1024,512]{1,0:T(8,128)(2,1)}, bf16[1024,512]{1,0:T(8,128)(2,1)}, u32[]{:S(2)}, u32[]{:S(2)}) %collective-permute-start.39) | collective-permute-done | bytes 1048608 | tf_op jit(solution)/shard_map/ppermute | solution.py:219
  565.6 10.9 %collective-permute-done.43.refs_3_.refs_1_ = bf16[1024,512]{1,0:T(8,128)(2,1)S(1)} collective-permute-done((bf16[1024,512]{1,0:T(8,128)(2,1)S(1)}, bf16[1024,512]{1,0:T(8,128)(2,1)S(1)}, u32[]{:S(2)}, u32[]{:S(2)}) %collective-permute-start.43) | collective-permute-done | bytes 1048608 | tf_op jit(solution)/shard_map/ppermute | solution.py:64
  581.0 16.4 %grads.4.refs_7_ = bf16[2,2048,1408]{2,1,0:T(8,128)(2,1)} custom-call(bf16[1024,2048]{1,0:T(8,128)(2,1)S(1)} %copy-done.5, bf16[1024,1408]{1,0:T(8,128)(2,1)S(1)} %copy-done.16, bf16[1024,1408]{1,0:T(8,128)(2,1)S(1)} %copy-done.14, bf16[1024,512]{1,0:T(8,128)(2,1)S(1)} %collective-permute-done.43.refs_3_.refs_1_, ...), custom_call_target="tpu_custom_call" | custom-call | flops 590558016 | bytes 1 | tf_op jit(solution)/shard_map/grads/pallas_call | solution.py:324
  601.2 26.7 %collective-permute-done.46.refs_2_.refs_4_ = bf16[1024,512]{1,0:T(8,128)(2,1)} collective-permute-done((bf16[1024,512]{1,0:T(8,128)(2,1)S(1)}, bf16[1024,512]{1,0:T(8,128)(2,1)}, u32[]{:S(2)}, u32[]{:S(2)}) %collective-permute-start.46) | collective-permute-done | bytes 1048608 | tf_op jit(solution)/shard_map/ppermute | solution.py:64
  633.1 14.6 %collective-permute-done.47 = bf16[1024,512]{1,0:T(8,128)(2,1)S(1)} collective-permute-done((bf16[1024,512]{1,0:T(8,128)(2,1)}, bf16[1024,512]{1,0:T(8,128)(2,1)S(1)}, u32[]{:S(2)}, u32[]{:S(2)}) %collective-permute-start.47) | collective-permute-done | bytes 1048608 | tf_op jit(solution)/shard_map/ppermute | solution.py:219
  679.1 15.3 %attention_backward.3 = (bf16[1024,512]{1,0:T(8,128)(2,1)S(1)}, bf16[1024,640]{1,0:T(8,128)(2,1)S(1)}, bf16[512,384]{1,0:T(8,128)(2,1)S(1)}, bf16[128,512]{1,0:T(8,128)(2,1)S(1)}) custom-call(bf16[1024,512]{1,0:T(8,128)(2,1)S(1)} %copy-done.64, bf16[1024,640]{1,0:T(8,128)(2,1)S(1)} %copy-done.51, bf16[512,384]{1,0:T(8,128)(2,1)S(1)} %copy-done.78, ...), custom_call_target="tpu_custom_call" | custom-call | flops 850000000 | bytes 1 | tf_op jit(solution)/shard_map/attention_backward/pallas_call | solution.py:624
  703.5 15.3 %attention_backward.2 = (bf16[1024,512]{1,0:T(8,128)(2,1)S(1)}, bf16[1024,640]{1,0:T(8,128)(2,1)S(1)}, bf16[512,384]{1,0:T(8,128)(2,1)S(1)}, bf16[128,512]{1,0:T(8,128)(2,1)S(1)}) custom-call(bf16[1024,512]{1,0:T(8,128)(2,1)S(1)} %copy-done.61, bf16[1024,640]{1,0:T(8,128)(2,1)S(1)} %copy-done.54, bf16[512,384]{1,0:T(8,128)(2,1)S(1)} %copy-done.75, ...), custom_call_target="tpu_custom_call" | custom-call | flops 850000000 | bytes 1 | tf_op jit(solution)/shard_map/attention_backward/pallas_call | solution.py:624
  733.5 9.1 grads.5.refs_3_
  806.4 13.6 %terms.13 = (bf16[1024,512]{1,0:T(8,128)(2,1)S(1)}, bf16[1024,512]{1,0:T(8,128)(2,1)S(1)}, f32[1024,512]{1,0:T(8,128)}) custom-call(s32[3]{0:T(128)S(1)} %slice_bitcast_fusion.dests, bf16[1024,512]{1,0:T(8,128)(2,1)S(1)} %copy-done.39, bf16[1024,512]{1,0:T(8,128)(2,1)S(1)} %copy-done.36, bf16[1024,640]{1,0:T(8,128)(2,1)} %copy-done.18, ...), custom_call_target="tpu_custom_call" | custom-call | flops 362387872 | bytes 1 | tf_op jit(solution)/shard_map/terms/pallas_call | solution.py:196
  851.7 7.8 collective-permute-start.63
  902.4 15.8 %reduce-scatter.12.cloned.1.call-done.refs_0_ = bf16[512,512]{1,0:T(8,128)(2,1)} async-done(((bf16[4096,512]{1,0:T(8,128)(2,1)}), bf16[512,512]{1,0:T(8,128)(2,1)}) %reduce-scatter.12.cloned.1.call-update) | async-done | bytes 524304 | tf_op jit(solution)/shard_map/reduce_scatter | solution.py:364
  (654 shorter events, 478.8 us)
Async XLA Ops:
  7.2 140.3 %all-gather.12.cloned.1.call-start = ((), (), s32[]{:S(2)}) async-start(), calls=%async_computation.5 | async-start | bytes 4718592 | tf_op jit(solution)/shard_map/all_gather | solution.py:274
  32.7 114.8 %all-gather.14.cloned.1.call-start = ((), (), s32[]{:S(2)}) async-start(), calls=%async_computation.6 | async-start | bytes 5898240 | tf_op jit(solution)/shard_map/all_gather | solution.py:274
  34.9 163.6 %all-gather.16.cloned.1.call-start = ((), (), s32[]{:S(2)}) async-start(), calls=%async_computation.7 | async-start | bytes 4718592 | tf_op jit(solution)/shard_map/all_gather | solution.py:274
  72.9 217.1 %all-gather.18.cloned.1.call-start = ((), (), s32[]{:S(2)}) async-start(), calls=%async_computation.8 | async-start | bytes 5242880 | tf_op jit(solution)/shard_map/all_gather | solution.py:751
  77.1 52.5 %collective-permute-start.7 = (bf16[1024,512]{1,0:T(8,128)(2,1)}, bf16[1024,512]{1,0:T(8,128)(2,1)}, u32[]{:S(2)}, u32[]{:S(2)}) collective-permute-start(bf16[1024,512]{1,0:T(8,128)(2,1)} %collective-permute-done.5.refs_3_), channel_id=1, source_target_pairs={{4,6},{5,7},{12,14},{13,15},{20,22},{21,23},{28,30},{29,31}} | collective-permute-start | bytes 3145736 | tf_op jit(solution)/shard_map/ppermute | solution.py:64
  135.1 171.1 %all-gather.22.cloned.1.call-start = ((), (), s32[]{:S(2)}) async-start(), calls=%async_computation.15 | async-start | bytes 6488064 | tf_op jit(solution)/shard_map/all_gather | solution.py:274
  135.7 281.1 %all-gather.24.cloned.1.call-start = ((), (), s32[]{:S(2)}) async-start(), calls=%async_computation.16 | async-start | bytes 12976128 | tf_op jit(solution)/shard_map/all_gather | solution.py:274
  136.3 374.0 %all-gather.26.cloned.1.call-start = ((), (), s32[]{:S(2)}) async-start(), calls=%async_computation.17 | async-start | bytes 1515520 | tf_op jit(solution)/shard_map/all_gather | solution.py:674
  201.4 47.7 %collective-permute-start.19 = (bf16[1024,512]{1,0:T(8,128)(2,1)S(1)}, bf16[1024,512]{1,0:T(8,128)(2,1)}, u32[]{:S(2)}, u32[]{:S(2)}) collective-permute-start(bf16[1024,512]{1,0:T(8,128)(2,1)S(1)} %terms.7.refs_4_), channel_id=1, source_target_pairs={{0,2},{1,3},{8,10},{9,11},{16,18},{17,19},{24,26},{25,27}} | collective-permute-start | bytes 3145736 | tf_op jit(solution)/shard_map/ppermute | solution.py:219
  204.7 44.4 %collective-permute-start.22 = (bf16[1024,512]{1,0:T(8,128)(2,1)S(1)}, bf16[1024,512]{1,0:T(8,128)(2,1)}, u32[]{:S(2)}, u32[]{:S(2)}) collective-permute-start(bf16[1024,512]{1,0:T(8,128)(2,1)S(1)} %terms.7.refs_4_), channel_id=1, source_target_pairs={{6,4},{7,5},{14,12},{15,13},{22,20},{23,21},{30,28},{31,29}} | collective-permute-start | bytes 3145736 | tf_op jit(solution)/shard_map/ppermute | solution.py:219
  281.8 39.5 %collective-permute-start.21 = (bf16[1024,512]{1,0:T(8,128)(2,1)}, bf16[1024,512]{1,0:T(8,128)(2,1)S(1)}, u32[]{:S(2)}, u32[]{:S(2)}) collective-permute-start(bf16[1024,512]{1,0:T(8,128)(2,1)} %get-tuple-element.310), channel_id=1, source_target_pairs={{0,2},{2,4},{4,6},{1,3},{3,5},{5,7},{8,10},{10,12},{12,14},{9,11},... | collective-permute-start | bytes 3145736 | tf_op jit(solution)/shard_map/ppermute | solution.py:219
  288.7 32.6 %collective-permute-start.24 = (bf16[1024,512]{1,0:T(8,128)(2,1)}, bf16[1024,512]{1,0:T(8,128)(2,1)S(1)}, u32[]{:S(2)}, u32[]{:S(2)}) collective-permute-start(bf16[1024,512]{1,0:T(8,128)(2,1)} %get-tuple-element.311), channel_id=1, source_target_pairs={{6,4},{4,2},{2,0},{7,5},{5,3},{3,1},{14,12},{12,10},{10,8},{15,13}... | collective-permute-start | bytes 3145736 | tf_op jit(solution)/shard_map/ppermute | solution.py:219
  363.7 47.5 %collective-permute-start.29 = (bf16[1024,512]{1,0:T(8,128)(2,1)}, bf16[1024,512]{1,0:T(8,128)(2,1)}, u32[]{:S(2)}, u32[]{:S(2)}) collective-permute-start(bf16[1024,512]{1,0:T(8,128)(2,1)} %collective-permute-done.27.refs_3_), channel_id=1, source_target_pairs={{4,6},{5,7},{12,14},{13,15},{20,22},{21,23},{28,30},{29,31}} | collective-permute-start | bytes 3145736 | tf_op jit(solution)/shard_map/ppermute | solution.py:64
  482.7 175.2 %all-gather.20.cloned.1.call-start = ((), (), s32[]{:S(2)}) async-start(), calls=%async_computation.9 | async-start | bytes 1479680 | tf_op jit(solution)/shard_map/all_gather | solution.py:676
  501.6 37.4 %collective-permute-start.37 = (bf16[1024,512]{1,0:T(8,128)(2,1)}, bf16[1024,512]{1,0:T(8,128)(2,1)}, u32[]{:S(2)}, u32[]{:S(2)}) collective-permute-start(bf16[1024,512]{1,0:T(8,128)(2,1)} %get-tuple-element.306), channel_id=1, source_target_pairs={{0,2},{2,4},{4,6},{1,3},{3,5},{5,7},{8,10},{10,12},{12,14},{9,11},... | collective-permute-start | bytes 3145736 | tf_op jit(solution)/shard_map/ppermute | solution.py:219
  509.0 42.2 %collective-permute-start.39 = (bf16[1024,512]{1,0:T(8,128)(2,1)}, bf16[1024,512]{1,0:T(8,128)(2,1)}, u32[]{:S(2)}, u32[]{:S(2)}) collective-permute-start(bf16[1024,512]{1,0:T(8,128)(2,1)} %get-tuple-element.307), channel_id=1, source_target_pairs={{6,4},{4,2},{2,0},{7,5},{5,3},{3,1},{14,12},{12,10},{10,8},{15,13}... | collective-permute-start | bytes 3145736 | tf_op jit(solution)/shard_map/ppermute | solution.py:219
  512.2 263.9 %reduce-scatter.6.cloned.1.call-start = ((), (), s32[]{:S(2)}) async-start(), calls=%async_computation.10 | async-start | bytes 12976128 | tf_op jit(solution)/shard_map/reduce_scatter | solution.py:364
  597.4 274.6 %reduce-scatter.14.cloned.1.call-start = ((), (), s32[]{:S(2)}) async-start(), calls=%async_computation.14 | async-start | bytes 6488064 | tf_op jit(solution)/shard_map/reduce_scatter | solution.py:364
  598.0 299.7 %reduce-scatter.10.cloned.1.call-start = ((), (), s32[]{:S(2)}) async-start(), calls=%async_computation.12 | async-start | bytes 4718592 | tf_op jit(solution)/shard_map/reduce_scatter | solution.py:364
  630.2 33.1 %collective-permute-start.55 = (bf16[1024,512]{1,0:T(8,128)(2,1)}, bf16[1024,512]{1,0:T(8,128)(2,1)}, u32[]{:S(2)}, u32[]{:S(2)}) collective-permute-start(bf16[1024,512]{1,0:T(8,128)(2,1)} %collective-permute-done.44.refs_1_.refs_3_), channel_id=1, source_target_pairs={{4,6},{5,7},{12,14},{13,15},{20,22},{21,23},{28,30},{29,31}} | collective-permute-start | bytes 3145736 | tf_op jit(solution)/shard_map/ppermute | solution.py:64
  631.8 31.5 %collective-permute-start.56 = (bf16[1024,512]{1,0:T(8,128)(2,1)}, bf16[1024,512]{1,0:T(8,128)(2,1)}, u32[]{:S(2)}, u32[]{:S(2)}) collective-permute-start(bf16[1024,512]{1,0:T(8,128)(2,1)} %collective-permute-done.46.refs_2_.refs_4_), channel_id=1, source_target_pairs={{2,0},{3,1},{10,8},{11,9},{18,16},{19,17},{26,24},{27,25}} | collective-permute-start | bytes 3145736 | tf_op jit(solution)/shard_map/ppermute | solution.py:64
  650.9 46.6 %collective-permute-start.48 = (bf16[1024,512]{1,0:T(8,128)(2,1)}, bf16[1024,512]{1,0:T(8,128)(2,1)}, u32[]{:S(2)}, u32[]{:S(2)}) collective-permute-start(bf16[1024,512]{1,0:T(8,128)(2,1)} %get-tuple-element.304.refs_2_), channel_id=1, source_target_pairs={{0,2},{2,4},{1,3},{3,5},{8,10},{10,12},{9,11},{11,13},{16,18},{18,... | collective-permute-start | bytes 3145736 | tf_op jit(solution)/shard_map/ppermute | solution.py:219
  656.1 41.4 %collective-permute-start.51 = (bf16[1024,512]{1,0:T(8,128)(2,1)}, bf16[1024,512]{1,0:T(8,128)(2,1)}, u32[]{:S(2)}, u32[]{:S(2)}) collective-permute-start(bf16[1024,512]{1,0:T(8,128)(2,1)} %get-tuple-element.305.refs_3_), channel_id=1, source_target_pairs={{6,4},{4,2},{7,5},{5,3},{14,12},{12,10},{15,13},{13,11},{22,20},{2... | collective-permute-start | bytes 3145736 | tf_op jit(solution)/shard_map/ppermute | solution.py:219
  702.1 28.8 %collective-permute-start.52 = (bf16[1024,512]{1,0:T(8,128)(2,1)S(1)}, bf16[1024,512]{1,0:T(8,128)(2,1)S(1)}, u32[]{:S(2)}, u32[]{:S(2)}) collective-permute-start(bf16[1024,512]{1,0:T(8,128)(2,1)S(1)} %get-tuple-element.303.rest_refs_1_), channel_id=1, source_target_pairs={{6,4},{4,2},{2,0},{7,5},{5,3},{3,1},{14,12},{12,10},{10,8},{15,13}... | collective-permute-start | bytes 3145736 | tf_op jit(solution)/shard_map/ppermute | solution.py:219
  753.7 145.2 %reduce-scatter.8.cloned.1.call-start = ((), (), s32[]{:S(2)}) async-start(), calls=%async_computation.11 | async-start | bytes 5898240 | tf_op jit(solution)/shard_map/reduce_scatter | solution.py:364
  754.3 163.9 %reduce-scatter.12.cloned.1.call-start = ((), (), s32[]{:S(2)}) async-start(), calls=%async_computation.13 | async-start | bytes 4718592 | tf_op jit(solution)/shard_map/reduce_scatter | solution.py:364
  756.7 46.1 %collective-permute-start.53 = (bf16[1024,256]{1,0:T(8,128)(2,1)}, bf16[1024,256]{1,0:T(8,128)(2,1)}, u32[]{:S(2)}, u32[]{:S(2)}) collective-permute-start(bf16[1024,256]{1,0:T(8,128)(2,1)} %get-tuple-element.334), channel_id=1, source_target_pairs={{0,0},{1,8},{8,1},{9,9},{2,2},{3,10},{10,3},{11,11},{4,4},{5,12},{... | collective-permute-start | bytes 1572872 | tf_op jit(solution)/shard_map/ppermute | solution.py:93
  762.1 40.6 %collective-permute-start.54 = (bf16[1024,256]{1,0:T(8,128)(2,1)}, bf16[1024,256]{1,0:T(8,128)(2,1)}, u32[]{:S(2)}, u32[]{:S(2)}) collective-permute-start(bf16[1024,256]{1,0:T(8,128)(2,1)} %get-tuple-element.335), channel_id=1, source_target_pairs={{8,0},{0,1},{9,8},{1,9},{10,2},{2,3},{11,10},{3,11},{12,4},{4,5},{... | collective-permute-start | bytes 1572872 | tf_op jit(solution)/shard_map/ppermute | solution.py:94
  784.0 36.0 %collective-permute-start.61 = (bf16[1024,512]{1,0:T(8,128)(2,1)}, bf16[1024,512]{1,0:T(8,128)(2,1)}, u32[]{:S(2)}, u32[]{:S(2)}) collective-permute-start(bf16[1024,512]{1,0:T(8,128)(2,1)} %terms.12.refs_8_), channel_id=1, source_target_pairs={{0,2},{1,3},{8,10},{9,11},{16,18},{17,19},{24,26},{25,27}} | collective-permute-start | bytes 3145736 | tf_op jit(solution)/shard_map/ppermute | solution.py:219
  789.0 31.0 %collective-permute-start.64 = (bf16[1024,512]{1,0:T(8,128)(2,1)}, bf16[1024,512]{1,0:T(8,128)(2,1)}, u32[]{:S(2)}, u32[]{:S(2)}) collective-permute-start(bf16[1024,512]{1,0:T(8,128)(2,1)} %terms.12.refs_8_), channel_id=1, source_target_pairs={{6,4},{7,5},{14,12},{15,13},{22,20},{23,21},{30,28},{31,29}} | collective-permute-start | bytes 3145736 | tf_op jit(solution)/shard_map/ppermute | solution.py:219
  851.7 28.9 %collective-permute-start.63 = (bf16[1024,512]{1,0:T(8,128)(2,1)}, bf16[1024,512]{1,0:T(8,128)(2,1)}, u32[]{:S(2)}, u32[]{:S(2)}) collective-permute-start(bf16[1024,512]{1,0:T(8,128)(2,1)} %get-tuple-element.298), channel_id=1, source_target_pairs={{0,2},{2,4},{4,6},{1,3},{3,5},{5,7},{8,10},{10,12},{12,14},{9,11},... | collective-permute-start | bytes 3145736 | tf_op jit(solution)/shard_map/ppermute | solution.py:219
  892.8 29.7 %collective-permute-start.72 = (f32[2,512]{1,0:T(2,128)S(1)}, f32[2,512]{1,0:T(2,128)S(1)}, u32[]{:S(2)}, u32[]{:S(2)}) collective-permute-start(f32[2,512]{1,0:T(2,128)S(1)} %pad_maximum_fusion.8), channel_id=1, source_target_pairs={{0,8},{8,0},{1,9},{9,1},{2,10},{10,2},{3,11},{11,3},{4,12},{12,4},... | collective-permute-start | bytes 12296 | tf_op jit(solution)/shard_map/ppermute | solution.py:58
  (221 other events, 2497.2 us)
Sparse Core Ops, SparseCore 0:
  32.9 37.3 all-gather.11
  72.7 41.1 all-gather.13
  116.3 38.1 all-gather.15
  156.5 99.6 all-gather.17
  258.6 47.5 all-gather.21
  308.5 67.6 all-gather.23
  482.9 15.0 all-gather.25
  512.3 36.4 all-gather.19
  597.6 87.3 reduce-scatter.5
  688.2 59.5 reduce-scatter.13
  753.8 49.4 reduce-scatter.9
  806.5 56.5 reduce-scatter.7
  866.8 51.3 reduce-scatter.11
